TPU v7x, 32 devices: a whole 2x2x4 slice. The times are simulated.
32 devices in a mesh: ctx: 8 (over z, y), exp: 4 (over x, core).
Axes of the slice: x: 2, y: 2, z: 4, core: 2. Of those that a mesh axis runs over, the one named last changes fastest.
Arguments:
- queries: bfloat16 [1024, 16, 576], P('ctx', 'exp'), may hold values from -300 to 300
- latents: bfloat16 [1024, 576], P('ctx'), may hold values from -6 to 6
- value_up: bfloat16 [16, 512, 128], P('exp'), may hold values from -0.5 to 0.5
- out_weight: bfloat16 [2048, 7168], P('exp', 'ctx'), may hold values from -0.25 to 0.25
Outputs:
- attn_out: bfloat16 [1024, 7168], P(('ctx', 'exp'))
All inputs are finite; a program needn't handle non-finite values.
Results may differ from a plain program's by a relative error of at most 0.014.
Values may be sent and summed in bfloat16 or wider, within the bound.
No kernel may reach another device: no remote copies, remote signals or barrier semaphores. Data moves between devices by JAX's collectives and lax.ppermute only.
A program may use at most 64 MiB of HBM per device.

v0:
```python
import jax
import jax.numpy as jnp
from jax import lax
from jax.sharding import PartitionSpec as P

VLAT = 512


score_scale = 192.0 ** (-0.5)


def update(carry, piece, query_rows, row_pos):
    run_max, run_total, accum = carry
    key_pos = jnp.arange(piece.shape[0])
    scores = (
        lax.dot_general(
            query_rows, piece, (((1,), (1,)), ((), ())), preferred_element_type=jnp.float32
        )
        * score_scale
    )
    visible = key_pos[None, :] <= row_pos[:, None]
    scores = jnp.where(visible, scores, -1e30)
    new_max = jnp.maximum(run_max, jnp.max(scores, axis=1))
    expo = jnp.where(visible, jnp.exp(scores - new_max[:, None]), 0.0)
    run_total = jnp.sum(expo, axis=1)
    accum = jnp.dot(expo.astype(jnp.bfloat16), piece[:, :VLAT], preferred_element_type=jnp.float32)
    return (new_max, run_total, accum)


def initial_state(nrows):
    return (
        jnp.full((nrows,), -1e30, jnp.float32),
        jnp.zeros((nrows,), jnp.float32),
        jnp.zeros((nrows, VLAT), jnp.float32),
    )


def shards(queries, latents, value_up, out_weight):
    tok_rows = queries.shape[0]
    head_count = queries.shape[1]
    lat_width = queries.shape[2]
    nrows = tok_rows * head_count
    first_row = lax.axis_index("ctx") * tok_rows
    query_rows = queries.reshape(nrows, lat_width)
    row_pos = first_row + jnp.arange(nrows) // head_count
    start_state = initial_state(nrows)
    folded = update(
        start_state, lax.all_gather(latents, "ctx", axis=0, tiled=True), query_rows, row_pos
    )
    run_max, run_total, accum = folded
    context = (accum / run_total[:, None]).astype(jnp.bfloat16).reshape(tok_rows, head_count, VLAT)
    values = jnp.einsum(
        "thc,hcd->thd", context, value_up, preferred_element_type=jnp.float32
    ).astype(jnp.bfloat16)
    values = values.reshape(tok_rows, head_count * value_up.shape[2])
    partial_out = jnp.dot(
        values,
        lax.all_gather(out_weight, "ctx", axis=1, tiled=True),
        preferred_element_type=jnp.float32,
    )
    return lax.psum_scatter(
        partial_out.astype(jnp.bfloat16), "exp", scatter_dimension=0, tiled=True
    )


def solution(mesh):
    in_specs = (P("ctx", "exp", None), P("ctx", None), P("exp", None, None), P("exp", "ctx"))
    out_specs = P(("ctx", "exp"), None)
    return jax.shard_map(shards, mesh=mesh, in_specs=in_specs, out_specs=out_specs, check_vma=False)
```

profile of v0, /device:TPU:0, one launch (start us, length us, event | category | flops | bytes accessed | tf_op | source)
XLA Modules:
  0.0 206.5 jit_solution(2437613514444822553)
XLA Ops:
  6.5 0.0 copy-start
  6.5 0.0 all-gather.3.cloned.1.call-start
  6.5 0.7 all-gather.3.cloned.1.call-update
  7.3 0.0 all-gather.5.cloned.1.call-start
  7.3 0.7 all-gather.5.cloned.1.call-update
  8.0 0.0 reduce-scatter.2.cloned.1.call-start
  8.1 1.6 copy.7
  9.7 0.3 reshape.27
  10.0 43.1 %all-gather.3.cloned.1.call-done = bf16[1024,576]{0,1:T(8,128)(2,1)} async-done(((bf16[128,576]{0,1:T(8,128)(2,1)}), bf16[1024,576]{0,1:T(8,128)(2,1)}) %all-gather.3.cloned.1.call-update) | async-done | bytes 1179664 | tf_op jit(solution)/shard_map/all_gather | solution.py:48
  53.1 2.4 %fusion = (f32[512]{0:T(512)S(1)}, f32[512,1024]{1,0:T(8,128)S(1)}) fusion(s32[512]{0:T(512)S(1)} %fusion.12, bf16[512,576]{1,0:T(8,128)(2,1)S(1)} %reshape.27, bf16[1024,576]{0,1:T(8,128)(2,1)} %all-gather.3.cloned.1.call-done), kind=kOutput, calls=%fused_computation.4 | convolution fusion | flops 606076416 | bytes 3870720 | tf_op jit(solution)/shard_map/dot_general | solution.py:16
  55.5 0.0 copy-start.1
  55.5 0.7 fusion.2
  56.3 0.5 copy-done.1
  56.8 0.9 fusion.1
  57.7 0.1 reshape.28
  57.8 0.0 copy-done
  57.8 0.3 convolution_convert_fusion.1
  58.2 108.0 %all-gather.5.cloned.1.call-done = bf16[512,7168]{1,0:T(8,128)(2,1)} async-done(((bf16[512,896]{1,0:T(8,128)(2,1)}), bf16[512,7168]{1,0:T(8,128)(2,1)}) %all-gather.5.cloned.1.call-update) | async-done | bytes 7340048 | tf_op jit(solution)/shard_map/all_gather | solution.py:58
  166.1 5.6 %convolution_convert_fusion = bf16[128,7168]{1,0:T(8,128)(2,1)} fusion(bf16[128,512]{0,1:T(8,128)(2,1)S(1)} %bitcast.8, bf16[512,7168]{1,0:T(8,128)(2,1)} %all-gather.5.cloned.1.call-done), kind=kOutput, calls=%fused_computation | convolution fusion | flops 940441600 | bytes 9306112 | tf_op jit(solution)/shard_map/dot_general | solution.py:56
  171.7 0.0 reduce-scatter.2.cloned.1.call-update
  171.7 28.2 %reduce-scatter.2.cloned.1.call-done = bf16[32,7168]{1,0:T(8,128)(2,1)} async-done(((bf16[128,7168]{1,0:T(8,128)(2,1)}), bf16[32,7168]{1,0:T(8,128)(2,1)}) %reduce-scatter.2.cloned.1.call-update) | async-done | bytes 458768 | tf_op jit(solution)/shard_map/reduce_scatter | solution.py:61
  (2 shorter events, 0.0 us)
Async XLA Ops:
  6.5 51.3 %copy-start = (bf16[4,512,128]{2,1,0:T(8,128)(2,1)S(1)}, bf16[4,512,128]{2,1,0:T(8,128)(2,1)}, u32[]{:S(2)}) copy-start(bf16[4,512,128]{2,1,0:T(8,128)(2,1)} %param.6) | copy-start | bytes 1572868
  6.5 46.5 %all-gather.3.cloned.1.call-start = ((), (), s32[]{:S(2)}) async-start(), calls=%async_computation.1 | async-start | bytes 1327104 | tf_op jit(solution)/shard_map/all_gather | solution.py:48
  7.3 158.9 %all-gather.5.cloned.1.call-start = ((), (), s32[]{:S(2)}) async-start(), calls=%async_computation.2 | async-start | bytes 8257536 | tf_op jit(solution)/shard_map/all_gather | solution.py:58
  8.0 191.9 %reduce-scatter.2.cloned.1.call-start = ((), (), s32[]{:S(2)}) async-start(), calls=%async_computation.3 | async-start | bytes 2293760 | tf_op jit(solution)/shard_map/reduce_scatter | solution.py:61
  55.5 1.3 copy-start.1
Sparse Core Ops, SparseCore 0:
  9.4 43.6 all-gather.2
  55.3 110.7 all-gather.4
  171.8 28.0 reduce-scatter.1
where the time goes:
time: 207 us; the launch traced here: 206 us
  waiting for transfers between devices  181 us (87%)
  between operations  13.2 us (6%)
  matrix products  9.21 us (4%)
  local copies, waits for them, and re-layouts  2.56 us (1%)
    all_gather x1, waiting for transfers between devices, shards(): lax.all_gather(out_weight, 'ctx', axis=1, tiled=True)  108 us
    all_gather x1, waiting for transfers between devices, shards(): lax.all_gather(latents, 'ctx', axis=0, tiled=True)  43.1 us
    reduce_scatter x1, waiting for transfers between devices, shards(): lax.psum_scatter(partial_out.astype(jnp.bfloat16), 'exp', scatter_dimensi...  28.2 us
    dot_general x1, matrix products, shards(): jnp.dot(values, lax.all_gather(out_weight, 'ctx', axis=1, tiled=True), pr...  5.55 us
  transfers between devices with their start and end apart: 3, of which 3 were waited for; matrix products, arithmetic and copies ran while one was open for 3% of the time, Pallas kernels for 0%

commit v1 on v0

v1 whole, which is shorter than its diff:
```python
import jax
import jax.numpy as jnp
from jax import lax
from jax.sharding import PartitionSpec as P

VLAT = 512

score_scale = 192.0 ** (-0.5)


def send(value, axis, size, shift):
    return lax.ppermute(value, axis, [(i, i ^ shift) for i in range(size)])


def gather_latents(latents, ctx, exp, core):
    count, heads = lax.axis_size("ctx"), lax.axis_size("exp")

    def fetch(piece, shifts):
        pairs = [
            (c * heads + e, (c ^ shifts[e % 2]) * heads + e) for c in range(count) for e in range(heads)
        ]
        return lax.ppermute(piece, ("ctx", "exp"), pairs)

    blocks, owners = [latents], [ctx]
    half = latents.shape[0] // 2
    for low in range(count - 2, 1, -2):
        shifts = (low - (low % 2), low - (low % 2) + 1)
        mine = fetch(latents, shifts)
        blocks += [mine, send(mine, "exp", heads, 1)]
        owners += [ctx ^ jnp.where(core == 0, shifts[0], shifts[1]), ctx ^ jnp.where(core == 0, shifts[1], shifts[0])]
    mine = fetch(lax.dynamic_slice_in_dim(latents, core * half, half, 0), (1, 1))
    blocks += [mine, send(mine, "exp", heads, 1)]
    owners += [ctx ^ 1, ctx ^ 1]
    return blocks, owners


def gather_weight(out_weight, count, heads):
    half = out_weight.shape[0] // 2
    beside = send(out_weight, "ctx", count, 1)
    near = [(out_weight, beside)]
    for shift in range(2, heads, 2):
        across = send(out_weight, "exp", heads, shift)
        upper = send(beside[:half], "exp", heads, shift)
        lower = send(across[half:], "ctx", count, 1)
        near.append((across, jnp.concatenate([upper, lower], 0)))
    rows = []
    for pair in near:
        rows.append(jnp.concatenate(pair, 1))
        rows.append(jnp.concatenate([send(p, "exp", heads, 1) for p in pair], 1))
    return jnp.concatenate(rows, 0)


def shards(queries, latents, value_up, out_weight):
    count, heads = lax.axis_size("ctx"), lax.axis_size("exp")
    ctx, exp = lax.axis_index("ctx"), lax.axis_index("exp")
    core = exp % 2
    tokens, own_heads, _ = queries.shape
    part = tokens // heads
    width = out_weight.shape[1]

    keys, owners = gather_latents(latents, ctx, exp, core)
    weight = gather_weight(out_weight, count, heads)

    order = exp ^ jnp.arange(heads)
    rows = jnp.take(queries.reshape(heads, part, own_heads, -1), order, axis=0)
    rows = rows.reshape(tokens, own_heads, -1).transpose(1, 0, 2)
    row_pos = ctx * tokens + (order[:, None] * part + jnp.arange(part)[None, :]).reshape(-1)
    key_pos = jnp.concatenate(
        [owner * tokens + jnp.arange(k.shape[0]) for owner, k in zip(owners[:-2], keys[:-2])]
        + [owner * tokens + jnp.zeros(k.shape[0], jnp.int32) for owner, k in zip(owners[-2:], keys[-2:])]
    )
    key = jnp.concatenate(keys, 0)
    visible = (key_pos[None, :] <= row_pos[:, None])[None]
    scores = jnp.einsum("htd,sd->hts", rows, key, preferred_element_type=jnp.float32) * score_scale
    scores = jnp.where(visible, scores, -1e30)
    expo = jnp.where(visible, jnp.exp(scores - jnp.max(scores, axis=2, keepdims=True)), 0.0)
    total = jnp.sum(expo, axis=2, keepdims=True)
    context = jnp.einsum(
        "hts,sc->htc", expo.astype(jnp.bfloat16), key[:, :VLAT], preferred_element_type=jnp.float32
    )
    context = (context / total).astype(jnp.bfloat16)
    values = jnp.einsum("htc,hcd->thd", context, value_up, preferred_element_type=jnp.float32).astype(jnp.bfloat16)
    values = values.reshape(heads // 2, 2, part, -1)

    held = [values[0]] + [send(values[s // 2], "exp", heads, s) for s in range(2, heads, 2)]
    held = jnp.stack(held)
    other = send(held[:, 1], "exp", heads, 1)
    full = jnp.stack([held[:, 0], other], 1).reshape(heads, part, -1).transpose(1, 0, 2).reshape(part, -1)

    gathered = [full] + [send(full, "ctx", count, s) for s in range(2, count, 2)]
    gathered = jnp.concatenate(gathered, 0)
    result = jnp.dot(gathered, weight, preferred_element_type=jnp.float32).astype(jnp.bfloat16)
    result = result.reshape(count // 2, part, -1)
    final = jnp.zeros((part, count * width), jnp.bfloat16)
    for s in range(0, count, 2):
        block = result[s // 2]
        if s:
            block = send(block, "ctx", count, s)
        for side in range(2):
            final = lax.dynamic_update_slice(
                final, block[:, side * width : (side + 1) * width], (0, (ctx ^ (s + side)) * width)
            )
    return final


def solution(mesh):
    in_specs = (P("ctx", "exp", None), P("ctx", None), P("exp", None, None), P("exp", "ctx"))
    out_specs = P(("ctx", "exp"), None)
    return jax.shard_map(shards, mesh=mesh, in_specs=in_specs, out_specs=out_specs, check_vma=False)
```

time: 207 us -> 127 us (0.61)
  waiting for transfers between devices: 181 us -> 63.8 us
  starting transfers between devices: 0.08 us -> 24.5 us
  matrix products: 9.21 us -> 27.3 us
  between operations: 13.2 us -> 0.33 us
  local copies, waits for them, and re-layouts: 2.56 us -> 10.1 us
    all_gather x2 -> x0, waiting for transfers between devices: 151 us -> none  [the longest x1 108 us: shards(): lax.all_gather(out_weight, 'ctx', axis=1, tiled=True)]
    ppermute x0 -> x24, waiting for transfers between devices: none -> 63.8 us  [the longest x20 38.6 us: send(): return lax.ppermute(value, axis, [(i, i ^ shift) for i in range(size)])]
    reduce_scatter x1 -> x0, waiting for transfers between devices: 28.2 us -> none  [shards(): lax.psum_scatter(partial_out.astype(jnp.bfloat16), 'exp', scatter_dimensi...]
    ppermute x0 -> x24, starting transfers between devices: none -> 24.5 us  [the longest x20 18 us: send(): return lax.ppermute(value, axis, [(i, i ^ shift) for i in range(size)])]
    dot_general x4 -> x2, matrix products: 9.21 us -> 23.7 us  [the longest x1 21.6 us: shards(): jnp.dot(gathered, weight, preferred_element_type=jnp.float32)]
    sub x0 -> x1, matrix products: none -> 3.55 us  [shards(): scores - jnp.max(scores, axis=2, keepdims=True)]
    slice x0 -> x7, local copies, waits for them, and re-layouts: none -> 3.06 us  [the longest x1 1.82 us: gather_weight(): lower = send(across[half:], 'ctx', count, 1)]
  transfers between devices with their start and end apart: 3 -> 24, of which waited for: 3 -> 13; matrix products, arithmetic and copies ran while one was open for 3% -> 12% of each run, Pallas kernels for 0% -> 0%
where the time goes in v1:
time: 127 us
  waiting for transfers between devices  63.8 us (50%)
  matrix products  27.3 us (21%)
  starting transfers between devices  24.5 us (19%)
  local copies, waits for them, and re-layouts  10.1 us (8%)
    ppermute x20, waiting for transfers between devices, send(): return lax.ppermute(value, axis, [(i, i ^ shift) for i in range(size)])  38.6 us
    ppermute x4, waiting for transfers between devices, fetch(): return lax.ppermute(piece, ('ctx', 'exp'), pairs)  25.2 us
    dot_general x1, matrix products, shards(): jnp.dot(gathered, weight, preferred_element_type=jnp.float32)  21.6 us
    ppermute x20, starting transfers between devices, send(): return lax.ppermute(value, axis, [(i, i ^ shift) for i in range(size)])  18 us
    ppermute x4, starting transfers between devices, fetch(): return lax.ppermute(piece, ('ctx', 'exp'), pairs)  6.45 us
    sub x1, matrix products, shards(): scores - jnp.max(scores, axis=2, keepdims=True)  3.55 us
  transfers between devices with their start and end apart: 24, of which 13 were waited for; matrix products, arithmetic and copies ran while one was open for 12% of the time, Pallas kernels for 0%

profile of v1, /device:TPU:0, one launch (start us, length us, event | category | flops | bytes accessed | tf_op | source)
XLA Modules:
  0.0 127.0 jit_solution(3494957707234612928)
XLA Ops:
  0.0 5.0 %collective-permute-start = (bf16[128,576]{0,1:T(8,128)(2,1)}, bf16[128,576]{0,1:T(8,128)(2,1)S(1)}, u32[]{:S(2)}, u32[]{:S(2)}) collective-permute-start(bf16[128,576]{0,1:T(8,128)(2,1)} %param.5), channel_id=1, source_target_pairs={{0,24},{1,29},{2,26},{3,31},{4,28},{5,25},{6,30},{7,27},{8,16},{9,... | collective-permute-start | bytes 442376 | tf_op jit(solution)/shard_map/ppermute | solution.py:22
  5.1 1.5 %collective-permute-start.13 = (bf16[512,896]{1,0:T(8,128)(2,1)}, bf16[512,896]{1,0:T(8,128)(2,1)}, u32[]{:S(2)}, u32[]{:S(2)}) collective-permute-start(bf16[512,896]{1,0:T(8,128)(2,1)} %param.7), channel_id=1, source_target_pairs={{0,4},{4,0},{8,12},{12,8},{16,20},{20,16},{24,28},{28,24},{1,5},{5... | collective-permute-start | bytes 2752520 | tf_op jit(solution)/shard_map/ppermute | solution.py:12
  6.6 1.5 %collective-permute-start.16 = (bf16[512,896]{1,0:T(8,128)(2,1)}, bf16[512,896]{1,0:T(8,128)(2,1)}, u32[]{:S(2)}, u32[]{:S(2)}) collective-permute-start(bf16[512,896]{1,0:T(8,128)(2,1)} %param.7), channel_id=1, source_target_pairs={{0,2},{1,3},{2,0},{3,1},{4,6},{5,7},{6,4},{7,5},{8,10},{9,11},{10,... | collective-permute-start | bytes 2752520 | tf_op jit(solution)/shard_map/ppermute | solution.py:12
  8.1 1.0 constant_dynamic-slice_fusion
  9.9 1.4 %copy.6 = bf16[128,4,576]{2,0,1:T(8,128)(2,1)S(1)} copy(bf16[128,4,576]{0,2,1:T(8,128)(2,1)} %param.4) | data formatting | bytes 1179648 | tf_op args[0]
  12.3 20.9 %collective-permute-done.6 = bf16[64,576]{0,1:T(8,128)(2,1)S(1)} collective-permute-done((bf16[64,576]{0,1:T(8,128)(2,1)S(1)}, bf16[64,576]{0,1:T(8,128)(2,1)S(1)}, u32[]{:S(2)}, u32[]{:S(2)}) %collective-permute-start.6) | collective-permute-done | bytes 73760 | tf_op jit(solution)/shard_map/ppermute | solution.py:22
  33.2 1.3 %collective-permute-done.7 = bf16[64,576]{0,1:T(8,128)(2,1)S(1)} collective-permute-done((bf16[64,576]{0,1:T(8,128)(2,1)S(1)}, bf16[64,576]{0,1:T(8,128)(2,1)S(1)}, u32[]{:S(2)}, u32[]{:S(2)}) %collective-permute-start.7) | collective-permute-done | bytes 73760 | tf_op jit(solution)/shard_map/ppermute | solution.py:12
  34.5 0.8 collective-permute-start.4
  35.5 1.2 collective-permute-start.1
  36.8 4.3 %collective-permute-done.4 = bf16[128,576]{0,1:T(8,128)(2,1)S(1)} collective-permute-done((bf16[128,576]{0,1:T(8,128)(2,1)S(1)}, bf16[128,576]{0,1:T(8,128)(2,1)S(1)}, u32[]{:S(2)}, u32[]{:S(2)}) %collective-permute-start.4) | collective-permute-done | bytes 147488 | tf_op jit(solution)/shard_map/ppermute | solution.py:22
  41.1 0.8 broadcast_compare_fusion
  42.6 1.9 %concatenate.28 = bf16[1024,576]{0,1:T(8,128)(2,1)S(1)} concatenate(bf16[128,576]{0,1:T(8,128)(2,1)S(1)} %copy-done.1, bf16[128,576]{0,1:T(8,128)(2,1)S(1)} %collective-permute-done, bf16[128,576]{0,1:T(8,128)(2,1)S(1)} %collective-permute-done.1, bf16[128,576]{0,1:T(8,128)(2,1)S(1)} %collective-permute-done.2, bf16[128,576]{0,1:T(8,128)(2,1)S(1)} %collective-permute-done.3, ...), dimensions={0} | concatenate | bytes 2359296 | tf_op jit(solution)/shard_map/concatenate | solution.py:72
  44.5 1.1 slice.91
  45.5 1.6 %collective-permute-start.17 = (bf16[256,896]{1,0:T(8,128)(2,1)S(1)}, bf16[256,896]{1,0:T(8,128)(2,1)S(1)}, u32[]{:S(2)}, u32[]{:S(2)}) collective-permute-start(bf16[256,896]{1,0:T(8,128)(2,1)S(1)} %slice.91), channel_id=1, source_target_pairs={{0,2},{1,3},{2,0},{3,1},{4,6},{5,7},{6,4},{7,5},{8,10},{9,11},{10,... | collective-permute-start | bytes 1376264 | tf_op jit(solution)/shard_map/ppermute | solution.py:12
  47.2 3.5 %fusion.51 = (f32[4,128]{1,0:T(4,128)S(1)}, bf16[4,128,1024]{2,1,0:T(8,128)(2,1)}) fusion(pred[128,1024]{1,0:T(8,128)(4,1)} %broadcast_compare_fusion, bf16[1024,576]{0,1:T(8,128)(2,1)S(1)} %concatenate.28, bf16[128,4,576]{2,0,1:T(8,128)(2,1)S(1)} %bitcast_select_fusion), kind=kOutput, calls=%fused_computation.83 | convolution fusion | flops 607126528 | bytes 2951168 | tf_op jit(solution)/shard_map/sub | solution.py:76
  50.7 1.8 %slice.92 = bf16[256,896]{1,0:T(8,128)(2,1)} slice(bf16[512,896]{1,0:T(8,128)(2,1)} %collective-permute-done.16), slice={[256:512], [0:896]} | slice | bytes 917504 | tf_op jit(solution)/shard_map/slice | solution.py:44
  52.6 1.0 collective-permute-start.18
  53.6 2.1 %fusion.26 = bf16[128,4,128]{2,0,1:T(8,128)(2,1)S(1)} fusion(bf16[4,512,128]{2,1,0:T(8,128)(2,1)S(1)} %copy-done, bf16[1024,576]{0,1:T(8,128)(2,1)S(1)} %concatenate.28, bf16[4,128,1024]{2,1,0:T(8,128)(2,1)} %get-tuple-element.13, f32[4,128]{1,0:T(4,128)S(1)} %get-tuple-element.12), kind=kOutput, calls=%fused_computation.28 | convolution fusion | flops 604569600 | bytes 2754560 | tf_op jit(solution)/shard_map/htc,hcd->thd/dot_general | solution.py:82
  56.2 1.9 %collective-permute-done.17 = bf16[256,896]{1,0:T(8,128)(2,1)S(1)} collective-permute-done((bf16[256,896]{1,0:T(8,128)(2,1)S(1)}, bf16[256,896]{1,0:T(8,128)(2,1)S(1)}, u32[]{:S(2)}, u32[]{:S(2)}) %collective-permute-start.17) | collective-permute-done | bytes 458784 | tf_op jit(solution)/shard_map/ppermute | solution.py:12
  58.2 6.8 %collective-permute-done.18 = bf16[256,896]{1,0:T(8,128)(2,1)S(1)} collective-permute-done((bf16[256,896]{1,0:T(8,128)(2,1)}, bf16[256,896]{1,0:T(8,128)(2,1)S(1)}, u32[]{:S(2)}, u32[]{:S(2)}) %collective-permute-start.18) | collective-permute-done | bytes 458784 | tf_op jit(solution)/shard_map/ppermute | solution.py:12
  65.9 3.9 %collective-permute-done.8 = bf16[2,32,512]{2,1,0:T(8,128)(2,1)S(1)} collective-permute-done((bf16[2,32,512]{2,1,0:T(8,128)(2,1)S(1)}, bf16[2,32,512]{2,1,0:T(8,128)(2,1)S(1)}, u32[]{:S(2)}, u32[]{:S(2)}) %collective-permute-start.8) | collective-permute-done | bytes 65568 | tf_op jit(solution)/shard_map/ppermute | solution.py:12
  70.0 1.2 collective-permute-done.9
  71.9 5.0 %collective-permute-done.10 = bf16[32,2048]{1,0:T(8,128)(2,1)S(1)} collective-permute-done((bf16[32,2048]{1,0:T(8,128)(2,1)S(1)}, bf16[32,2048]{1,0:T(8,128)(2,1)S(1)}, u32[]{:S(2)}, u32[]{:S(2)}) %collective-permute-start.10) | collective-permute-done | bytes 131104 | tf_op jit(solution)/shard_map/ppermute | solution.py:12
  76.9 1.7 %collective-permute-start.11 = (bf16[32,2048]{1,0:T(8,128)(2,1)S(1)}, bf16[32,2048]{1,0:T(8,128)(2,1)S(1)}, u32[]{:S(2)}, u32[]{:S(2)}) collective-permute-start(bf16[32,2048]{1,0:T(8,128)(2,1)S(1)} %bitcast.41), channel_id=1, source_target_pairs={{0,16},{4,20},{8,24},{12,28},{16,0},{20,4},{24,8},{28,12},{1,17},{... | collective-permute-start | bytes 393224 | tf_op jit(solution)/shard_map/ppermute | solution.py:12
  78.6 6.7 %collective-permute-done.11 = bf16[32,2048]{1,0:T(8,128)(2,1)S(1)} collective-permute-done((bf16[32,2048]{1,0:T(8,128)(2,1)S(1)}, bf16[32,2048]{1,0:T(8,128)(2,1)S(1)}, u32[]{:S(2)}, u32[]{:S(2)}) %collective-permute-start.11) | collective-permute-done | bytes 131104 | tf_op jit(solution)/shard_map/ppermute | solution.py:12
  85.3 2.6 %collective-permute-start.12 = (bf16[32,2048]{1,0:T(8,128)(2,1)S(1)}, bf16[32,2048]{1,0:T(8,128)(2,1)S(1)}, u32[]{:S(2)}, u32[]{:S(2)}) collective-permute-start(bf16[32,2048]{1,0:T(8,128)(2,1)S(1)} %bitcast.42), channel_id=1, source_target_pairs={{0,24},{4,28},{8,16},{12,20},{16,8},{20,12},{24,0},{28,4},{1,25},{... | collective-permute-start | bytes 393224 | tf_op jit(solution)/shard_map/ppermute | solution.py:12
  87.9 4.6 %collective-permute-done.12 = bf16[32,2048]{1,0:T(8,128)(2,1)S(1)} collective-permute-done((bf16[32,2048]{1,0:T(8,128)(2,1)S(1)}, bf16[32,2048]{1,0:T(8,128)(2,1)S(1)}, u32[]{:S(2)}, u32[]{:S(2)}) %collective-permute-start.12) | collective-permute-done | bytes 131104 | tf_op jit(solution)/shard_map/ppermute | solution.py:12
  92.6 21.6 %fusion.17 = bf16[128,1792]{1,0:T(8,128)(2,1)S(1)} fusion(bf16[512,896]{1,0:T(8,128)(2,1)} %collective-permute-done.20, bf16[512,896]{1,0:T(8,128)(2,1)} %collective-permute-done.19, bf16[512,896]{1,0:T(8,128)(2,1)S(1)} %constant_dynamic-update-slice_fusion, bf16[512,896]{1,0:T(8,128)(2,1)} %collective-permute-done.16, ...), kind=kOutput, calls=%fused_computation.18 | convolution fusion | flops 1000570880 | bytes 8323072 | tf_op jit(solution)/shard_map/dot_general | solution.py:92
  115.0 2.4 %collective-permute-start.22 = (bf16[32,1792]{1,0:T(8,128)(2,1)S(1)}, bf16[32,1792]{1,0:T(8,128)(2,1)S(1)}, u32[]{:S(2)}, u32[]{:S(2)}) collective-permute-start(bf16[32,1792]{1,0:T(8,128)(2,1)S(1)} %get-tuple-element.6), channel_id=1, source_target_pairs={{0,16},{4,20},{8,24},{12,28},{16,0},{20,4},{24,8},{28,12},{1,17},{... | collective-permute-start | bytes 344072 | tf_op jit(solution)/shard_map/ppermute | solution.py:12
  117.3 1.4 %collective-permute-start.23 = (bf16[32,1792]{1,0:T(8,128)(2,1)S(1)}, bf16[32,1792]{1,0:T(8,128)(2,1)S(1)}, u32[]{:S(2)}, u32[]{:S(2)}) collective-permute-start(bf16[32,1792]{1,0:T(8,128)(2,1)S(1)} %get-tuple-element.5), channel_id=1, source_target_pairs={{0,24},{4,28},{8,16},{12,20},{16,8},{20,12},{24,0},{28,4},{1,25},{... | collective-permute-start | bytes 344072 | tf_op jit(solution)/shard_map/ppermute | solution.py:12
  118.8 0.8 collective-permute-done.21
  119.7 5.9 %collective-permute-done.22 = bf16[32,1792]{1,0:T(8,128)(2,1)S(1)} collective-permute-done((bf16[32,1792]{1,0:T(8,128)(2,1)S(1)}, bf16[32,1792]{1,0:T(8,128)(2,1)S(1)}, u32[]{:S(2)}, u32[]{:S(2)}) %collective-permute-start.22) | collective-permute-done | bytes 114720 | tf_op jit(solution)/shard_map/ppermute | solution.py:12
  (72 shorter events, 7.2 us)
Async XLA Ops:
  0.0 53.6 %copy-start = (bf16[4,512,128]{2,1,0:T(8,128)(2,1)S(1)}, bf16[4,512,128]{2,1,0:T(8,128)(2,1)}, u32[]{:S(2)}) copy-start(bf16[4,512,128]{2,1,0:T(8,128)(2,1)} %param.6) | copy-start | bytes 1572868
  0.0 35.5 %collective-permute-start = (bf16[128,576]{0,1:T(8,128)(2,1)}, bf16[128,576]{0,1:T(8,128)(2,1)S(1)}, u32[]{:S(2)}, u32[]{:S(2)}) collective-permute-start(bf16[128,576]{0,1:T(8,128)(2,1)} %param.5), channel_id=1, source_target_pairs={{0,24},{1,29},{2,26},{3,31},{4,28},{5,25},{6,30},{7,27},{8,16},{9,... | collective-permute-start | bytes 442376 | tf_op jit(solution)/shard_map/ppermute | solution.py:22
  5.1 31.7 %collective-permute-start.2 = (bf16[128,576]{0,1:T(8,128)(2,1)}, bf16[128,576]{0,1:T(8,128)(2,1)S(1)}, u32[]{:S(2)}, u32[]{:S(2)}) collective-permute-start(bf16[128,576]{0,1:T(8,128)(2,1)} %param.5), channel_id=1, source_target_pairs={{0,16},{1,21},{2,18},{3,23},{4,20},{5,17},{6,22},{7,19},{8,24},{9,... | collective-permute-start | bytes 442376 | tf_op jit(solution)/shard_map/ppermute | solution.py:22
  5.1 39.4 %collective-permute-start.13 = (bf16[512,896]{1,0:T(8,128)(2,1)}, bf16[512,896]{1,0:T(8,128)(2,1)}, u32[]{:S(2)}, u32[]{:S(2)}) collective-permute-start(bf16[512,896]{1,0:T(8,128)(2,1)} %param.7), channel_id=1, source_target_pairs={{0,4},{4,0},{8,12},{12,8},{16,20},{20,16},{24,28},{28,24},{1,5},{5... | collective-permute-start | bytes 2752520 | tf_op jit(solution)/shard_map/ppermute | solution.py:12
  6.6 44.2 %collective-permute-start.16 = (bf16[512,896]{1,0:T(8,128)(2,1)}, bf16[512,896]{1,0:T(8,128)(2,1)}, u32[]{:S(2)}, u32[]{:S(2)}) collective-permute-start(bf16[512,896]{1,0:T(8,128)(2,1)} %param.7), channel_id=1, source_target_pairs={{0,2},{1,3},{2,0},{3,1},{4,6},{5,7},{6,4},{7,5},{8,10},{9,11},{10,... | collective-permute-start | bytes 2752520 | tf_op jit(solution)/shard_map/ppermute | solution.py:12
  9.1 24.1 %collective-permute-start.6 = (bf16[64,576]{0,1:T(8,128)(2,1)S(1)}, bf16[64,576]{0,1:T(8,128)(2,1)S(1)}, u32[]{:S(2)}, u32[]{:S(2)}) collective-permute-start(bf16[64,576]{0,1:T(8,128)(2,1)S(1)} %constant_dynamic-slice_fusion), channel_id=1, source_target_pairs={{0,4},{1,5},{2,6},{3,7},{4,0},{5,1},{6,2},{7,3},{8,12},{9,13},{10,... | collective-permute-start | bytes 221192 | tf_op jit(solution)/shard_map/ppermute | solution.py:22
  11.3 23.2 %copy-start.1 = (bf16[128,576]{0,1:T(8,128)(2,1)S(1)}, bf16[128,576]{0,1:T(8,128)(2,1)}, u32[]{:S(2)}) copy-start(bf16[128,576]{0,1:T(8,128)(2,1)} %param.5) | copy-start | bytes 442372
  33.2 1.4 %collective-permute-start.7 = (bf16[64,576]{0,1:T(8,128)(2,1)S(1)}, bf16[64,576]{0,1:T(8,128)(2,1)S(1)}, u32[]{:S(2)}, u32[]{:S(2)}) collective-permute-start(bf16[64,576]{0,1:T(8,128)(2,1)S(1)} %collective-permute-done.6), channel_id=1, source_target_pairs={{0,1},{1,0},{2,3},{3,2},{4,5},{5,4},{6,7},{7,6},{8,9},{9,8},{10,11... | collective-permute-start | bytes 221192 | tf_op jit(solution)/shard_map/ppermute | solution.py:12
  34.5 6.6 %collective-permute-start.4 = (bf16[128,576]{0,1:T(8,128)(2,1)S(1)}, bf16[128,576]{0,1:T(8,128)(2,1)S(1)}, u32[]{:S(2)}, u32[]{:S(2)}) collective-permute-start(bf16[128,576]{0,1:T(8,128)(2,1)S(1)} %copy-done.1), channel_id=1, source_target_pairs={{0,8},{1,13},{2,10},{3,15},{4,12},{5,9},{6,14},{7,11},{8,0},{9,5},... | collective-permute-start | bytes 442376 | tf_op jit(solution)/shard_map/ppermute | solution.py:22
  35.5 6.4 %collective-permute-start.1 = (bf16[128,576]{0,1:T(8,128)(2,1)S(1)}, bf16[128,576]{0,1:T(8,128)(2,1)S(1)}, u32[]{:S(2)}, u32[]{:S(2)}) collective-permute-start(bf16[128,576]{0,1:T(8,128)(2,1)S(1)} %collective-permute-done), channel_id=1, source_target_pairs={{0,1},{1,0},{2,3},{3,2},{4,5},{5,4},{6,7},{7,6},{8,9},{9,8},{10,11... | collective-permute-start | bytes 442376 | tf_op jit(solution)/shard_map/ppermute | solution.py:12
  36.7 5.7 %collective-permute-start.3 = (bf16[128,576]{0,1:T(8,128)(2,1)S(1)}, bf16[128,576]{0,1:T(8,128)(2,1)S(1)}, u32[]{:S(2)}, u32[]{:S(2)}) collective-permute-start(bf16[128,576]{0,1:T(8,128)(2,1)S(1)} %collective-permute-done.2), channel_id=1, source_target_pairs={{0,1},{1,0},{2,3},{3,2},{4,5},{5,4},{6,7},{7,6},{8,9},{9,8},{10,11... | collective-permute-start | bytes 442376 | tf_op jit(solution)/shard_map/ppermute | solution.py:12
  41.1 1.5 %collective-permute-start.5 = (bf16[128,576]{0,1:T(8,128)(2,1)S(1)}, bf16[128,576]{0,1:T(8,128)(2,1)}, u32[]{:S(2)}, u32[]{:S(2)}) collective-permute-start(bf16[128,576]{0,1:T(8,128)(2,1)S(1)} %collective-permute-done.4), channel_id=1, source_target_pairs={{0,1},{1,0},{2,3},{3,2},{4,5},{5,4},{6,7},{7,6},{8,9},{9,8},{10,11... | collective-permute-start | bytes 442376 | tf_op jit(solution)/shard_map/ppermute | solution.py:12
  41.9 50.6 %collective-permute-start.14 = (bf16[512,896]{1,0:T(8,128)(2,1)}, bf16[512,896]{1,0:T(8,128)(2,1)}, u32[]{:S(2)}, u32[]{:S(2)}) collective-permute-start(bf16[512,896]{1,0:T(8,128)(2,1)} %param.7), channel_id=1, source_target_pairs={{0,1},{1,0},{2,3},{3,2},{4,5},{5,4},{6,7},{7,6},{8,9},{9,8},{10,11... | collective-permute-start | bytes 2752520 | tf_op jit(solution)/shard_map/ppermute | solution.py:12
  45.5 12.6 %collective-permute-start.17 = (bf16[256,896]{1,0:T(8,128)(2,1)S(1)}, bf16[256,896]{1,0:T(8,128)(2,1)S(1)}, u32[]{:S(2)}, u32[]{:S(2)}) collective-permute-start(bf16[256,896]{1,0:T(8,128)(2,1)S(1)} %slice.91), channel_id=1, source_target_pairs={{0,2},{1,3},{2,0},{3,1},{4,6},{5,7},{6,4},{7,5},{8,10},{9,11},{10,... | collective-permute-start | bytes 1376264 | tf_op jit(solution)/shard_map/ppermute | solution.py:12
  52.6 12.5 %collective-permute-start.18 = (bf16[256,896]{1,0:T(8,128)(2,1)}, bf16[256,896]{1,0:T(8,128)(2,1)S(1)}, u32[]{:S(2)}, u32[]{:S(2)}) collective-permute-start(bf16[256,896]{1,0:T(8,128)(2,1)} %slice.92), channel_id=1, source_target_pairs={{0,4},{4,0},{8,12},{12,8},{16,20},{20,16},{24,28},{28,24},{1,5},{5... | collective-permute-start | bytes 1376264 | tf_op jit(solution)/shard_map/ppermute | solution.py:12
  55.7 36.9 %collective-permute-start.15 = (bf16[512,896]{1,0:T(8,128)(2,1)}, bf16[512,896]{1,0:T(8,128)(2,1)}, u32[]{:S(2)}, u32[]{:S(2)}) collective-permute-start(bf16[512,896]{1,0:T(8,128)(2,1)} %collective-permute-done.13), channel_id=1, source_target_pairs={{0,1},{1,0},{2,3},{3,2},{4,5},{5,4},{6,7},{7,6},{8,9},{9,8},{10,11... | collective-permute-start | bytes 2752520 | tf_op jit(solution)/shard_map/ppermute | solution.py:12
  55.7 36.8 %collective-permute-start.19 = (bf16[512,896]{1,0:T(8,128)(2,1)}, bf16[512,896]{1,0:T(8,128)(2,1)}, u32[]{:S(2)}, u32[]{:S(2)}) collective-permute-start(bf16[512,896]{1,0:T(8,128)(2,1)} %collective-permute-done.16), channel_id=1, source_target_pairs={{0,1},{1,0},{2,3},{3,2},{4,5},{5,4},{6,7},{7,6},{8,9},{9,8},{10,11... | collective-permute-start | bytes 2752520 | tf_op jit(solution)/shard_map/ppermute | solution.py:12
  65.1 27.4 %copy-start.3 = (bf16[512,896]{1,0:T(8,128)(2,1)S(1)}, bf16[512,896]{1,0:T(8,128)(2,1)}, u32[]{:S(2)}) copy-start(bf16[512,896]{1,0:T(8,128)(2,1)} %param.7) | copy-start | bytes 2752516
  65.1 27.4 %collective-permute-start.20 = (bf16[512,896]{1,0:T(8,128)(2,1)S(1)}, bf16[512,896]{1,0:T(8,128)(2,1)}, u32[]{:S(2)}, u32[]{:S(2)}) collective-permute-start(bf16[512,896]{1,0:T(8,128)(2,1)S(1)} %constant_dynamic-update-slice_fusion), channel_id=1, source_target_pairs={{0,1},{1,0},{2,3},{3,2},{4,5},{5,4},{6,7},{7,6},{8,9},{9,8},{10,11... | collective-permute-start | bytes 2752520 | tf_op jit(solution)/shard_map/ppermute | solution.py:12
  65.3 4.6 %collective-permute-start.8 = (bf16[2,32,512]{2,1,0:T(8,128)(2,1)S(1)}, bf16[2,32,512]{2,1,0:T(8,128)(2,1)S(1)}, u32[]{:S(2)}, u32[]{:S(2)}) collective-permute-start(bf16[2,32,512]{2,1,0:T(8,128)(2,1)S(1)} %squeeze.4), channel_id=1, source_target_pairs={{0,2},{1,3},{2,0},{3,1},{4,6},{5,7},{6,4},{7,5},{8,10},{9,11},{10,... | collective-permute-start | bytes 196616 | tf_op jit(solution)/shard_map/ppermute | solution.py:12
  69.9 1.3 %collective-permute-start.9 = (bf16[2,32,512]{2,1,0:T(8,128)(2,1)S(1)}, bf16[2,32,512]{2,1,0:T(8,128)(2,1)S(1)}, u32[]{:S(2)}, u32[]{:S(2)}) collective-permute-start(bf16[2,32,512]{2,1,0:T(8,128)(2,1)S(1)} %get-tuple-element.9), channel_id=1, source_target_pairs={{0,1},{1,0},{2,3},{3,2},{4,5},{5,4},{6,7},{7,6},{8,9},{9,8},{10,11... | collective-permute-start | bytes 196616 | tf_op jit(solution)/shard_map/ppermute | solution.py:12
  71.3 5.6 %collective-permute-start.10 = (bf16[32,2048]{1,0:T(8,128)(2,1)S(1)}, bf16[32,2048]{1,0:T(8,128)(2,1)S(1)}, u32[]{:S(2)}, u32[]{:S(2)}) collective-permute-start(bf16[32,2048]{1,0:T(8,128)(2,1)S(1)} %bitcast.40), channel_id=1, source_target_pairs={{0,8},{4,12},{8,0},{12,4},{16,24},{20,28},{24,16},{28,20},{1,9},{5... | collective-permute-start | bytes 393224 | tf_op jit(solution)/shard_map/ppermute | solution.py:12
  76.9 8.4 %collective-permute-start.11 = (bf16[32,2048]{1,0:T(8,128)(2,1)S(1)}, bf16[32,2048]{1,0:T(8,128)(2,1)S(1)}, u32[]{:S(2)}, u32[]{:S(2)}) collective-permute-start(bf16[32,2048]{1,0:T(8,128)(2,1)S(1)} %bitcast.41), channel_id=1, source_target_pairs={{0,16},{4,20},{8,24},{12,28},{16,0},{20,4},{24,8},{28,12},{1,17},{... | collective-permute-start | bytes 393224 | tf_op jit(solution)/shard_map/ppermute | solution.py:12
  85.3 7.2 %collective-permute-start.12 = (bf16[32,2048]{1,0:T(8,128)(2,1)S(1)}, bf16[32,2048]{1,0:T(8,128)(2,1)S(1)}, u32[]{:S(2)}, u32[]{:S(2)}) collective-permute-start(bf16[32,2048]{1,0:T(8,128)(2,1)S(1)} %bitcast.42), channel_id=1, source_target_pairs={{0,24},{4,28},{8,16},{12,20},{16,8},{20,12},{24,0},{28,4},{1,25},{... | collective-permute-start | bytes 393224 | tf_op jit(solution)/shard_map/ppermute | solution.py:12
  114.3 5.4 %collective-permute-start.21 = (bf16[32,1792]{1,0:T(8,128)(2,1)S(1)}, bf16[32,1792]{1,0:T(8,128)(2,1)S(1)}, u32[]{:S(2)}, u32[]{:S(2)}) collective-permute-start(bf16[32,1792]{1,0:T(8,128)(2,1)S(1)} %get-tuple-element.7), channel_id=1, source_target_pairs={{0,8},{4,12},{8,0},{12,4},{16,24},{20,28},{24,16},{28,20},{1,9},{5... | collective-permute-start | bytes 344072 | tf_op jit(solution)/shard_map/ppermute | solution.py:12
  115.0 10.6 %collective-permute-start.22 = (bf16[32,1792]{1,0:T(8,128)(2,1)S(1)}, bf16[32,1792]{1,0:T(8,128)(2,1)S(1)}, u32[]{:S(2)}, u32[]{:S(2)}) collective-permute-start(bf16[32,1792]{1,0:T(8,128)(2,1)S(1)} %get-tuple-element.6), channel_id=1, source_target_pairs={{0,16},{4,20},{8,24},{12,28},{16,0},{20,4},{24,8},{28,12},{1,17},{... | collective-permute-start | bytes 344072 | tf_op jit(solution)/shard_map/ppermute | solution.py:12
  117.3 8.3 %collective-permute-start.23 = (bf16[32,1792]{1,0:T(8,128)(2,1)S(1)}, bf16[32,1792]{1,0:T(8,128)(2,1)S(1)}, u32[]{:S(2)}, u32[]{:S(2)}) collective-permute-start(bf16[32,1792]{1,0:T(8,128)(2,1)S(1)} %get-tuple-element.5), channel_id=1, source_target_pairs={{0,24},{4,28},{8,16},{12,20},{16,8},{20,12},{24,0},{28,4},{1,25},{... | collective-permute-start | bytes 344072 | tf_op jit(solution)/shard_map/ppermute | solution.py:12
  125.6 0.8 copy-start.2

commit v2 on v1

v2 whole, which is shorter than its diff:
```python
import functools

import jax
import jax.numpy as jnp
from jax import lax
from jax.experimental import pallas as pl
from jax.experimental.pallas import tpu as pltpu
from jax.sharding import PartitionSpec as P

VLAT = 512

score_scale = 192.0 ** (-0.5)

VMEM = pl.BlockSpec(memory_space=pltpu.VMEM)
SMEM = pl.BlockSpec(memory_space=pltpu.SMEM)


def send(value, axis, size, shift):
    return lax.ppermute(value, axis, [(i, i ^ shift) for i in range(size)])


def after(value, *others):
    return lax.optimization_barrier((value, *others))[0]


def gather_latents(own, ctx, core, count, heads):
    def fetch(shifts):
        pairs = [
            (c * heads + e, (c ^ shifts[e % 2]) * heads + e) for c in range(count) for e in range(heads)
        ]
        return lax.ppermute(own, ("ctx", "exp"), pairs)

    shifts = [(low, low + 1) for low in range(count - 2, 1, -2)]
    mine = [fetch(pair) for pair in shifts]
    beside = fetch((1, 1))
    other = [send(block, "exp", heads, 1) for block in mine]
    blocks, owners = [own], [ctx]
    for (even, odd), a, b in zip(shifts, mine, other):
        blocks += [a, b]
        owners += [ctx ^ jnp.where(core == 0, even, odd), ctx ^ jnp.where(core == 0, odd, even)]
    return blocks + [beside], owners + [ctx ^ 1]


def attend(part, place, query, *refs):
    *blocks, value_up, values, keys = refs
    own_heads, tokens, _ = query.shape
    width = blocks[0].shape[1]
    count = len(blocks)
    for j, block in enumerate(blocks):
        keys[:, j * width : (j + 1) * width] = block[...]
    ctx, exp = place[count], place[count + 1]
    row = lax.broadcasted_iota(jnp.int32, (tokens, width), 0)
    row = ((row // part) ^ exp) * part + row % part
    col = lax.broadcasted_iota(jnp.int32, (tokens, width), 1)
    inside = col <= row
    group = 2
    for first in range(0, own_heads, group):
        rows = query[first : first + group].reshape(group * tokens, -1)
        scores = jnp.dot(rows, keys[...], preferred_element_type=jnp.float32) * score_scale
        pieces = [
            jnp.where(jnp.concatenate([inside] * group, 0), scores[:, :width], -1e30)
        ]
        for j in range(1, count):
            pieces.append(jnp.where(place[j] < ctx, scores[:, j * width : (j + 1) * width], -1e30))
        scores = jnp.concatenate(pieces, 1)
        expo = jnp.exp(scores - jnp.max(scores, axis=1, keepdims=True))
        total = jnp.sum(expo, axis=1, keepdims=True)
        context = lax.dot_general(
            expo.astype(jnp.bfloat16),
            keys[:VLAT],
            (((1,), (1,)), ((), ())),
            preferred_element_type=jnp.float32,
        )
        context = (context / total).astype(jnp.bfloat16)
        for h in range(group):
            up = jnp.dot(
                context[h * tokens : (h + 1) * tokens], value_up[first + h], preferred_element_type=jnp.float32
            )
            depth = value_up.shape[2]
            values[:, (first + h) * depth : (first + h + 1) * depth] = up.astype(values.dtype)


def project(splits, values, *refs):
    *pieces, keep, away = refs
    half = values.shape[0] // 2
    width = pieces[0].shape[1]
    at = 0
    for group, size in enumerate(splits):
        total, depth = None, 0
        for piece in pieces[at : at + size]:
            term = jnp.dot(
                values[:, depth : depth + piece.shape[0]], piece[...], preferred_element_type=jnp.float32
            )
            total = term if total is None else total + term
            depth += piece.shape[0]
        at += size
        keep[:, group * width : (group + 1) * width] = total[:half]
        away[:, group * width : (group + 1) * width] = total[half:].astype(away.dtype)


def shards(queries, latents, value_up, out_weight):
    count, heads = lax.axis_size("ctx"), lax.axis_size("exp")
    ctx, exp = lax.axis_index("ctx"), lax.axis_index("exp")
    core = exp % 2
    tokens, own_heads, lat = queries.shape
    part = tokens // heads
    width = out_weight.shape[1]
    inner = own_heads * value_up.shape[2]
    half = inner // 2

    across = [send(out_weight, "exp", heads, s) for s in range(2, heads, 2)]
    blocks, owners = gather_latents(latents.T, ctx, core, count, heads)
    beside = send(after(out_weight, *blocks[1::2]), "ctx", count, 1)
    upper = [send(beside[:half], "exp", heads, s) for s in range(2, heads, 2)]
    lower = [send(a[half:], "ctx", count, 1) for a in across]

    order = exp ^ jnp.arange(heads)
    rows = jnp.take(queries.reshape(heads, part, own_heads, lat), order, axis=0)
    rows = rows.reshape(tokens, own_heads, lat).transpose(1, 0, 2)
    place = jnp.stack(owners + [ctx, exp]).astype(jnp.int32)
    values = pl.pallas_call(
        functools.partial(attend, part),
        out_shape=jax.ShapeDtypeStruct((tokens, inner), jnp.bfloat16),
        in_specs=[SMEM] + [VMEM] * (len(blocks) + 2),
        out_specs=VMEM,
        scratch_shapes=[pltpu.VMEM((lat, count * tokens), jnp.bfloat16)],
        compiler_params=pltpu.CompilerParams(vmem_limit_bytes=48 * 2**20),
        cost_estimate=pl.CostEstimate(
            flops=2 * tokens * own_heads * count * tokens * (lat + VLAT),
            bytes_accessed=2 * (rows.size + value_up.size + count * latents.size),
            transcendentals=tokens * own_heads * count * tokens,
        ),
    )(place, rows, *blocks, value_up)

    values = values.reshape(heads // 2, 2 * part, inner)
    held = [values[0]] + [send(values[s // 2], "exp", heads, s) for s in range(2, heads, 2)]
    held = jnp.concatenate(held, 1)
    gathered = [held] + [send(held, "ctx", count, s) for s in range(2, count, 2)]
    gathered = jnp.concatenate([g[:part] for g in gathered] + [g[part:] for g in gathered], 0)

    pieces, splits = [out_weight, *across], [len(across) + 1]
    pieces.append(beside)
    for u, l in zip(upper, lower):
        pieces += [u, l]
    splits.append(1 + 2 * len(across))
    mine = count // 2 * part
    keep, away = pl.pallas_call(
        functools.partial(project, splits),
        out_shape=(
            jax.ShapeDtypeStruct((mine, 2 * width), jnp.float32),
            jax.ShapeDtypeStruct((mine, 2 * width), jnp.bfloat16),
        ),
        in_specs=[VMEM] * (1 + len(pieces)),
        out_specs=(VMEM, VMEM),
        compiler_params=pltpu.CompilerParams(vmem_limit_bytes=48 * 2**20),
        cost_estimate=pl.CostEstimate(
            flops=2 * gathered.size * 2 * width,
            bytes_accessed=2 * (gathered.size + 2 * width * gathered.shape[1]) + 6 * mine * 2 * width,
            transcendentals=0,
        ),
    )(gathered, *pieces)
    result = (keep + send(away, "exp", heads, 1).astype(jnp.float32)).astype(jnp.bfloat16)
    result = result.reshape(count // 2, part, 2 * width)
    final = jnp.zeros((part, count * width), jnp.bfloat16)
    for s in range(0, count, 2):
        block = result[s // 2]
        if s:
            block = send(block, "ctx", count, s)
        for side in range(2):
            final = lax.dynamic_update_slice(
                final, block[:, side * width : (side + 1) * width], (0, (ctx ^ (s + side)) * width)
            )
    return final


def solution(mesh):
    in_specs = (P("ctx", "exp", None), P("ctx", None), P("exp", None, None), P("exp", "ctx"))
    out_specs = P(("ctx", "exp"), None)
    return jax.shard_map(shards, mesh=mesh, in_specs=in_specs, out_specs=out_specs, check_vma=False)
```

time: 127 us -> 79.7 us (0.63)
  matrix products: 27.3 us -> 0 us
  waiting for transfers between devices: 63.8 us -> 48.6 us
  local copies, waits for them, and re-layouts: 10.1 us -> 4.1 us
  Pallas kernels: 0 us -> 4.19 us
  starting transfers between devices: 24.5 us -> 22.1 us
    dot_general x2 -> x0, matrix products: 23.7 us -> none  [the longest x1 21.6 us: shards(): jnp.dot(gathered, weight, preferred_element_type=jnp.float32)]
    ppermute x4, waiting for transfers between devices: 25.2 us -> 8.82 us  [fetch(): return lax.ppermute(own, ('ctx', 'exp'), pairs)]
    pallas_call x0 -> x2, Pallas kernels: none -> 4.19 us  [the longest x1 2.93 us: shards(): pl.pallas_call(functools.partial(attend, part), out_shape=jax.ShapeDtypeS...]
    sub x1 -> x0, matrix products: 3.55 us -> none  [shards(): scores - jnp.max(scores, axis=2, keepdims=True)]
    ppermute x20 -> x15, starting transfers between devices: 18 us -> 14.8 us  [send(): return lax.ppermute(value, axis, [(i, i ^ shift) for i in range(size)])]
    slice x5 -> x2, local copies, waits for them, and re-layouts: 2.98 us -> 0.07 us  [the longest x1 0.04 us: shards(): upper = [send(beside[:half], 'exp', heads, s) for s in range(2, heads, 2)]]
    concatenate x3 -> x1, local copies, waits for them, and re-layouts: 1.98 us -> 0.01 us  [shards(): jnp.concatenate([g[:part] for g in gathered] + [g[part:] for g in gathere...]
    ppermute x20 -> x15, waiting for transfers between devices: 38.6 us -> 39.7 us  [send(): return lax.ppermute(value, axis, [(i, i ^ shift) for i in range(size)])]
  transfers between devices with their start and end apart: 24 -> 19, of which waited for: 13 -> 13; matrix products, arithmetic and copies ran while one was open for 12% -> 4% of each run, Pallas kernels for 0% -> 0%
where the time goes in v2:
time: 79.7 us; the launch traced here: 79.6 us
  waiting for transfers between devices  48.6 us (61%)
  starting transfers between devices  22.1 us (28%)
  Pallas kernels  4.19 us (5%)
  local copies, waits for them, and re-layouts  4.1 us (5%)
    ppermute x15, waiting for transfers between devices, send(): return lax.ppermute(value, axis, [(i, i ^ shift) for i in range(size)])  39.7 us
    ppermute x15, starting transfers between devices, send(): return lax.ppermute(value, axis, [(i, i ^ shift) for i in range(size)])  14.8 us
    ppermute x4, waiting for transfers between devices, fetch(): return lax.ppermute(own, ('ctx', 'exp'), pairs)  8.82 us
    ppermute x4, starting transfers between devices, fetch(): return lax.ppermute(own, ('ctx', 'exp'), pairs)  7.35 us
    pallas_call x1, Pallas kernels, shards(): pl.pallas_call(functools.partial(attend, part), out_shape=jax.ShapeDtypeS...  2.93 us
    unnamed x14, local copies, waits for them, and re-layouts  2.17 us
  transfers between devices with their start and end apart: 19, of which 13 were waited for; matrix products, arithmetic and copies ran while one was open for 4% of the time, Pallas kernels for 0%

profile of v2, /device:TPU:0, one launch (start us, length us, event | category | flops | bytes accessed | tf_op | source)
XLA Modules:
  0.0 79.6 jit_solution(6039677204788725138)
XLA Ops:
  0.0 5.0 %collective-permute-start = (bf16[576,128]{1,0:T(8,128)(2,1)}, bf16[576,128]{1,0:T(8,128)(2,1)S(1)}, u32[]{:S(2)}, u32[]{:S(2)}) collective-permute-start(bf16[576,128]{1,0:T(8,128)(2,1)} %bitcast.17), channel_id=1, source_target_pairs={{0,24},{1,29},{2,26},{3,31},{4,28},{5,25},{6,30},{7,27},{8,16},{9,... | collective-permute-start | bytes 442376 | tf_op jit(solution)/shard_map/ppermute | solution.py:31
  5.1 0.6 collective-permute-start.4
  5.6 1.7 %collective-permute-start.6 = (bf16[576,128]{1,0:T(8,128)(2,1)}, bf16[576,128]{1,0:T(8,128)(2,1)S(1)}, u32[]{:S(2)}, u32[]{:S(2)}) collective-permute-start(bf16[576,128]{1,0:T(8,128)(2,1)} %bitcast.20), channel_id=1, source_target_pairs={{0,4},{1,5},{2,6},{3,7},{4,0},{5,1},{6,2},{7,3},{8,12},{9,13},{10,... | collective-permute-start | bytes 442376 | tf_op jit(solution)/shard_map/ppermute | solution.py:31
  7.4 1.4 %copy.5 = bf16[128,4,576]{2,0,1:T(8,128)(2,1)S(1)} copy(bf16[128,4,576]{0,2,1:T(8,128)(2,1)} %param.4) | data formatting | bytes 1179648 | tf_op args[0]
  8.8 0.7 gather_fusion
  9.9 0.2 collective-permute-done.refs_1_
  10.1 8.6 %collective-permute-done.2.refs_3_ = bf16[576,128]{1,0:T(8,128)(2,1)S(1)} collective-permute-done((bf16[576,128]{1,0:T(8,128)(2,1)}, bf16[576,128]{1,0:T(8,128)(2,1)S(1)}, u32[]{:S(2)}, u32[]{:S(2)}) %collective-permute-start.2) | collective-permute-done | bytes 147488 | tf_op jit(solution)/shard_map/ppermute | solution.py:31
  18.7 0.5 collective-permute-start.5
  19.4 0.7 collective-permute-done.3.refs_4_
  20.3 2.9 %shard_map.46 = bf16[128,512]{1,0:T(8,128)(2,1)S(1)} custom-call(s32[10]{0:T(128)S(1)} %stack.40.place, bf16[4,128,576]{2,1,0:T(8,128)(2,1)S(1)} %bitcast.16, bf16[576,128]{1,0:T(8,128)(2,1)S(1)} %bitcast.21, bf16[576,128]{1,0:T(8,128)(2,1)S(1)} %collective-permute-done.refs_1_, bf16[576,128]{1,0:T(8,128)(2,1)S(1)} %collective-permute-done.1.refs_2_, ...), custom_call_target="tpu_custom_call" | custom-call | flops 1140850688 | bytes 2293760 | tf_op jit(solution)/shard_map/pallas_call | solution.py:121
  23.2 1.6 %collective-permute-start.7 = (bf16[64,512]{1,0:T(8,128)(2,1)S(1)}, bf16[64,512]{1,0:T(8,128)(2,1)S(1)}, u32[]{:S(2)}, u32[]{:S(2)}) collective-permute-start(bf16[64,512]{1,0:T(8,128)(2,1)S(1)} %get-tuple-element.14), channel_id=1, source_target_pairs={{0,2},{1,3},{2,0},{3,1},{4,6},{5,7},{6,4},{7,5},{8,10},{9,11},{10,... | collective-permute-start | bytes 196616 | tf_op jit(solution)/shard_map/ppermute | solution.py:19
  24.8 2.8 %collective-permute-done.7 = bf16[64,512]{1,0:T(8,128)(2,1)S(1)} collective-permute-done((bf16[64,512]{1,0:T(8,128)(2,1)S(1)}, bf16[64,512]{1,0:T(8,128)(2,1)S(1)}, u32[]{:S(2)}, u32[]{:S(2)}) %collective-permute-start.7) | collective-permute-done | bytes 65568 | tf_op jit(solution)/shard_map/ppermute | solution.py:19
  27.7 1.6 %collective-permute-start.11 = (bf16[512,896]{1,0:T(8,128)(2,1)S(1)}, bf16[512,896]{1,0:T(8,128)(2,1)S(1)}, u32[]{:S(2)}, u32[]{:S(2)}) collective-permute-start(bf16[512,896]{1,0:T(8,128)(2,1)S(1)} %copy-done), channel_id=1, source_target_pairs={{0,2},{1,3},{2,0},{3,1},{4,6},{5,7},{6,4},{7,5},{8,10},{9,11},{10,... | collective-permute-start | bytes 2752520 | tf_op jit(solution)/shard_map/ppermute | solution.py:19
  29.3 0.9 %collective-permute-start.12 = (bf16[512,896]{1,0:T(8,128)(2,1)S(1)}, bf16[512,896]{1,0:T(8,128)(2,1)S(1)}, u32[]{:S(2)}, u32[]{:S(2)}) collective-permute-start(bf16[512,896]{1,0:T(8,128)(2,1)S(1)} %copy-done), channel_id=1, source_target_pairs={{0,4},{4,0},{8,12},{12,8},{16,20},{20,16},{24,28},{28,24},{1,5},{5... | collective-permute-start | bytes 2752520 | tf_op jit(solution)/shard_map/ppermute | solution.py:19
  30.1 3.0 %collective-permute-start.9 = (bf16[64,1024]{1,0:T(8,128)(2,1)S(1)}, bf16[64,1024]{1,0:T(8,128)(2,1)S(1)}, u32[]{:S(2)}, u32[]{:S(2)}) collective-permute-start(bf16[64,1024]{1,0:T(8,128)(2,1)S(1)} %pad_maximum_fusion), channel_id=1, source_target_pairs={{0,16},{4,20},{8,24},{12,28},{16,0},{20,4},{24,8},{28,12},{1,17},{... | collective-permute-start | bytes 393224 | tf_op jit(solution)/shard_map/ppermute | solution.py:19
  33.1 1.4 %collective-permute-start.10 = (bf16[64,1024]{1,0:T(8,128)(2,1)S(1)}, bf16[64,1024]{1,0:T(8,128)(2,1)S(1)}, u32[]{:S(2)}, u32[]{:S(2)}) collective-permute-start(bf16[64,1024]{1,0:T(8,128)(2,1)S(1)} %pad_maximum_fusion), channel_id=1, source_target_pairs={{0,24},{4,28},{8,16},{12,20},{16,8},{20,12},{24,0},{28,4},{1,25},{... | collective-permute-start | bytes 393224 | tf_op jit(solution)/shard_map/ppermute | solution.py:19
  34.5 7.5 %collective-permute-done.9 = bf16[64,1024]{1,0:T(8,128)(2,1)S(1)} collective-permute-done((bf16[64,1024]{1,0:T(8,128)(2,1)S(1)}, bf16[64,1024]{1,0:T(8,128)(2,1)S(1)}, u32[]{:S(2)}, u32[]{:S(2)}) %collective-permute-start.9) | collective-permute-done | bytes 131104 | tf_op jit(solution)/shard_map/ppermute | solution.py:19
  42.0 7.6 %collective-permute-done.11.refs_1_ = bf16[512,896]{1,0:T(8,128)(2,1)S(1)} collective-permute-done((bf16[512,896]{1,0:T(8,128)(2,1)S(1)}, bf16[512,896]{1,0:T(8,128)(2,1)S(1)}, u32[]{:S(2)}, u32[]{:S(2)}) %collective-permute-start.11) | collective-permute-done | bytes 917536 | tf_op jit(solution)/shard_map/ppermute | solution.py:19
  49.6 0.5 collective-permute-start.14
  50.1 0.7 collective-permute-done.12.refs_2_
  50.8 0.9 %collective-permute-start.13 = (bf16[256,896]{1,0:T(8,128)(2,1)S(1)}, bf16[256,896]{1,0:T(8,128)(2,1)S(1)}, u32[]{:S(2)}, u32[]{:S(2)}) collective-permute-start(bf16[256,896]{1,0:T(8,128)(2,1)S(1)} %slice.115), channel_id=1, source_target_pairs={{0,2},{1,3},{2,0},{3,1},{4,6},{5,7},{6,4},{7,5},{8,10},{9,11},{10,... | collective-permute-start | bytes 1376264 | tf_op jit(solution)/shard_map/ppermute | solution.py:19
  51.7 8.9 %collective-permute-done.14.refs_4_ = bf16[256,896]{1,0:T(8,128)(2,1)S(1)} collective-permute-done((bf16[256,896]{1,0:T(8,128)(2,1)S(1)}, bf16[256,896]{1,0:T(8,128)(2,1)S(1)}, u32[]{:S(2)}, u32[]{:S(2)}) %collective-permute-start.14) | collective-permute-done | bytes 458784 | tf_op jit(solution)/shard_map/ppermute | solution.py:19
  60.6 0.9 %collective-permute-done.13.refs_3_ = bf16[256,896]{1,0:T(8,128)(2,1)S(1)} collective-permute-done((bf16[256,896]{1,0:T(8,128)(2,1)S(1)}, bf16[256,896]{1,0:T(8,128)(2,1)S(1)}, u32[]{:S(2)}, u32[]{:S(2)}) %collective-permute-start.13) | collective-permute-done | bytes 458784 | tf_op jit(solution)/shard_map/ppermute | solution.py:19
  61.5 1.3 %shard_map.47 = (f32[128,1792]{1,0:T(8,128)S(1)}, bf16[128,1792]{1,0:T(8,128)(2,1)S(1)}) custom-call(bf16[256,1024]{1,0:T(8,128)(2,1)S(1)} %slice_dynamic-update-slice_fusion.values, bf16[512,896]{1,0:T(8,128)(2,1)S(1)} %copy-done, bf16[512,896]{1,0:T(8,128)(2,1)S(1)} %collective-permute-done.11.refs_1_, ...), custom_call_target="tpu_custom_call" | custom-call | flops 939524096 | bytes 5570560 | tf_op jit(solution)/shard_map/pallas_call | solution.py:147
  62.9 1.8 %collective-permute-done.15 = bf16[128,1792]{1,0:T(8,128)(2,1)S(1)} collective-permute-done((bf16[128,1792]{1,0:T(8,128)(2,1)S(1)}, bf16[128,1792]{1,0:T(8,128)(2,1)S(1)}, u32[]{:S(2)}, u32[]{:S(2)}) %collective-permute-start.15) | collective-permute-done | bytes 458784 | tf_op jit(solution)/shard_map/ppermute | solution.py:19
  64.8 1.4 %collective-permute-start.16 = (bf16[32,1792]{1,0:T(8,128)(2,1)S(1)}, bf16[32,1792]{1,0:T(8,128)(2,1)S(1)}, u32[]{:S(2)}, u32[]{:S(2)}) collective-permute-start(bf16[32,1792]{1,0:T(8,128)(2,1)S(1)} %get-tuple-element.13), channel_id=1, source_target_pairs={{0,8},{4,12},{8,0},{12,4},{16,24},{20,28},{24,16},{28,20},{1,9},{5... | collective-permute-start | bytes 344072 | tf_op jit(solution)/shard_map/ppermute | solution.py:19
  66.3 1.7 %collective-permute-start.17 = (bf16[32,1792]{1,0:T(8,128)(2,1)S(1)}, bf16[32,1792]{1,0:T(8,128)(2,1)S(1)}, u32[]{:S(2)}, u32[]{:S(2)}) collective-permute-start(bf16[32,1792]{1,0:T(8,128)(2,1)S(1)} %get-tuple-element.12), channel_id=1, source_target_pairs={{0,16},{4,20},{8,24},{12,28},{16,0},{20,4},{24,8},{28,12},{1,17},{... | collective-permute-start | bytes 344072 | tf_op jit(solution)/shard_map/ppermute | solution.py:19
  67.9 1.3 %collective-permute-start.18 = (bf16[32,1792]{1,0:T(8,128)(2,1)S(1)}, bf16[32,1792]{1,0:T(8,128)(2,1)S(1)}, u32[]{:S(2)}, u32[]{:S(2)}) collective-permute-start(bf16[32,1792]{1,0:T(8,128)(2,1)S(1)} %get-tuple-element.11), channel_id=1, source_target_pairs={{0,24},{4,28},{8,16},{12,20},{16,8},{20,12},{24,0},{28,4},{1,25},{... | collective-permute-start | bytes 344072 | tf_op jit(solution)/shard_map/ppermute | solution.py:19
  69.3 2.3 %collective-permute-done.16 = bf16[32,1792]{1,0:T(8,128)(2,1)S(1)} collective-permute-done((bf16[32,1792]{1,0:T(8,128)(2,1)S(1)}, bf16[32,1792]{1,0:T(8,128)(2,1)S(1)}, u32[]{:S(2)}, u32[]{:S(2)}) %collective-permute-start.16) | collective-permute-done | bytes 114720 | tf_op jit(solution)/shard_map/ppermute | solution.py:19
  71.6 6.5 %collective-permute-done.17 = bf16[32,1792]{1,0:T(8,128)(2,1)S(1)} collective-permute-done((bf16[32,1792]{1,0:T(8,128)(2,1)S(1)}, bf16[32,1792]{1,0:T(8,128)(2,1)S(1)}, u32[]{:S(2)}, u32[]{:S(2)}) %collective-permute-start.17) | collective-permute-done | bytes 114720 | tf_op jit(solution)/shard_map/ppermute | solution.py:19
  78.2 0.8 copy-done.3
  78.9 0.6 slice_dynamic-update-slice_fusion.6
  (50 shorter events, 1.4 us)
Async XLA Ops:
  0.0 10.1 %collective-permute-start = (bf16[576,128]{1,0:T(8,128)(2,1)}, bf16[576,128]{1,0:T(8,128)(2,1)S(1)}, u32[]{:S(2)}, u32[]{:S(2)}) collective-permute-start(bf16[576,128]{1,0:T(8,128)(2,1)} %bitcast.17), channel_id=1, source_target_pairs={{0,24},{1,29},{2,26},{3,31},{4,28},{5,25},{6,30},{7,27},{8,16},{9,... | collective-permute-start | bytes 442376 | tf_op jit(solution)/shard_map/ppermute | solution.py:31
  5.0 13.6 %collective-permute-start.2 = (bf16[576,128]{1,0:T(8,128)(2,1)}, bf16[576,128]{1,0:T(8,128)(2,1)S(1)}, u32[]{:S(2)}, u32[]{:S(2)}) collective-permute-start(bf16[576,128]{1,0:T(8,128)(2,1)} %bitcast.18), channel_id=1, source_target_pairs={{0,16},{1,21},{2,18},{3,23},{4,20},{5,17},{6,22},{7,19},{8,24},{9,... | collective-permute-start | bytes 442376 | tf_op jit(solution)/shard_map/ppermute | solution.py:31
  5.1 13.6 %collective-permute-start.4 = (bf16[576,128]{1,0:T(8,128)(2,1)}, bf16[576,128]{1,0:T(8,128)(2,1)S(1)}, u32[]{:S(2)}, u32[]{:S(2)}) collective-permute-start(bf16[576,128]{1,0:T(8,128)(2,1)} %bitcast.19), channel_id=1, source_target_pairs={{0,8},{1,13},{2,10},{3,15},{4,12},{5,9},{6,14},{7,11},{8,0},{9,5},... | collective-permute-start | bytes 442376 | tf_op jit(solution)/shard_map/ppermute | solution.py:31
  5.6 13.8 %collective-permute-start.6 = (bf16[576,128]{1,0:T(8,128)(2,1)}, bf16[576,128]{1,0:T(8,128)(2,1)S(1)}, u32[]{:S(2)}, u32[]{:S(2)}) collective-permute-start(bf16[576,128]{1,0:T(8,128)(2,1)} %bitcast.20), channel_id=1, source_target_pairs={{0,4},{1,5},{2,6},{3,7},{4,0},{5,1},{6,2},{7,3},{8,12},{9,13},{10,... | collective-permute-start | bytes 442376 | tf_op jit(solution)/shard_map/ppermute | solution.py:31
  9.9 10.4 %copy-start.1 = (bf16[4,512,128]{2,1,0:T(8,128)(2,1)S(1)}, bf16[4,512,128]{2,1,0:T(8,128)(2,1)}, u32[]{:S(2)}) copy-start(bf16[4,512,128]{2,1,0:T(8,128)(2,1)} %refs_8_.1) | copy-start | bytes 1572868
  9.9 10.4 %copy-start.2 = (bf16[128,576]{0,1:T(8,128)(2,1)S(1)}, bf16[128,576]{0,1:T(8,128)(2,1)}, u32[]{:S(2)}) copy-start(bf16[128,576]{0,1:T(8,128)(2,1)} %param.5) | copy-start | bytes 442372
  10.1 9.3 %collective-permute-start.1 = (bf16[576,128]{1,0:T(8,128)(2,1)S(1)}, bf16[576,128]{1,0:T(8,128)(2,1)S(1)}, u32[]{:S(2)}, u32[]{:S(2)}) collective-permute-start(bf16[576,128]{1,0:T(8,128)(2,1)S(1)} %collective-permute-done.refs_1_), channel_id=1, source_target_pairs={{0,1},{1,0},{2,3},{3,2},{4,5},{5,4},{6,7},{7,6},{8,9},{9,8},{10,11... | collective-permute-start | bytes 442376 | tf_op jit(solution)/shard_map/ppermute | solution.py:19
  18.7 1.4 %collective-permute-start.3 = (bf16[576,128]{1,0:T(8,128)(2,1)S(1)}, bf16[576,128]{1,0:T(8,128)(2,1)S(1)}, u32[]{:S(2)}, u32[]{:S(2)}) collective-permute-start(bf16[576,128]{1,0:T(8,128)(2,1)S(1)} %collective-permute-done.2.refs_3_), channel_id=1, source_target_pairs={{0,1},{1,0},{2,3},{3,2},{4,5},{5,4},{6,7},{7,6},{8,9},{9,8},{10,11... | collective-permute-start | bytes 442376 | tf_op jit(solution)/shard_map/ppermute | solution.py:19
  18.7 1.6 %collective-permute-start.5 = (bf16[576,128]{1,0:T(8,128)(2,1)S(1)}, bf16[576,128]{1,0:T(8,128)(2,1)S(1)}, u32[]{:S(2)}, u32[]{:S(2)}) collective-permute-start(bf16[576,128]{1,0:T(8,128)(2,1)S(1)} %collective-permute-done.4.refs_5_), channel_id=1, source_target_pairs={{0,1},{1,0},{2,3},{3,2},{4,5},{5,4},{6,7},{7,6},{8,9},{9,8},{10,11... | collective-permute-start | bytes 442376 | tf_op jit(solution)/shard_map/ppermute | solution.py:19
  20.3 7.4 %copy-start = (bf16[512,896]{1,0:T(8,128)(2,1)S(1)}, bf16[512,896]{1,0:T(8,128)(2,1)}, u32[]{:S(2)}) copy-start(bf16[512,896]{1,0:T(8,128)(2,1)} %refs_0_.1) | copy-start | bytes 2752516
  23.2 4.4 %collective-permute-start.7 = (bf16[64,512]{1,0:T(8,128)(2,1)S(1)}, bf16[64,512]{1,0:T(8,128)(2,1)S(1)}, u32[]{:S(2)}, u32[]{:S(2)}) collective-permute-start(bf16[64,512]{1,0:T(8,128)(2,1)S(1)} %get-tuple-element.14), channel_id=1, source_target_pairs={{0,2},{1,3},{2,0},{3,1},{4,6},{5,7},{6,4},{7,5},{8,10},{9,11},{10,... | collective-permute-start | bytes 196616 | tf_op jit(solution)/shard_map/ppermute | solution.py:19
  27.6 6.8 %collective-permute-start.8 = (bf16[64,1024]{1,0:T(8,128)(2,1)S(1)}, bf16[64,1024]{1,0:T(8,128)(2,1)S(1)}, u32[]{:S(2)}, u32[]{:S(2)}) collective-permute-start(bf16[64,1024]{1,0:T(8,128)(2,1)S(1)} %pad_maximum_fusion), channel_id=1, source_target_pairs={{0,8},{4,12},{8,0},{12,4},{16,24},{20,28},{24,16},{28,20},{1,9},{5... | collective-permute-start | bytes 393224 | tf_op jit(solution)/shard_map/ppermute | solution.py:19
  27.7 21.8 %collective-permute-start.11 = (bf16[512,896]{1,0:T(8,128)(2,1)S(1)}, bf16[512,896]{1,0:T(8,128)(2,1)S(1)}, u32[]{:S(2)}, u32[]{:S(2)}) collective-permute-start(bf16[512,896]{1,0:T(8,128)(2,1)S(1)} %copy-done), channel_id=1, source_target_pairs={{0,2},{1,3},{2,0},{3,1},{4,6},{5,7},{6,4},{7,5},{8,10},{9,11},{10,... | collective-permute-start | bytes 2752520 | tf_op jit(solution)/shard_map/ppermute | solution.py:19
  29.3 21.5 %collective-permute-start.12 = (bf16[512,896]{1,0:T(8,128)(2,1)S(1)}, bf16[512,896]{1,0:T(8,128)(2,1)S(1)}, u32[]{:S(2)}, u32[]{:S(2)}) collective-permute-start(bf16[512,896]{1,0:T(8,128)(2,1)S(1)} %copy-done), channel_id=1, source_target_pairs={{0,4},{4,0},{8,12},{12,8},{16,20},{20,16},{24,28},{28,24},{1,5},{5... | collective-permute-start | bytes 2752520 | tf_op jit(solution)/shard_map/ppermute | solution.py:19
  30.1 11.8 %collective-permute-start.9 = (bf16[64,1024]{1,0:T(8,128)(2,1)S(1)}, bf16[64,1024]{1,0:T(8,128)(2,1)S(1)}, u32[]{:S(2)}, u32[]{:S(2)}) collective-permute-start(bf16[64,1024]{1,0:T(8,128)(2,1)S(1)} %pad_maximum_fusion), channel_id=1, source_target_pairs={{0,16},{4,20},{8,24},{12,28},{16,0},{20,4},{24,8},{28,12},{1,17},{... | collective-permute-start | bytes 393224 | tf_op jit(solution)/shard_map/ppermute | solution.py:19
  33.1 8.8 %collective-permute-start.10 = (bf16[64,1024]{1,0:T(8,128)(2,1)S(1)}, bf16[64,1024]{1,0:T(8,128)(2,1)S(1)}, u32[]{:S(2)}, u32[]{:S(2)}) collective-permute-start(bf16[64,1024]{1,0:T(8,128)(2,1)S(1)} %pad_maximum_fusion), channel_id=1, source_target_pairs={{0,24},{4,28},{8,16},{12,20},{16,8},{20,12},{24,0},{28,4},{1,25},{... | collective-permute-start | bytes 393224 | tf_op jit(solution)/shard_map/ppermute | solution.py:19
  49.6 11.1 %collective-permute-start.14 = (bf16[256,896]{1,0:T(8,128)(2,1)S(1)}, bf16[256,896]{1,0:T(8,128)(2,1)S(1)}, u32[]{:S(2)}, u32[]{:S(2)}) collective-permute-start(bf16[256,896]{1,0:T(8,128)(2,1)S(1)} %slice.116), channel_id=1, source_target_pairs={{0,4},{4,0},{8,12},{12,8},{16,20},{20,16},{24,28},{28,24},{1,5},{5... | collective-permute-start | bytes 1376264 | tf_op jit(solution)/shard_map/ppermute | solution.py:19
  50.8 10.8 %collective-permute-start.13 = (bf16[256,896]{1,0:T(8,128)(2,1)S(1)}, bf16[256,896]{1,0:T(8,128)(2,1)S(1)}, u32[]{:S(2)}, u32[]{:S(2)}) collective-permute-start(bf16[256,896]{1,0:T(8,128)(2,1)S(1)} %slice.115), channel_id=1, source_target_pairs={{0,2},{1,3},{2,0},{3,1},{4,6},{5,7},{6,4},{7,5},{8,10},{9,11},{10,... | collective-permute-start | bytes 1376264 | tf_op jit(solution)/shard_map/ppermute | solution.py:19
  62.8 1.9 %collective-permute-start.15 = (bf16[128,1792]{1,0:T(8,128)(2,1)S(1)}, bf16[128,1792]{1,0:T(8,128)(2,1)S(1)}, u32[]{:S(2)}, u32[]{:S(2)}) collective-permute-start(bf16[128,1792]{1,0:T(8,128)(2,1)S(1)} %get-tuple-element.10), channel_id=1, source_target_pairs={{0,1},{1,0},{2,3},{3,2},{4,5},{5,4},{6,7},{7,6},{8,9},{9,8},{10,11... | collective-permute-start | bytes 1376264 | tf_op jit(solution)/shard_map/ppermute | solution.py:19
  64.8 6.8 %collective-permute-start.16 = (bf16[32,1792]{1,0:T(8,128)(2,1)S(1)}, bf16[32,1792]{1,0:T(8,128)(2,1)S(1)}, u32[]{:S(2)}, u32[]{:S(2)}) collective-permute-start(bf16[32,1792]{1,0:T(8,128)(2,1)S(1)} %get-tuple-element.13), channel_id=1, source_target_pairs={{0,8},{4,12},{8,0},{12,4},{16,24},{20,28},{24,16},{28,20},{1,9},{5... | collective-permute-start | bytes 344072 | tf_op jit(solution)/shard_map/ppermute | solution.py:19
  66.3 11.8 %collective-permute-start.17 = (bf16[32,1792]{1,0:T(8,128)(2,1)S(1)}, bf16[32,1792]{1,0:T(8,128)(2,1)S(1)}, u32[]{:S(2)}, u32[]{:S(2)}) collective-permute-start(bf16[32,1792]{1,0:T(8,128)(2,1)S(1)} %get-tuple-element.12), channel_id=1, source_target_pairs={{0,16},{4,20},{8,24},{12,28},{16,0},{20,4},{24,8},{28,12},{1,17},{... | collective-permute-start | bytes 344072 | tf_op jit(solution)/shard_map/ppermute | solution.py:19
  67.9 10.2 %collective-permute-start.18 = (bf16[32,1792]{1,0:T(8,128)(2,1)S(1)}, bf16[32,1792]{1,0:T(8,128)(2,1)S(1)}, u32[]{:S(2)}, u32[]{:S(2)}) collective-permute-start(bf16[32,1792]{1,0:T(8,128)(2,1)S(1)} %get-tuple-element.11), channel_id=1, source_target_pairs={{0,24},{4,28},{8,16},{12,20},{16,8},{20,12},{24,0},{28,4},{1,25},{... | collective-permute-start | bytes 344072 | tf_op jit(solution)/shard_map/ppermute | solution.py:19
  78.2 0.8 copy-start.3

commit v3 on v2

v3 whole, which is shorter than its diff:
```python
import functools

import jax
import jax.numpy as jnp
from jax import lax
from jax.experimental import pallas as pl
from jax.experimental.pallas import tpu as pltpu
from jax.sharding import PartitionSpec as P

VLAT = 512

score_scale = 192.0 ** (-0.5)

VMEM = pl.BlockSpec(memory_space=pltpu.VMEM)
SMEM = pl.BlockSpec(memory_space=pltpu.SMEM)


def send(value, axis, size, shift):
    return lax.ppermute(value, axis, [(i, i ^ shift) for i in range(size)])


def after(value, *others):
    return lax.optimization_barrier((value, *others))[0]


def route(value, count, heads, shift):
    pairs = [
        (c * heads + e, (c ^ shift[e % 2][0]) * heads + (e ^ shift[e % 2][1]))
        for c in range(count)
        for e in range(heads)
    ]
    return lax.ppermute(value, ("ctx", "exp"), pairs)


def gather_latents(own, ctx, core, count, heads):
    shifts = [(low, low + 1) for low in range(count - 2, 1, -2)]
    mine = [route(own, count, heads, ((even, 0), (odd, 0))) for even, odd in shifts]
    beside = send(own, "ctx", count, 1)
    other = [send(block, "exp", heads, 1) for block in mine]
    blocks, owners = [own], [ctx]
    for (even, odd), a, b in zip(shifts, mine, other):
        blocks += [a, b]
        owners += [ctx ^ jnp.where(core == 0, even, odd), ctx ^ jnp.where(core == 0, odd, even)]
    return blocks + [beside], owners + [ctx ^ 1]


def attend(part, low, place, query, *refs):
    *blocks, value_up, values, keys = refs
    own_heads, tokens, _ = query.shape
    width = blocks[0].shape[1]
    count = len(blocks)
    for j, block in enumerate(blocks):
        keys[:, j * width : (j + 1) * width] = block[...]
    ctx, exp = place[count], place[count + 1]
    row = lax.broadcasted_iota(jnp.int32, (tokens, width), 0) + low
    row = ((row // part) ^ exp) * part + row % part
    col = lax.broadcasted_iota(jnp.int32, (tokens, width), 1)
    inside = col <= row
    group = own_heads
    for first in range(0, own_heads, group):
        rows = query[first : first + group].reshape(group * tokens, -1)
        scores = jnp.dot(rows, keys[...], preferred_element_type=jnp.float32) * score_scale
        pieces = [
            jnp.where(jnp.concatenate([inside] * group, 0), scores[:, :width], -1e30)
        ]
        for j in range(1, count):
            pieces.append(jnp.where(place[j] < ctx, scores[:, j * width : (j + 1) * width], -1e30))
        scores = jnp.concatenate(pieces, 1)
        expo = jnp.exp(scores - jnp.max(scores, axis=1, keepdims=True))
        total = jnp.sum(expo, axis=1, keepdims=True)
        context = lax.dot_general(
            expo.astype(jnp.bfloat16),
            keys[:VLAT],
            (((1,), (1,)), ((), ())),
            preferred_element_type=jnp.float32,
        )
        context = (context / total).astype(jnp.bfloat16)
        for h in range(group):
            up = jnp.dot(
                context[h * tokens : (h + 1) * tokens], value_up[first + h], preferred_element_type=jnp.float32
            )
            depth = value_up.shape[2]
            values[:, (first + h) * depth : (first + h + 1) * depth] = up.astype(values.dtype)


def project(place, values, own, first, second, corner, *refs):
    *rest, keep, away = refs
    half = values.shape[0] // 2
    depth, width = own.shape

    def columns(at, pieces):
        total = None
        for j, piece in enumerate(pieces):
            term = jnp.dot(
                values[:, j * depth : (j + 1) * depth], piece[...], preferred_element_type=jnp.float32
            )
            total = term if total is None else total + term
        keep[:, at : at + width] = total[:half]
        away[:, at : at + width] = total[half:].astype(away.dtype)

    def both(across, beside):
        columns(0, [own, across, *rest[::2]])
        columns(width, [beside, corner, *rest[1::2]])

    @pl.when(place[0] == 0)
    def _():
        both(first, second)

    @pl.when(place[0] != 0)
    def _():
        both(second, first)


def shards(queries, latents, value_up, out_weight):
    count, heads = lax.axis_size("ctx"), lax.axis_size("exp")
    ctx, exp = lax.axis_index("ctx"), lax.axis_index("exp")
    core = exp % 2
    tokens, own_heads, lat = queries.shape
    part = tokens // heads
    width = out_weight.shape[1]
    inner = own_heads * value_up.shape[2]

    first = route(out_weight, count, heads, ((0, 2), (1, 0)))
    blocks, owners = gather_latents(latents.T, ctx, core, count, heads)
    second = route(out_weight, count, heads, ((1, 0), (0, 2)))
    corner = route(first, count, heads, ((1, 0), (0, 2)))
    rest = []
    for s in range(4, heads, 2):
        rest += [send(out_weight, "exp", heads, s), route(out_weight, count, heads, ((1, s), (1, s)))]

    order = exp ^ jnp.arange(heads)
    rows = jnp.take(queries.reshape(heads, part, own_heads, lat), order, axis=0)
    rows = rows.reshape(tokens, own_heads, lat).transpose(1, 0, 2)
    rows = after(rows, first)
    place = jnp.stack(owners + [ctx, exp]).astype(jnp.int32)

    def attention(low, high):
        size = high - low
        return pl.pallas_call(
            functools.partial(attend, part, low),
            out_shape=jax.ShapeDtypeStruct((size, inner), jnp.bfloat16),
            in_specs=[SMEM] + [VMEM] * (len(blocks) + 2),
            out_specs=VMEM,
            scratch_shapes=[pltpu.VMEM((lat, count * tokens), jnp.bfloat16)],
            compiler_params=pltpu.CompilerParams(vmem_limit_bytes=48 * 2**20),
            cost_estimate=pl.CostEstimate(
                flops=2 * size * own_heads * count * tokens * (lat + VLAT),
                bytes_accessed=2 * (rows.size + value_up.size + count * latents.size),
                transcendentals=size * own_heads * count * tokens,
            ),
        )(place, rows[:, low:high], *blocks, value_up)

    away = attention(2 * part, tokens)
    away = [send(away[(s - 2) * part : s * part], "exp", heads, s) for s in range(2, heads, 2)]
    held = jnp.concatenate([attention(0, 2 * part)] + away, 1)
    held = after(held, second)
    gathered = [held] + [send(held, "ctx", count, s) for s in range(2, count, 2)]
    gathered = jnp.concatenate([g[:part] for g in gathered] + [g[part:] for g in gathered], 0)

    mine = count // 2 * part
    keep, away = pl.pallas_call(
        project,
        out_shape=(
            jax.ShapeDtypeStruct((mine, 2 * width), jnp.float32),
            jax.ShapeDtypeStruct((mine, 2 * width), jnp.bfloat16),
        ),
        in_specs=[SMEM] + [VMEM] * (5 + len(rest)),
        out_specs=(VMEM, VMEM),
        compiler_params=pltpu.CompilerParams(vmem_limit_bytes=48 * 2**20),
        cost_estimate=pl.CostEstimate(
            flops=2 * gathered.size * 2 * width,
            bytes_accessed=2 * (gathered.size + 2 * width * gathered.shape[1]) + 6 * mine * 2 * width,
            transcendentals=0,
        ),
    )(core[None].astype(jnp.int32), gathered, out_weight, first, second, corner, *rest)
    result = (keep + send(away, "exp", heads, 1).astype(jnp.float32)).astype(jnp.bfloat16)
    result = result.reshape(count // 2, part, 2 * width)
    final = jnp.zeros((part, count * width), jnp.bfloat16)
    for s in range(0, count, 2):
        block = result[s // 2]
        if s:
            block = send(block, "ctx", count, s)
        for side in range(2):
            final = lax.dynamic_update_slice(
                final, block[:, side * width : (side + 1) * width], (0, (ctx ^ (s + side)) * width)
            )
    return final


def solution(mesh):
    in_specs = (P("ctx", "exp", None), P("ctx", None), P("exp", None, None), P("exp", "ctx"))
    out_specs = P(("ctx", "exp"), None)
    return jax.shard_map(shards, mesh=mesh, in_specs=in_specs, out_specs=out_specs, check_vma=False)
```

time: 79.7 us -> 67.9 us (0.85)
  waiting for transfers between devices: 48.6 us -> 27.5 us
  local copies, waits for them, and re-layouts: 4.1 us -> 8.61 us
  starting transfers between devices: 22.1 us -> 26 us
    ppermute x15 -> x12, waiting for transfers between devices: 39.7 us -> 25.1 us  [send(): return lax.ppermute(value, axis, [(i, i ^ shift) for i in range(size)])]
    ppermute x4 -> x6, waiting for transfers between devices: 8.82 us -> 2.4 us  [route(): return lax.ppermute(value, ('ctx', 'exp'), pairs)]
    ppermute x4 -> x6, starting transfers between devices: 7.35 us -> 10.4 us  [route(): return lax.ppermute(value, ('ctx', 'exp'), pairs)]
    gather x2, local copies, waits for them, and re-layouts: 0.73 us -> 2.64 us  [shards(): rows = jnp.take(queries.reshape(heads, part, own_heads, lat), order, axis=0)]
    unnamed x14 -> x16, local copies, waits for them, and re-layouts: 2.17 us -> 3.71 us
    reshape x1, local copies, waits for them, and re-layouts: 0.07 us -> 1.15 us  [shards(): rows = jnp.take(queries.reshape(heads, part, own_heads, lat), order, axis=0)]
    ppermute x15 -> x12, starting transfers between devices: 14.8 us -> 15.6 us  [send(): return lax.ppermute(value, axis, [(i, i ^ shift) for i in range(size)])]
    pallas_call x2 -> x3, Pallas kernels: 4.19 us -> 4.95 us  [the longest x2 3.68 us: attention(): pl.pallas_call(functools.partial(attend, part, low), out_shape=jax.ShapeD...]
  transfers between devices with their start and end apart: 19 -> 18, of which waited for: 13 -> 8; matrix products, arithmetic and copies ran while one was open for 4% -> 10% of each run, Pallas kernels for 0% -> 5%
where the time goes in v3:
time: 67.9 us; the launch traced here: 67.7 us
  waiting for transfers between devices  27.5 us (41%)
  starting transfers between devices  26 us (38%)
  local copies, waits for them, and re-layouts  8.61 us (13%)
  Pallas kernels  4.95 us (7%)
    ppermute x12, waiting for transfers between devices, send(): return lax.ppermute(value, axis, [(i, i ^ shift) for i in range(size)])  25.1 us
    ppermute x12, starting transfers between devices, send(): return lax.ppermute(value, axis, [(i, i ^ shift) for i in range(size)])  15.6 us
    ppermute x6, starting transfers between devices, route(): return lax.ppermute(value, ('ctx', 'exp'), pairs)  10.4 us
    unnamed x16, local copies, waits for them, and re-layouts  3.71 us
    pallas_call x2, Pallas kernels, attention(): pl.pallas_call(functools.partial(attend, part, low), out_shape=jax.ShapeD...  3.68 us
    gather x2, local copies, waits for them, and re-layouts, shards(): rows = jnp.take(queries.reshape(heads, part, own_heads, lat), order, axis=0)  2.64 us
    ppermute x6, waiting for transfers between devices, route(): return lax.ppermute(value, ('ctx', 'exp'), pairs)  2.4 us
  transfers between devices with their start and end apart: 18, of which 8 were waited for; matrix products, arithmetic and copies ran while one was open for 10% of the time, Pallas kernels for 5%

profile of v3, /device:TPU:0, one launch (start us, length us, event | category | flops | bytes accessed | tf_op | source)
XLA Modules:
  0.0 67.7 jit_solution(3884172701343831746)
XLA Ops:
  0.0 2.9 %collective-permute-start = (bf16[512,896]{1,0:T(8,128)(2,1)}, bf16[512,896]{1,0:T(8,128)(2,1)S(1)}, u32[]{:S(2)}, u32[]{:S(2)}) collective-permute-start(bf16[512,896]{1,0:T(8,128)(2,1)} %own.1), channel_id=1, source_target_pairs={{0,2},{1,5},{2,0},{3,7},{4,6},{5,1},{6,4},{7,3},{8,10},{9,13},{10,... | collective-permute-start | bytes 2752520 | tf_op jit(solution)/shard_map/ppermute | solution.py:32
  2.9 3.6 %collective-permute-start.1 = (bf16[576,128]{1,0:T(8,128)(2,1)}, bf16[576,128]{1,0:T(8,128)(2,1)S(1)}, u32[]{:S(2)}, u32[]{:S(2)}) collective-permute-start(bf16[576,128]{1,0:T(8,128)(2,1)} %bitcast.17), channel_id=1, source_target_pairs={{0,24},{1,29},{2,26},{3,31},{4,28},{5,25},{6,30},{7,27},{8,16},{9,... | collective-permute-start | bytes 442376 | tf_op jit(solution)/shard_map/ppermute | solution.py:32
  6.5 0.8 %collective-permute-start.5 = (bf16[576,128]{1,0:T(8,128)(2,1)}, bf16[576,128]{1,0:T(8,128)(2,1)S(1)}, u32[]{:S(2)}, u32[]{:S(2)}) collective-permute-start(bf16[576,128]{1,0:T(8,128)(2,1)} %bitcast.19), channel_id=1, source_target_pairs={{0,8},{1,13},{2,10},{3,15},{4,12},{5,9},{6,14},{7,11},{8,0},{9,5},... | collective-permute-start | bytes 442376 | tf_op jit(solution)/shard_map/ppermute | solution.py:32
  7.3 1.5 %collective-permute-start.9 = (bf16[512,896]{1,0:T(8,128)(2,1)}, bf16[512,896]{1,0:T(8,128)(2,1)S(1)}, u32[]{:S(2)}, u32[]{:S(2)}) collective-permute-start(bf16[512,896]{1,0:T(8,128)(2,1)} %own.1), channel_id=1, source_target_pairs={{0,4},{1,3},{2,6},{3,1},{4,0},{5,7},{6,2},{7,5},{8,12},{9,11},{10,... | collective-permute-start | bytes 2752520 | tf_op jit(solution)/shard_map/ppermute | solution.py:32
  8.8 2.2 %copy.5 = bf16[128,4,576]{2,0,1:T(8,128)(2,1)} copy(bf16[128,4,576]{0,2,1:T(8,128)(2,1)} %param.4) | data formatting | bytes 1179648 | tf_op args[0]
  11.0 1.2 %copy.6 = bf16[4,32,4,576]{3,1,2,0:T(8,128)(2,1)S(1)} copy(bf16[4,32,4,576]{3,1,0,2:T(8,128)(2,1)} %bitcast.24) | data formatting | bytes 1179648 | tf_op jit(solution)/shard_map/reshape | solution.py:132
  12.2 1.5 %gather_fusion = bf16[4,32,4,576]{3,1,2,0:T(8,128)(2,1)} fusion(bf16[4,32,4,576]{3,1,2,0:T(8,128)(2,1)S(1)} %copy.6, s32[1024]{0:T(1024)S(1)} %pad_clamp_fusion), kind=kCustom, calls=%fused_computation | custom fusion | bytes 1179664 | tf_op jit(solution)/shard_map/jit(_take)/gather | solution.py:132
  13.7 1.2 %copy.7 = bf16[4,32,4,576]{3,1,0,2:T(8,128)(2,1)S(1)} copy(bf16[4,32,4,576]{3,1,2,0:T(8,128)(2,1)} %gather_fusion) | data formatting | bytes 1179648 | tf_op jit(solution)/shard_map/jit(_take)/gather | solution.py:132
  15.3 0.7 %copy-done.2 = bf16[128,576]{0,1:T(8,128)(2,1)S(1)} copy-done((bf16[128,576]{0,1:T(8,128)(2,1)S(1)}, bf16[128,576]{0,1:T(8,128)(2,1)}, u32[]{:S(2)}) %copy-start.2) | copy-done | bytes 147480
  16.0 0.5 collective-permute-start.7
  16.5 2.4 %collective-permute-done.3.refs_3_ = bf16[576,128]{1,0:T(8,128)(2,1)S(1)} collective-permute-done((bf16[576,128]{1,0:T(8,128)(2,1)}, bf16[576,128]{1,0:T(8,128)(2,1)S(1)}, u32[]{:S(2)}, u32[]{:S(2)}) %collective-permute-start.3) | collective-permute-done | bytes 147488 | tf_op jit(solution)/shard_map/ppermute | solution.py:32
  18.9 0.5 collective-permute-start.4
  19.4 3.8 %collective-permute-start.6 = (bf16[576,128]{1,0:T(8,128)(2,1)S(1)}, bf16[576,128]{1,0:T(8,128)(2,1)S(1)}, u32[]{:S(2)}, u32[]{:S(2)}) collective-permute-start(bf16[576,128]{1,0:T(8,128)(2,1)S(1)} %collective-permute-done.5.refs_5_), channel_id=1, source_target_pairs={{0,1},{1,0},{2,3},{3,2},{4,5},{5,4},{6,7},{7,6},{8,9},{9,8},{10,11... | collective-permute-start | bytes 442376 | tf_op jit(solution)/shard_map/ppermute | solution.py:19
  23.4 8.1 %collective-permute-done.7.refs_7_ = bf16[576,128]{1,0:T(8,128)(2,1)S(1)} collective-permute-done((bf16[576,128]{1,0:T(8,128)(2,1)S(1)}, bf16[576,128]{1,0:T(8,128)(2,1)S(1)}, u32[]{:S(2)}, u32[]{:S(2)}) %collective-permute-start.7) | collective-permute-done | bytes 147488 | tf_op jit(solution)/shard_map/ppermute | solution.py:19
  31.4 1.8 %shard_map.47 = bf16[64,512]{1,0:T(8,128)(2,1)S(1)} custom-call(s32[10]{0:T(128)S(1)} %stack.40.place, bf16[4,64,576]{2,1,0:T(8,128)(2,1)S(1)} %get-tuple-element.14.query, bf16[576,128]{1,0:T(8,128)(2,1)S(1)} %bitcast.21, bf16[576,128]{1,0:T(8,128)(2,1)S(1)} %collective-permute-done.1.refs_1_, bf16[576,128]{1,0:T(8,128)(2,1)S(1)} %collective-permute-done.2.refs_2_, ...), custom_call_target="tpu_custom_call" | custom-call | flops 570425344 | bytes 2293760 | tf_op jit(solution)/shard_map/pallas_call | solution.py:139
  33.3 1.8 %collective-permute-start.8 = (bf16[64,512]{1,0:T(8,128)(2,1)S(1)}, bf16[64,512]{1,0:T(8,128)(2,1)S(1)}, u32[]{:S(2)}, u32[]{:S(2)}) collective-permute-start(bf16[64,512]{1,0:T(8,128)(2,1)S(1)} %shard_map.47), channel_id=1, source_target_pairs={{0,2},{1,3},{2,0},{3,1},{4,6},{5,7},{6,4},{7,5},{8,10},{9,11},{10,... | collective-permute-start | bytes 196616 | tf_op jit(solution)/shard_map/ppermute | solution.py:19
  35.1 1.5 %collective-permute-start.13 = (bf16[512,896]{1,0:T(8,128)(2,1)S(1)}, bf16[512,896]{1,0:T(8,128)(2,1)S(1)}, u32[]{:S(2)}, u32[]{:S(2)}) collective-permute-start(bf16[512,896]{1,0:T(8,128)(2,1)S(1)} %collective-permute-done.first), channel_id=1, source_target_pairs={{0,4},{1,3},{2,6},{3,1},{4,0},{5,7},{6,2},{7,5},{8,12},{9,11},{10,... | collective-permute-start | bytes 2752520 | tf_op jit(solution)/shard_map/ppermute | solution.py:32
  36.6 1.8 %shard_map.46 = bf16[64,512]{1,0:T(8,128)(2,1)S(1)} custom-call(s32[10]{0:T(128)S(1)} %stack.40.place, bf16[4,64,576]{2,1,0:T(8,128)(2,1)S(1)} %get-tuple-element.13.query, bf16[576,128]{1,0:T(8,128)(2,1)S(1)} %bitcast.22, bf16[576,128]{1,0:T(8,128)(2,1)S(1)} %collective-permute-done.1.refs_1_, bf16[576,128]{1,0:T(8,128)(2,1)S(1)} %collective-permute-done.2.refs_2_, ...), custom_call_target="tpu_custom_call" | custom-call | flops 570425344 | bytes 2293760 | tf_op jit(solution)/shard_map/pallas_call | solution.py:139
  38.5 1.8 %collective-permute-start.10 = (bf16[64,1024]{1,0:T(8,128)(2,1)S(1)}, bf16[64,1024]{1,0:T(8,128)(2,1)S(1)}, u32[]{:S(2)}, u32[]{:S(2)}) collective-permute-start(bf16[64,1024]{1,0:T(8,128)(2,1)S(1)} %pad_maximum_fusion), channel_id=1, source_target_pairs={{0,8},{4,12},{8,0},{12,4},{16,24},{20,28},{24,16},{28,20},{1,9},{5... | collective-permute-start | bytes 393224 | tf_op jit(solution)/shard_map/ppermute | solution.py:19
  40.3 2.6 %collective-permute-start.11 = (bf16[64,1024]{1,0:T(8,128)(2,1)S(1)}, bf16[64,1024]{1,0:T(8,128)(2,1)S(1)}, u32[]{:S(2)}, u32[]{:S(2)}) collective-permute-start(bf16[64,1024]{1,0:T(8,128)(2,1)S(1)} %pad_maximum_fusion), channel_id=1, source_target_pairs={{0,16},{4,20},{8,24},{12,28},{16,0},{20,4},{24,8},{28,12},{1,17},{... | collective-permute-start | bytes 393224 | tf_op jit(solution)/shard_map/ppermute | solution.py:19
  43.0 0.6 collective-permute-done.10
  43.5 4.0 %collective-permute-done.11 = bf16[64,1024]{1,0:T(8,128)(2,1)S(1)} collective-permute-done((bf16[64,1024]{1,0:T(8,128)(2,1)S(1)}, bf16[64,1024]{1,0:T(8,128)(2,1)S(1)}, u32[]{:S(2)}, u32[]{:S(2)}) %collective-permute-start.11) | collective-permute-done | bytes 131104 | tf_op jit(solution)/shard_map/ppermute | solution.py:19
  47.6 2.2 %collective-permute-done.12 = bf16[64,1024]{1,0:T(8,128)(2,1)S(1)} collective-permute-done((bf16[64,1024]{1,0:T(8,128)(2,1)S(1)}, bf16[64,1024]{1,0:T(8,128)(2,1)S(1)}, u32[]{:S(2)}, u32[]{:S(2)}) %collective-permute-start.12) | collective-permute-done | bytes 131104 | tf_op jit(solution)/shard_map/ppermute | solution.py:19
  49.8 1.3 %shard_map.48 = (f32[128,1792]{1,0:T(8,128)S(1)}, bf16[128,1792]{1,0:T(8,128)(2,1)S(1)}) custom-call(s32[1]{0:T(128)} %bitcast.place, bf16[256,1024]{1,0:T(8,128)(2,1)S(1)} %slice_dynamic-update-slice_fusion.values, bf16[512,896]{1,0:T(8,128)(2,1)S(1)} %copy-done, bf16[512,896]{1,0:T(8,128)(2,1)S(1)} %collective-permute-done.first, ...), custom_call_target="tpu_custom_call" | custom-call | flops 939524096 | bytes 5570560 | tf_op jit(solution)/shard_map/pallas_call | solution.py:161
  51.2 1.8 %collective-permute-done.14 = bf16[128,1792]{1,0:T(8,128)(2,1)S(1)} collective-permute-done((bf16[128,1792]{1,0:T(8,128)(2,1)S(1)}, bf16[128,1792]{1,0:T(8,128)(2,1)S(1)}, u32[]{:S(2)}, u32[]{:S(2)}) %collective-permute-start.14) | collective-permute-done | bytes 458784 | tf_op jit(solution)/shard_map/ppermute | solution.py:19
  53.1 1.3 %collective-permute-start.15 = (bf16[32,1792]{1,0:T(8,128)(2,1)S(1)}, bf16[32,1792]{1,0:T(8,128)(2,1)S(1)}, u32[]{:S(2)}, u32[]{:S(2)}) collective-permute-start(bf16[32,1792]{1,0:T(8,128)(2,1)S(1)} %get-tuple-element.17), channel_id=1, source_target_pairs={{0,8},{4,12},{8,0},{12,4},{16,24},{20,28},{24,16},{28,20},{1,9},{5... | collective-permute-start | bytes 344072 | tf_op jit(solution)/shard_map/ppermute | solution.py:19
  54.3 1.6 %collective-permute-start.16 = (bf16[32,1792]{1,0:T(8,128)(2,1)S(1)}, bf16[32,1792]{1,0:T(8,128)(2,1)S(1)}, u32[]{:S(2)}, u32[]{:S(2)}) collective-permute-start(bf16[32,1792]{1,0:T(8,128)(2,1)S(1)} %get-tuple-element.16), channel_id=1, source_target_pairs={{0,16},{4,20},{8,24},{12,28},{16,0},{20,4},{24,8},{28,12},{1,17},{... | collective-permute-start | bytes 344072 | tf_op jit(solution)/shard_map/ppermute | solution.py:19
  56.0 1.6 %collective-permute-start.17 = (bf16[32,1792]{1,0:T(8,128)(2,1)S(1)}, bf16[32,1792]{1,0:T(8,128)(2,1)S(1)}, u32[]{:S(2)}, u32[]{:S(2)}) collective-permute-start(bf16[32,1792]{1,0:T(8,128)(2,1)S(1)} %get-tuple-element.15), channel_id=1, source_target_pairs={{0,24},{4,28},{8,16},{12,20},{16,8},{20,12},{24,0},{28,4},{1,25},{... | collective-permute-start | bytes 344072 | tf_op jit(solution)/shard_map/ppermute | solution.py:19
  57.6 2.3 %collective-permute-done.15 = bf16[32,1792]{1,0:T(8,128)(2,1)S(1)} collective-permute-done((bf16[32,1792]{1,0:T(8,128)(2,1)S(1)}, bf16[32,1792]{1,0:T(8,128)(2,1)S(1)}, u32[]{:S(2)}, u32[]{:S(2)}) %collective-permute-start.15) | collective-permute-done | bytes 114720 | tf_op jit(solution)/shard_map/ppermute | solution.py:19
  60.0 6.2 %collective-permute-done.16 = bf16[32,1792]{1,0:T(8,128)(2,1)S(1)} collective-permute-done((bf16[32,1792]{1,0:T(8,128)(2,1)S(1)}, bf16[32,1792]{1,0:T(8,128)(2,1)S(1)}, u32[]{:S(2)}, u32[]{:S(2)}) %collective-permute-start.16) | collective-permute-done | bytes 114720 | tf_op jit(solution)/shard_map/ppermute | solution.py:19
  66.3 0.8 %copy-done.3 = bf16[32,7168]{1,0:T(8,128)(2,1)} copy-done((bf16[32,7168]{1,0:T(8,128)(2,1)}, bf16[32,7168]{1,0:T(8,128)(2,1)S(1)}, u32[]{:S(2)}) %copy-start.3) | copy-done | bytes 458776
  67.0 0.6 slice_dynamic-update-slice_fusion.8
  (47 shorter events, 1.0 us)
Async XLA Ops:
  0.0 19.4 %collective-permute-start = (bf16[512,896]{1,0:T(8,128)(2,1)}, bf16[512,896]{1,0:T(8,128)(2,1)S(1)}, u32[]{:S(2)}, u32[]{:S(2)}) collective-permute-start(bf16[512,896]{1,0:T(8,128)(2,1)} %own.1), channel_id=1, source_target_pairs={{0,2},{1,5},{2,0},{3,7},{4,6},{5,1},{6,4},{7,3},{8,10},{9,13},{10,... | collective-permute-start | bytes 2752520 | tf_op jit(solution)/shard_map/ppermute | solution.py:32
  2.9 12.4 %collective-permute-start.1 = (bf16[576,128]{1,0:T(8,128)(2,1)}, bf16[576,128]{1,0:T(8,128)(2,1)S(1)}, u32[]{:S(2)}, u32[]{:S(2)}) collective-permute-start(bf16[576,128]{1,0:T(8,128)(2,1)} %bitcast.17), channel_id=1, source_target_pairs={{0,24},{1,29},{2,26},{3,31},{4,28},{5,25},{6,30},{7,27},{8,16},{9,... | collective-permute-start | bytes 442376 | tf_op jit(solution)/shard_map/ppermute | solution.py:32
  6.5 12.4 %collective-permute-start.3 = (bf16[576,128]{1,0:T(8,128)(2,1)}, bf16[576,128]{1,0:T(8,128)(2,1)S(1)}, u32[]{:S(2)}, u32[]{:S(2)}) collective-permute-start(bf16[576,128]{1,0:T(8,128)(2,1)} %bitcast.18), channel_id=1, source_target_pairs={{0,16},{1,21},{2,18},{3,23},{4,20},{5,17},{6,22},{7,19},{8,24},{9,... | collective-permute-start | bytes 442376 | tf_op jit(solution)/shard_map/ppermute | solution.py:32
  6.5 12.4 %collective-permute-start.5 = (bf16[576,128]{1,0:T(8,128)(2,1)}, bf16[576,128]{1,0:T(8,128)(2,1)S(1)}, u32[]{:S(2)}, u32[]{:S(2)}) collective-permute-start(bf16[576,128]{1,0:T(8,128)(2,1)} %bitcast.19), channel_id=1, source_target_pairs={{0,8},{1,13},{2,10},{3,15},{4,12},{5,9},{6,14},{7,11},{8,0},{9,5},... | collective-permute-start | bytes 442376 | tf_op jit(solution)/shard_map/ppermute | solution.py:32
  7.3 31.2 %collective-permute-start.9 = (bf16[512,896]{1,0:T(8,128)(2,1)}, bf16[512,896]{1,0:T(8,128)(2,1)S(1)}, u32[]{:S(2)}, u32[]{:S(2)}) collective-permute-start(bf16[512,896]{1,0:T(8,128)(2,1)} %own.1), channel_id=1, source_target_pairs={{0,4},{1,3},{2,6},{3,1},{4,0},{5,7},{6,2},{7,5},{8,12},{9,11},{10,... | collective-permute-start | bytes 2752520 | tf_op jit(solution)/shard_map/ppermute | solution.py:32
  15.1 0.9 %copy-start.2 = (bf16[128,576]{0,1:T(8,128)(2,1)S(1)}, bf16[128,576]{0,1:T(8,128)(2,1)}, u32[]{:S(2)}) copy-start(bf16[128,576]{0,1:T(8,128)(2,1)} %param.5) | copy-start | bytes 442372
  16.0 15.4 %collective-permute-start.7 = (bf16[576,128]{1,0:T(8,128)(2,1)S(1)}, bf16[576,128]{1,0:T(8,128)(2,1)S(1)}, u32[]{:S(2)}, u32[]{:S(2)}) collective-permute-start(bf16[576,128]{1,0:T(8,128)(2,1)S(1)} %bitcast.20), channel_id=1, source_target_pairs={{0,4},{4,0},{8,12},{12,8},{16,20},{20,16},{24,28},{28,24},{1,5},{5... | collective-permute-start | bytes 442376 | tf_op jit(solution)/shard_map/ppermute | solution.py:19
  18.9 12.5 %collective-permute-start.2 = (bf16[576,128]{1,0:T(8,128)(2,1)S(1)}, bf16[576,128]{1,0:T(8,128)(2,1)S(1)}, u32[]{:S(2)}, u32[]{:S(2)}) collective-permute-start(bf16[576,128]{1,0:T(8,128)(2,1)S(1)} %collective-permute-done.1.refs_1_), channel_id=1, source_target_pairs={{0,1},{1,0},{2,3},{3,2},{4,5},{5,4},{6,7},{7,6},{8,9},{9,8},{10,11... | collective-permute-start | bytes 442376 | tf_op jit(solution)/shard_map/ppermute | solution.py:19
  18.9 12.5 %collective-permute-start.4 = (bf16[576,128]{1,0:T(8,128)(2,1)S(1)}, bf16[576,128]{1,0:T(8,128)(2,1)S(1)}, u32[]{:S(2)}, u32[]{:S(2)}) collective-permute-start(bf16[576,128]{1,0:T(8,128)(2,1)S(1)} %collective-permute-done.3.refs_3_), channel_id=1, source_target_pairs={{0,1},{1,0},{2,3},{3,2},{4,5},{5,4},{6,7},{7,6},{8,9},{9,8},{10,11... | collective-permute-start | bytes 442376 | tf_op jit(solution)/shard_map/ppermute | solution.py:19
  19.4 12.0 %collective-permute-start.6 = (bf16[576,128]{1,0:T(8,128)(2,1)S(1)}, bf16[576,128]{1,0:T(8,128)(2,1)S(1)}, u32[]{:S(2)}, u32[]{:S(2)}) collective-permute-start(bf16[576,128]{1,0:T(8,128)(2,1)S(1)} %collective-permute-done.5.refs_5_), channel_id=1, source_target_pairs={{0,1},{1,0},{2,3},{3,2},{4,5},{5,4},{6,7},{7,6},{8,9},{9,8},{10,11... | collective-permute-start | bytes 442376 | tf_op jit(solution)/shard_map/ppermute | solution.py:19
  23.3 8.2 %copy-start.1 = (bf16[4,512,128]{2,1,0:T(8,128)(2,1)S(1)}, bf16[4,512,128]{2,1,0:T(8,128)(2,1)}, u32[]{:S(2)}) copy-start(bf16[4,512,128]{2,1,0:T(8,128)(2,1)} %refs_8_.3) | copy-start | bytes 1572868
  33.3 5.2 %collective-permute-start.8 = (bf16[64,512]{1,0:T(8,128)(2,1)S(1)}, bf16[64,512]{1,0:T(8,128)(2,1)S(1)}, u32[]{:S(2)}, u32[]{:S(2)}) collective-permute-start(bf16[64,512]{1,0:T(8,128)(2,1)S(1)} %shard_map.47), channel_id=1, source_target_pairs={{0,2},{1,3},{2,0},{3,1},{4,6},{5,7},{6,4},{7,5},{8,10},{9,11},{10,... | collective-permute-start | bytes 196616 | tf_op jit(solution)/shard_map/ppermute | solution.py:19
  35.1 14.7 %collective-permute-start.13 = (bf16[512,896]{1,0:T(8,128)(2,1)S(1)}, bf16[512,896]{1,0:T(8,128)(2,1)S(1)}, u32[]{:S(2)}, u32[]{:S(2)}) collective-permute-start(bf16[512,896]{1,0:T(8,128)(2,1)S(1)} %collective-permute-done.first), channel_id=1, source_target_pairs={{0,4},{1,3},{2,6},{3,1},{4,0},{5,7},{6,2},{7,5},{8,12},{9,11},{10,... | collective-permute-start | bytes 2752520 | tf_op jit(solution)/shard_map/ppermute | solution.py:32
  38.4 11.4 %copy-start = (bf16[512,896]{1,0:T(8,128)(2,1)S(1)}, bf16[512,896]{1,0:T(8,128)(2,1)}, u32[]{:S(2)}) copy-start(bf16[512,896]{1,0:T(8,128)(2,1)} %own.1) | copy-start | bytes 2752516
  38.5 5.0 %collective-permute-start.10 = (bf16[64,1024]{1,0:T(8,128)(2,1)S(1)}, bf16[64,1024]{1,0:T(8,128)(2,1)S(1)}, u32[]{:S(2)}, u32[]{:S(2)}) collective-permute-start(bf16[64,1024]{1,0:T(8,128)(2,1)S(1)} %pad_maximum_fusion), channel_id=1, source_target_pairs={{0,8},{4,12},{8,0},{12,4},{16,24},{20,28},{24,16},{28,20},{1,9},{5... | collective-permute-start | bytes 393224 | tf_op jit(solution)/shard_map/ppermute | solution.py:19
  40.3 7.3 %collective-permute-start.11 = (bf16[64,1024]{1,0:T(8,128)(2,1)S(1)}, bf16[64,1024]{1,0:T(8,128)(2,1)S(1)}, u32[]{:S(2)}, u32[]{:S(2)}) collective-permute-start(bf16[64,1024]{1,0:T(8,128)(2,1)S(1)} %pad_maximum_fusion), channel_id=1, source_target_pairs={{0,16},{4,20},{8,24},{12,28},{16,0},{20,4},{24,8},{28,12},{1,17},{... | collective-permute-start | bytes 393224 | tf_op jit(solution)/shard_map/ppermute | solution.py:19
  42.9 6.9 %collective-permute-start.12 = (bf16[64,1024]{1,0:T(8,128)(2,1)S(1)}, bf16[64,1024]{1,0:T(8,128)(2,1)S(1)}, u32[]{:S(2)}, u32[]{:S(2)}) collective-permute-start(bf16[64,1024]{1,0:T(8,128)(2,1)S(1)} %pad_maximum_fusion), channel_id=1, source_target_pairs={{0,24},{4,28},{8,16},{12,20},{16,8},{20,12},{24,0},{28,4},{1,25},{... | collective-permute-start | bytes 393224 | tf_op jit(solution)/shard_map/ppermute | solution.py:19
  51.1 1.9 %collective-permute-start.14 = (bf16[128,1792]{1,0:T(8,128)(2,1)S(1)}, bf16[128,1792]{1,0:T(8,128)(2,1)S(1)}, u32[]{:S(2)}, u32[]{:S(2)}) collective-permute-start(bf16[128,1792]{1,0:T(8,128)(2,1)S(1)} %get-tuple-element.12), channel_id=1, source_target_pairs={{0,1},{1,0},{2,3},{3,2},{4,5},{5,4},{6,7},{7,6},{8,9},{9,8},{10,11... | collective-permute-start | bytes 1376264 | tf_op jit(solution)/shard_map/ppermute | solution.py:19
  53.1 6.9 %collective-permute-start.15 = (bf16[32,1792]{1,0:T(8,128)(2,1)S(1)}, bf16[32,1792]{1,0:T(8,128)(2,1)S(1)}, u32[]{:S(2)}, u32[]{:S(2)}) collective-permute-start(bf16[32,1792]{1,0:T(8,128)(2,1)S(1)} %get-tuple-element.17), channel_id=1, source_target_pairs={{0,8},{4,12},{8,0},{12,4},{16,24},{20,28},{24,16},{28,20},{1,9},{5... | collective-permute-start | bytes 344072 | tf_op jit(solution)/shard_map/ppermute | solution.py:19
  54.3 11.8 %collective-permute-start.16 = (bf16[32,1792]{1,0:T(8,128)(2,1)S(1)}, bf16[32,1792]{1,0:T(8,128)(2,1)S(1)}, u32[]{:S(2)}, u32[]{:S(2)}) collective-permute-start(bf16[32,1792]{1,0:T(8,128)(2,1)S(1)} %get-tuple-element.16), channel_id=1, source_target_pairs={{0,16},{4,20},{8,24},{12,28},{16,0},{20,4},{24,8},{28,12},{1,17},{... | collective-permute-start | bytes 344072 | tf_op jit(solution)/shard_map/ppermute | solution.py:19
  56.0 10.3 %collective-permute-start.17 = (bf16[32,1792]{1,0:T(8,128)(2,1)S(1)}, bf16[32,1792]{1,0:T(8,128)(2,1)S(1)}, u32[]{:S(2)}, u32[]{:S(2)}) collective-permute-start(bf16[32,1792]{1,0:T(8,128)(2,1)S(1)} %get-tuple-element.15), channel_id=1, source_target_pairs={{0,24},{4,28},{8,16},{12,20},{16,8},{20,12},{24,0},{28,4},{1,25},{... | collective-permute-start | bytes 344072 | tf_op jit(solution)/shard_map/ppermute | solution.py:19
  66.3 0.8 %copy-start.3 = (bf16[32,7168]{1,0:T(8,128)(2,1)}, bf16[32,7168]{1,0:T(8,128)(2,1)S(1)}, u32[]{:S(2)}) copy-start(bf16[32,7168]{1,0:T(8,128)(2,1)S(1)} %slice_dynamic-update-slice_fusion.9) | copy-start | bytes 1376260

commit v4 on v3

v4 whole, which is shorter than its diff:
```python
import functools

import jax
import jax.numpy as jnp
from jax import lax
from jax.experimental import pallas as pl
from jax.experimental.pallas import tpu as pltpu
from jax.sharding import PartitionSpec as P

VLAT = 512

score_scale = 192.0 ** (-0.5)

VMEM = pl.BlockSpec(memory_space=pltpu.VMEM)
SMEM = pl.BlockSpec(memory_space=pltpu.SMEM)


def send(value, axis, size, shift):
    return lax.ppermute(value, axis, [(i, i ^ shift) for i in range(size)])


def route(value, count, heads, shift):
    pairs = [
        (c * heads + e, (c ^ shift[e % 2][0]) * heads + (e ^ shift[e % 2][1]))
        for c in range(count)
        for e in range(heads)
    ]
    return lax.ppermute(value, ("ctx", "exp"), pairs)


def after(value, *others):
    return lax.optimization_barrier((value, *others))[0]


def gather_latents(own, ctx, core, count, heads):
    shifts = [(low, low + 1) for low in range(count - 2, 1, -2)]
    mine = [route(own, count, heads, ((even, 0), (odd, 0))) for even, odd in shifts]
    beside = send(own, "ctx", count, 1)
    other = [send(block, "exp", heads, 1) for block in mine]
    blocks, owners = [own], [ctx]
    for (even, odd), a, b in zip(shifts, mine, other):
        blocks += [a, b]
        owners += [ctx ^ jnp.where(core == 0, even, odd), ctx ^ jnp.where(core == 0, odd, even)]
    return blocks + [beside], owners + [ctx ^ 1]


def attend(part, low, place, query, *refs):
    *blocks, value_up, values, keys = refs
    own_heads, tokens, _ = query.shape
    width = blocks[0].shape[1]
    count = len(blocks)
    for j, block in enumerate(blocks):
        keys[:, j * width : (j + 1) * width] = block[...]
    ctx, exp = place[count], place[count + 1]
    row = lax.broadcasted_iota(jnp.int32, (tokens, width), 0) + low
    row = ((row // part) ^ exp) * part + row % part
    col = lax.broadcasted_iota(jnp.int32, (tokens, width), 1)
    inside = jnp.concatenate([col <= row] * own_heads, 0)
    scores = jnp.dot(
        query[...].reshape(own_heads * tokens, -1), keys[...], preferred_element_type=jnp.float32
    )
    scores = scores * score_scale
    pieces = [jnp.where(inside, scores[:, :width], -1e30)]
    for j in range(1, count):
        pieces.append(jnp.where(place[j] < ctx, scores[:, j * width : (j + 1) * width], -1e30))
    scores = jnp.concatenate(pieces, 1)
    expo = jnp.exp(scores - jnp.max(scores, axis=1, keepdims=True))
    total = jnp.sum(expo, axis=1, keepdims=True)
    context = lax.dot_general(
        expo.astype(jnp.bfloat16),
        keys[:VLAT],
        (((1,), (1,)), ((), ())),
        preferred_element_type=jnp.float32,
    )
    context = (context / total).astype(jnp.bfloat16)
    depth = value_up.shape[2]
    for h in range(own_heads):
        up = jnp.dot(
            context[h * tokens : (h + 1) * tokens], value_up[h], preferred_element_type=jnp.float32
        )
        values[:, h * depth : (h + 1) * depth] = up.astype(values.dtype)


def project(chips, groups, place, *refs):
    *operands, keep, away = refs
    values, pieces = operands[:chips], operands[chips:]
    rows, width = values[0].shape[0], pieces[0].shape[1]
    values = jnp.concatenate([part[...] for part in values], 0)

    def columns(at, depth, chosen):
        total = None
        for piece in chosen:
            term = jnp.dot(
                values[:, depth : depth + piece.shape[0]], piece[...], preferred_element_type=jnp.float32
            )
            total = term if total is None else total + term
            depth += piece.shape[0]
        total = total.reshape(chips, 2, rows // 2, width)
        keep[:, at : at + width] = total[:, 0].reshape(-1, width)
        away[:, at : at + width] = total[:, 1].reshape(-1, width).astype(away.dtype)

    for core in range(2):

        @pl.when(place[0] == core)
        def _():
            for j, (depth, *chosen) in enumerate(groups):
                columns(j * width, depth, [pieces[i] for i in chosen[core]])


def shards(queries, latents, value_up, out_weight):
    count, heads = lax.axis_size("ctx"), lax.axis_size("exp")
    ctx, exp = lax.axis_index("ctx"), lax.axis_index("exp")
    core = exp % 2
    tokens, own_heads, lat = queries.shape
    part = tokens // heads
    depth, width = out_weight.shape
    inner = own_heads * value_up.shape[2]

    blocks, owners = gather_latents(latents.T, ctx, core, count, heads)
    first = route(out_weight, count, heads, ((0, 2), (1, 0)))
    second = route(after(out_weight, blocks[-1]), count, heads, ((1, 0), (0, 2)))

    order = exp ^ jnp.arange(heads)
    rows = jnp.take(queries.reshape(heads, part, own_heads, lat), order, axis=0)
    rows = rows.reshape(tokens, own_heads, lat).transpose(1, 0, 2)
    place = jnp.stack(owners + [ctx, exp]).astype(jnp.int32)

    def attention(low, high):
        size = high - low
        return pl.pallas_call(
            functools.partial(attend, part, low),
            out_shape=jax.ShapeDtypeStruct((size, inner), jnp.bfloat16),
            in_specs=[SMEM] + [VMEM] * (len(blocks) + 2),
            out_specs=VMEM,
            scratch_shapes=[pltpu.VMEM((lat, count * tokens), jnp.bfloat16)],
            compiler_params=pltpu.CompilerParams(
                vmem_limit_bytes=count * tokens * (2 * lat + 32 * size * own_heads) + 2**22
            ),
            cost_estimate=pl.CostEstimate(
                flops=2 * size * own_heads * count * tokens * (lat + VLAT),
                bytes_accessed=2 * (rows.size + value_up.size + count * latents.size),
                transcendentals=size * own_heads * count * tokens,
            ),
        )(place, rows[:, low:high], *blocks, value_up)

    away = attention(2 * part, tokens)
    away = [send(away[(s - 2) * part : s * part], "exp", heads, s) for s in range(2, heads, 2)]
    kept = attention(0, 2 * part)
    held = jnp.concatenate([kept] + away, 1)
    corner = route(after(first, kept, *away), count, heads, ((1, 0), (0, 2)))
    values = [held] + [send(held, "ctx", count, s) for s in range(2, count, 2)]

    rest = []
    for s in range(4, heads, 2):
        rest += [send(out_weight, "exp", heads, s), route(out_weight, count, heads, ((1, s), (1, s)))]

    mine = len(values) * part

    def projection(groups, *pieces):
        out = (mine, len(groups) * width)
        return pl.pallas_call(
            functools.partial(project, len(values), groups),
            out_shape=(
                jax.ShapeDtypeStruct(out, jnp.float32),
                jax.ShapeDtypeStruct(out, jnp.bfloat16),
            ),
            in_specs=[SMEM] + [VMEM] * (len(values) + len(pieces)),
            out_specs=(VMEM, VMEM),
            compiler_params=pltpu.CompilerParams(vmem_limit_bytes=2**24),
            cost_estimate=pl.CostEstimate(
                flops=4 * mine * sum(p.size for p in pieces),
                bytes_accessed=2 * (len(values) * held.size + sum(p.size for p in pieces)) + 6 * mine * out[1],
                transcendentals=0,
            ),
        )(core[None].astype(jnp.int32), *values, *pieces)

    others = list(range(3, 3 + len(rest) // 2))
    keep, away = projection(
        [(0, [0, 1, *others], [0, 2, *others]), (0, [2], [1])], out_weight, first, second, *rest[::2]
    )
    other = send(away, "exp", heads, 1).astype(jnp.float32)
    last = list(range(1 + len(rest) // 2))
    keep_last, away = projection([(depth, last, last)], corner, *rest[1::2])
    other_last = send(away, "exp", heads, 1).astype(jnp.float32)
    left = keep[:, :width] + other[:, :width]
    right = keep[:, width:] + other[:, width:] + keep_last + other_last
    result = jnp.concatenate([left, right], 1).astype(jnp.bfloat16)
    result = result.reshape(count // 2, part, 2 * width)

    shifts = list(range(2, count, 2))
    if len(shifts) > 1:
        shifts = [shifts[1], shifts[0]] + shifts[2:]
    final = jnp.zeros((part, count * width), jnp.bfloat16)
    for s in [0] + shifts:
        block = send(result[s // 2], "ctx", count, s) if s else result[0]
        for side in range(2):
            final = lax.dynamic_update_slice(
                final, block[:, side * width : (side + 1) * width], (0, (ctx ^ (s + side)) * width)
            )
    return final


def solution(mesh):
    in_specs = (P("ctx", "exp", None), P("ctx", None), P("exp", None, None), P("exp", "ctx"))
    out_specs = P(("ctx", "exp"), None)
    return jax.shard_map(shards, mesh=mesh, in_specs=in_specs, out_specs=out_specs, check_vma=False)
```

time: 67.9 us -> 61.1 us (0.90)
  waiting for transfers between devices: 27.5 us -> 22 us
  local copies, waits for them, and re-layouts: 8.61 us -> 4.01 us
  starting transfers between devices: 26 us -> 29.1 us
    ppermute x12 -> x13, waiting for transfers between devices: 25.1 us -> 18.8 us  [send(): return lax.ppermute(value, axis, [(i, i ^ shift) for i in range(size)])]
    ppermute x12 -> x13, starting transfers between devices: 15.6 us -> 19 us  [send(): return lax.ppermute(value, axis, [(i, i ^ shift) for i in range(size)])]
    gather x2, local copies, waits for them, and re-layouts: 2.64 us -> 0.73 us  [shards(): rows = jnp.take(queries.reshape(heads, part, own_heads, lat), order, axis=0)]
    unnamed x16 -> x9, local copies, waits for them, and re-layouts: 3.71 us -> 2.13 us
    reshape x1, local copies, waits for them, and re-layouts: 1.15 us -> 0.07 us  [shards(): rows = jnp.take(queries.reshape(heads, part, own_heads, lat), order, axis=0)]
    ppermute x6, waiting for transfers between devices: 2.4 us -> 3.21 us  [route(): return lax.ppermute(value, ('ctx', 'exp'), pairs)]
    pallas_call x1 -> x2, Pallas kernels: 1.27 us -> 1.49 us  [projection(): pl.pallas_call(functools.partial(project, len(values), groups), out_shape...]
  transfers between devices with their start and end apart: 18 -> 19, of which waited for: 8 -> 11; matrix products, arithmetic and copies ran while one was open for 10% -> 5% of each run, Pallas kernels for 5% -> 9%
where the time goes in v4:
time: 61.1 us; the launch traced here: 60.9 us
  starting transfers between devices  29.1 us (48%)
  waiting for transfers between devices  22 us (36%)
  Pallas kernels  5.18 us (8%)
  local copies, waits for them, and re-layouts  4.01 us (7%)
    ppermute x13, starting transfers between devices, send(): return lax.ppermute(value, axis, [(i, i ^ shift) for i in range(size)])  19 us
    ppermute x13, waiting for transfers between devices, send(): return lax.ppermute(value, axis, [(i, i ^ shift) for i in range(size)])  18.8 us
    ppermute x6, starting transfers between devices, route(): return lax.ppermute(value, ('ctx', 'exp'), pairs)  10.1 us
    pallas_call x2, Pallas kernels, attention(): pl.pallas_call(functools.partial(attend, part, low), out_shape=jax.ShapeD...  3.7 us
    ppermute x6, waiting for transfers between devices, route(): return lax.ppermute(value, ('ctx', 'exp'), pairs)  3.21 us
    unnamed x9, local copies, waits for them, and re-layouts  2.13 us
    pallas_call x2, Pallas kernels, projection(): pl.pallas_call(functools.partial(project, len(values), groups), out_shape...  1.49 us
  transfers between devices with their start and end apart: 19, of which 11 were waited for; matrix products, arithmetic and copies ran while one was open for 5% of the time, Pallas kernels for 9%

profile of v4, /device:TPU:0, one launch (start us, length us, event | category | flops | bytes accessed | tf_op | source)
XLA Modules:
  0.0 60.9 jit_solution(11778701158574197998)
XLA Ops:
  0.0 5.0 %collective-permute-start = (bf16[576,128]{1,0:T(8,128)(2,1)}, bf16[576,128]{1,0:T(8,128)(2,1)S(1)}, u32[]{:S(2)}, u32[]{:S(2)}) collective-permute-start(bf16[576,128]{1,0:T(8,128)(2,1)} %bitcast.17), channel_id=1, source_target_pairs={{0,24},{1,29},{2,26},{3,31},{4,28},{5,25},{6,30},{7,27},{8,16},{9,... | collective-permute-start | bytes 442376 | tf_op jit(solution)/shard_map/ppermute | solution.py:28
  5.1 0.6 collective-permute-start.4
  5.6 1.7 %collective-permute-start.6 = (bf16[576,128]{1,0:T(8,128)(2,1)}, bf16[576,128]{1,0:T(8,128)(2,1)S(1)}, u32[]{:S(2)}, u32[]{:S(2)}) collective-permute-start(bf16[576,128]{1,0:T(8,128)(2,1)} %bitcast.20), channel_id=1, source_target_pairs={{0,4},{4,0},{8,12},{12,8},{16,20},{20,16},{24,28},{28,24},{1,5},{5... | collective-permute-start | bytes 442376 | tf_op jit(solution)/shard_map/ppermute | solution.py:19
  7.4 1.5 %collective-permute-start.11 = (bf16[512,896]{1,0:T(8,128)(2,1)}, bf16[512,896]{1,0:T(8,128)(2,1)S(1)}, u32[]{:S(2)}, u32[]{:S(2)}) collective-permute-start(bf16[512,896]{1,0:T(8,128)(2,1)} %refs_4_.1), channel_id=1, source_target_pairs={{0,2},{1,5},{2,0},{3,7},{4,6},{5,1},{6,4},{7,3},{8,10},{9,13},{10,... | collective-permute-start | bytes 2752520 | tf_op jit(solution)/shard_map/ppermute | solution.py:28
  8.8 1.4 %copy.5 = bf16[128,4,576]{2,0,1:T(8,128)(2,1)S(1)} copy(bf16[128,4,576]{0,2,1:T(8,128)(2,1)} %param.4) | data formatting | bytes 1179648 | tf_op args[0]
  10.3 0.7 %gather_fusion = bf16[4,32,4,576]{3,1,2,0:T(8,128)(2,1)S(1)} fusion(bf16[4,32,4,576]{3,1,2,0:T(8,128)(2,1)S(1)} %copy.6, s32[1024]{0:T(1024)S(1)} %pad_clamp_fusion), kind=kCustom, calls=%fused_computation | custom fusion | bytes 1179664 | tf_op jit(solution)/shard_map/jit(_take)/gather | solution.py:124
  11.5 2.5 %collective-permute-done.6.refs_7_ = bf16[576,128]{1,0:T(8,128)(2,1)S(1)} collective-permute-done((bf16[576,128]{1,0:T(8,128)(2,1)}, bf16[576,128]{1,0:T(8,128)(2,1)S(1)}, u32[]{:S(2)}, u32[]{:S(2)}) %collective-permute-start.6) | collective-permute-done | bytes 147488 | tf_op jit(solution)/shard_map/ppermute | solution.py:19
  14.0 2.0 %collective-permute-start.12 = (bf16[512,896]{1,0:T(8,128)(2,1)S(1)}, bf16[512,896]{1,0:T(8,128)(2,1)S(1)}, u32[]{:S(2)}, u32[]{:S(2)}) collective-permute-start(bf16[512,896]{1,0:T(8,128)(2,1)S(1)} %copy-done), channel_id=1, source_target_pairs={{0,4},{1,3},{2,6},{3,1},{4,0},{5,7},{6,2},{7,5},{8,12},{9,11},{10,... | collective-permute-start | bytes 2752520 | tf_op jit(solution)/shard_map/ppermute | solution.py:28
  16.1 2.6 %collective-permute-done.2.refs_3_ = bf16[576,128]{1,0:T(8,128)(2,1)S(1)} collective-permute-done((bf16[576,128]{1,0:T(8,128)(2,1)}, bf16[576,128]{1,0:T(8,128)(2,1)S(1)}, u32[]{:S(2)}, u32[]{:S(2)}) %collective-permute-start.2) | collective-permute-done | bytes 147488 | tf_op jit(solution)/shard_map/ppermute | solution.py:28
  18.7 0.5 collective-permute-start.5
  19.3 0.8 %collective-permute-done.3.refs_4_ = bf16[576,128]{1,0:T(8,128)(2,1)S(1)} collective-permute-done((bf16[576,128]{1,0:T(8,128)(2,1)S(1)}, bf16[576,128]{1,0:T(8,128)(2,1)S(1)}, u32[]{:S(2)}, u32[]{:S(2)}) %collective-permute-start.3) | collective-permute-done | bytes 147488 | tf_op jit(solution)/shard_map/ppermute | solution.py:19
  20.3 1.8 %shard_map.47 = bf16[64,512]{1,0:T(8,128)(2,1)S(1)} custom-call(s32[10]{0:T(128)S(1)} %stack.40.place, bf16[4,64,576]{2,1,0:T(8,128)(2,1)S(1)} %get-tuple-element.20.query, bf16[576,128]{1,0:T(8,128)(2,1)S(1)} %bitcast.21, bf16[576,128]{1,0:T(8,128)(2,1)S(1)} %collective-permute-done.refs_1_, bf16[576,128]{1,0:T(8,128)(2,1)S(1)} %collective-permute-done.1.refs_2_, ...), custom_call_target="tpu_custom_call" | custom-call | flops 570425344 | bytes 2293760 | tf_op jit(solution)/shard_map/pallas_call | solution.py:130
  22.1 1.6 %collective-permute-start.7 = (bf16[64,512]{1,0:T(8,128)(2,1)S(1)}, bf16[64,512]{1,0:T(8,128)(2,1)S(1)}, u32[]{:S(2)}, u32[]{:S(2)}) collective-permute-start(bf16[64,512]{1,0:T(8,128)(2,1)S(1)} %shard_map.47), channel_id=1, source_target_pairs={{0,2},{1,3},{2,0},{3,1},{4,6},{5,7},{6,4},{7,5},{8,10},{9,11},{10,... | collective-permute-start | bytes 196616 | tf_op jit(solution)/shard_map/ppermute | solution.py:19
  23.7 1.9 %shard_map.46 = bf16[64,512]{1,0:T(8,128)(2,1)S(1)} custom-call(s32[10]{0:T(128)S(1)} %stack.40.place, bf16[4,64,576]{2,1,0:T(8,128)(2,1)S(1)} %get-tuple-element.19.query, bf16[576,128]{1,0:T(8,128)(2,1)S(1)} %bitcast.22, bf16[576,128]{1,0:T(8,128)(2,1)S(1)} %collective-permute-done.refs_1_, bf16[576,128]{1,0:T(8,128)(2,1)S(1)} %collective-permute-done.1.refs_2_, ...), custom_call_target="tpu_custom_call" | custom-call | flops 570425344 | bytes 2293760 | tf_op jit(solution)/shard_map/pallas_call | solution.py:130
  25.6 1.7 %collective-permute-done.7 = bf16[64,512]{1,0:T(8,128)(2,1)S(1)} collective-permute-done((bf16[64,512]{1,0:T(8,128)(2,1)S(1)}, bf16[64,512]{1,0:T(8,128)(2,1)S(1)}, u32[]{:S(2)}, u32[]{:S(2)}) %collective-permute-start.7) | collective-permute-done | bytes 65568 | tf_op jit(solution)/shard_map/ppermute | solution.py:19
  27.2 0.9 %collective-permute-start.14 = (bf16[512,896]{1,0:T(8,128)(2,1)S(1)}, bf16[512,896]{1,0:T(8,128)(2,1)S(1)}, u32[]{:S(2)}, u32[]{:S(2)}) collective-permute-start(bf16[512,896]{1,0:T(8,128)(2,1)S(1)} %collective-permute-done.11.refs_5_), channel_id=1, source_target_pairs={{0,4},{1,3},{2,6},{3,1},{4,0},{5,7},{6,2},{7,5},{8,12},{9,11},{10,... | collective-permute-start | bytes 2752520 | tf_op jit(solution)/shard_map/ppermute | solution.py:28
  28.2 2.5 %collective-permute-start.10 = (bf16[64,1024]{1,0:T(8,128)(2,1)S(1)}, bf16[64,1024]{1,0:T(8,128)(2,1)S(1)}, u32[]{:S(2)}, u32[]{:S(2)}) collective-permute-start(bf16[64,1024]{1,0:T(8,128)(2,1)S(1)} %pad_maximum_fusion.refs_0_), channel_id=1, source_target_pairs={{0,24},{4,28},{8,16},{12,20},{16,8},{20,12},{24,0},{28,4},{1,25},{... | collective-permute-start | bytes 393224 | tf_op jit(solution)/shard_map/ppermute | solution.py:19
  30.7 1.9 %collective-permute-start.9 = (bf16[64,1024]{1,0:T(8,128)(2,1)S(1)}, bf16[64,1024]{1,0:T(8,128)(2,1)S(1)}, u32[]{:S(2)}, u32[]{:S(2)}) collective-permute-start(bf16[64,1024]{1,0:T(8,128)(2,1)S(1)} %pad_maximum_fusion.refs_0_), channel_id=1, source_target_pairs={{0,16},{4,20},{8,24},{12,28},{16,0},{20,4},{24,8},{28,12},{1,17},{... | collective-permute-start | bytes 393224 | tf_op jit(solution)/shard_map/ppermute | solution.py:19
  32.6 2.5 %collective-permute-done.10.refs_3_ = bf16[64,1024]{1,0:T(8,128)(2,1)S(1)} collective-permute-done((bf16[64,1024]{1,0:T(8,128)(2,1)S(1)}, bf16[64,1024]{1,0:T(8,128)(2,1)S(1)}, u32[]{:S(2)}, u32[]{:S(2)}) %collective-permute-start.10) | collective-permute-done | bytes 131104 | tf_op jit(solution)/shard_map/ppermute | solution.py:19
  35.1 2.7 %collective-permute-done.8.refs_1_ = bf16[64,1024]{1,0:T(8,128)(2,1)S(1)} collective-permute-done((bf16[64,1024]{1,0:T(8,128)(2,1)S(1)}, bf16[64,1024]{1,0:T(8,128)(2,1)S(1)}, u32[]{:S(2)}, u32[]{:S(2)}) %collective-permute-start.8) | collective-permute-done | bytes 131104 | tf_op jit(solution)/shard_map/ppermute | solution.py:19
  37.8 1.0 %shard_map.48 = (f32[128,1792]{1,0:T(8,128)S(1)}, bf16[128,1792]{1,0:T(8,128)(2,1)S(1)}) custom-call(s32[1]{0:T(128)} %bitcast.place, bf16[64,1024]{1,0:T(8,128)(2,1)S(1)} %pad_maximum_fusion.refs_0_, bf16[64,1024]{1,0:T(8,128)(2,1)S(1)} %collective-permute-done.8.refs_1_, bf16[64,1024]{1,0:T(8,128)(2,1)S(1)} %collective-permute-done.9.refs_2_, ...), custom_call_target="tpu_custom_call" | custom-call | flops 704643072 | bytes 4653056 | tf_op jit(solution)/shard_map/pallas_call | solution.py:161
  38.8 5.7 %collective-permute-start.13 = (bf16[128,1792]{1,0:T(8,128)(2,1)S(1)}, bf16[128,1792]{1,0:T(8,128)(2,1)S(1)}, u32[]{:S(2)}, u32[]{:S(2)}) collective-permute-start(bf16[128,1792]{1,0:T(8,128)(2,1)S(1)} %get-tuple-element.13), channel_id=1, source_target_pairs={{0,1},{1,0},{2,3},{3,2},{4,5},{5,4},{6,7},{7,6},{8,9},{9,8},{10,11... | collective-permute-start | bytes 1376264 | tf_op jit(solution)/shard_map/ppermute | solution.py:19
  44.6 0.6 collective-permute-done.14.refs_4_
  45.1 0.5 shard_map.49
  45.6 0.6 collective-permute-start.15
  46.2 1.0 %collective-permute-done.15 = bf16[128,896]{1,0:T(8,128)(2,1)S(1)} collective-permute-done((bf16[128,896]{1,0:T(8,128)(2,1)S(1)}, bf16[128,896]{1,0:T(8,128)(2,1)S(1)}, u32[]{:S(2)}, u32[]{:S(2)}) %collective-permute-start.15) | collective-permute-done | bytes 229408 | tf_op jit(solution)/shard_map/ppermute | solution.py:19
  47.5 1.8 %collective-permute-start.16 = (bf16[32,1792]{1,0:T(8,128)(2,1)S(1)}, bf16[32,1792]{1,0:T(8,128)(2,1)S(1)}, u32[]{:S(2)}, u32[]{:S(2)}) collective-permute-start(bf16[32,1792]{1,0:T(8,128)(2,1)S(1)} %get-tuple-element.23), channel_id=1, source_target_pairs={{0,16},{4,20},{8,24},{12,28},{16,0},{20,4},{24,8},{28,12},{1,17},{... | collective-permute-start | bytes 344072 | tf_op jit(solution)/shard_map/ppermute | solution.py:19
  49.3 2.2 %collective-permute-start.17 = (bf16[32,1792]{1,0:T(8,128)(2,1)S(1)}, bf16[32,1792]{1,0:T(8,128)(2,1)S(1)}, u32[]{:S(2)}, u32[]{:S(2)}) collective-permute-start(bf16[32,1792]{1,0:T(8,128)(2,1)S(1)} %get-tuple-element.22), channel_id=1, source_target_pairs={{0,8},{4,12},{8,0},{12,4},{16,24},{20,28},{24,16},{28,20},{1,9},{5... | collective-permute-start | bytes 344072 | tf_op jit(solution)/shard_map/ppermute | solution.py:19
  52.0 5.3 %collective-permute-done.16 = bf16[32,1792]{1,0:T(8,128)(2,1)S(1)} collective-permute-done((bf16[32,1792]{1,0:T(8,128)(2,1)S(1)}, bf16[32,1792]{1,0:T(8,128)(2,1)S(1)}, u32[]{:S(2)}, u32[]{:S(2)}) %collective-permute-start.16) | collective-permute-done | bytes 114720 | tf_op jit(solution)/shard_map/ppermute | solution.py:19
  57.4 2.1 %collective-permute-done.18 = bf16[32,1792]{1,0:T(8,128)(2,1)S(1)} collective-permute-done((bf16[32,1792]{1,0:T(8,128)(2,1)S(1)}, bf16[32,1792]{1,0:T(8,128)(2,1)S(1)}, u32[]{:S(2)}, u32[]{:S(2)}) %collective-permute-start.18) | collective-permute-done | bytes 114720 | tf_op jit(solution)/shard_map/ppermute | solution.py:19
  59.5 0.8 %copy-done.3 = bf16[32,7168]{1,0:T(8,128)(2,1)} copy-done((bf16[32,7168]{1,0:T(8,128)(2,1)}, bf16[32,7168]{1,0:T(8,128)(2,1)S(1)}, u32[]{:S(2)}) %copy-start.3) | copy-done | bytes 458776
  60.3 0.6 %slice_dynamic-update-slice_fusion = bf16[32,7168]{1,0:T(8,128)(2,1)} fusion(bf16[32,7168]{1,0:T(8,128)(2,1)} %copy-done.3, s32[]{:T(128)S(6)} %select_n.88, bf16[32,1792]{1,0:T(8,128)(2,1)S(1)} %collective-permute-done.18), kind=kLoop, calls=%fused_computation.12 | loop fusion | bytes 114692 | tf_op jit(solution)/shard_map/dynamic_update_slice | solution.py:197
  (43 shorter events, 1.7 us)
Async XLA Ops:
  0.0 16.1 %collective-permute-start = (bf16[576,128]{1,0:T(8,128)(2,1)}, bf16[576,128]{1,0:T(8,128)(2,1)S(1)}, u32[]{:S(2)}, u32[]{:S(2)}) collective-permute-start(bf16[576,128]{1,0:T(8,128)(2,1)} %bitcast.17), channel_id=1, source_target_pairs={{0,24},{1,29},{2,26},{3,31},{4,28},{5,25},{6,30},{7,27},{8,16},{9,... | collective-permute-start | bytes 442376 | tf_op jit(solution)/shard_map/ppermute | solution.py:28
  5.0 13.6 %collective-permute-start.2 = (bf16[576,128]{1,0:T(8,128)(2,1)}, bf16[576,128]{1,0:T(8,128)(2,1)S(1)}, u32[]{:S(2)}, u32[]{:S(2)}) collective-permute-start(bf16[576,128]{1,0:T(8,128)(2,1)} %bitcast.18), channel_id=1, source_target_pairs={{0,16},{1,21},{2,18},{3,23},{4,20},{5,17},{6,22},{7,19},{8,24},{9,... | collective-permute-start | bytes 442376 | tf_op jit(solution)/shard_map/ppermute | solution.py:28
  5.1 13.6 %collective-permute-start.4 = (bf16[576,128]{1,0:T(8,128)(2,1)}, bf16[576,128]{1,0:T(8,128)(2,1)S(1)}, u32[]{:S(2)}, u32[]{:S(2)}) collective-permute-start(bf16[576,128]{1,0:T(8,128)(2,1)} %bitcast.19), channel_id=1, source_target_pairs={{0,8},{1,13},{2,10},{3,15},{4,12},{5,9},{6,14},{7,11},{8,0},{9,5},... | collective-permute-start | bytes 442376 | tf_op jit(solution)/shard_map/ppermute | solution.py:28
  5.6 8.4 %collective-permute-start.6 = (bf16[576,128]{1,0:T(8,128)(2,1)}, bf16[576,128]{1,0:T(8,128)(2,1)S(1)}, u32[]{:S(2)}, u32[]{:S(2)}) collective-permute-start(bf16[576,128]{1,0:T(8,128)(2,1)} %bitcast.20), channel_id=1, source_target_pairs={{0,4},{4,0},{8,12},{12,8},{16,20},{20,16},{24,28},{28,24},{1,5},{5... | collective-permute-start | bytes 442376 | tf_op jit(solution)/shard_map/ppermute | solution.py:19
  7.4 19.9 %collective-permute-start.11 = (bf16[512,896]{1,0:T(8,128)(2,1)}, bf16[512,896]{1,0:T(8,128)(2,1)S(1)}, u32[]{:S(2)}, u32[]{:S(2)}) collective-permute-start(bf16[512,896]{1,0:T(8,128)(2,1)} %refs_4_.1), channel_id=1, source_target_pairs={{0,2},{1,5},{2,0},{3,7},{4,6},{5,1},{6,4},{7,3},{8,10},{9,13},{10,... | collective-permute-start | bytes 2752520 | tf_op jit(solution)/shard_map/ppermute | solution.py:28
  11.1 3.0 %copy-start = (bf16[512,896]{1,0:T(8,128)(2,1)S(1)}, bf16[512,896]{1,0:T(8,128)(2,1)}, u32[]{:S(2)}) copy-start(bf16[512,896]{1,0:T(8,128)(2,1)} %refs_4_.1) | copy-start | bytes 2752516
  14.0 23.8 %collective-permute-start.12 = (bf16[512,896]{1,0:T(8,128)(2,1)S(1)}, bf16[512,896]{1,0:T(8,128)(2,1)S(1)}, u32[]{:S(2)}, u32[]{:S(2)}) collective-permute-start(bf16[512,896]{1,0:T(8,128)(2,1)S(1)} %copy-done), channel_id=1, source_target_pairs={{0,4},{1,3},{2,6},{3,1},{4,0},{5,7},{6,2},{7,5},{8,12},{9,11},{10,... | collective-permute-start | bytes 2752520 | tf_op jit(solution)/shard_map/ppermute | solution.py:28
  16.1 3.2 %collective-permute-start.1 = (bf16[576,128]{1,0:T(8,128)(2,1)S(1)}, bf16[576,128]{1,0:T(8,128)(2,1)S(1)}, u32[]{:S(2)}, u32[]{:S(2)}) collective-permute-start(bf16[576,128]{1,0:T(8,128)(2,1)S(1)} %collective-permute-done.refs_1_), channel_id=1, source_target_pairs={{0,1},{1,0},{2,3},{3,2},{4,5},{5,4},{6,7},{7,6},{8,9},{9,8},{10,11... | collective-permute-start | bytes 442376 | tf_op jit(solution)/shard_map/ppermute | solution.py:19
  18.7 1.4 %collective-permute-start.3 = (bf16[576,128]{1,0:T(8,128)(2,1)S(1)}, bf16[576,128]{1,0:T(8,128)(2,1)S(1)}, u32[]{:S(2)}, u32[]{:S(2)}) collective-permute-start(bf16[576,128]{1,0:T(8,128)(2,1)S(1)} %collective-permute-done.2.refs_3_), channel_id=1, source_target_pairs={{0,1},{1,0},{2,3},{3,2},{4,5},{5,4},{6,7},{7,6},{8,9},{9,8},{10,11... | collective-permute-start | bytes 442376 | tf_op jit(solution)/shard_map/ppermute | solution.py:19
  18.7 1.6 %collective-permute-start.5 = (bf16[576,128]{1,0:T(8,128)(2,1)S(1)}, bf16[576,128]{1,0:T(8,128)(2,1)S(1)}, u32[]{:S(2)}, u32[]{:S(2)}) collective-permute-start(bf16[576,128]{1,0:T(8,128)(2,1)S(1)} %collective-permute-done.4.refs_5_), channel_id=1, source_target_pairs={{0,1},{1,0},{2,3},{3,2},{4,5},{5,4},{6,7},{7,6},{8,9},{9,8},{10,11... | collective-permute-start | bytes 442376 | tf_op jit(solution)/shard_map/ppermute | solution.py:19
  19.2 1.1 %copy-start.1 = (bf16[4,512,128]{2,1,0:T(8,128)(2,1)S(1)}, bf16[4,512,128]{2,1,0:T(8,128)(2,1)}, u32[]{:S(2)}) copy-start(bf16[4,512,128]{2,1,0:T(8,128)(2,1)} %refs_8_.3) | copy-start | bytes 1572868
  19.2 1.1 %copy-start.2 = (bf16[128,576]{0,1:T(8,128)(2,1)S(1)}, bf16[128,576]{0,1:T(8,128)(2,1)}, u32[]{:S(2)}) copy-start(bf16[128,576]{0,1:T(8,128)(2,1)} %param.5) | copy-start | bytes 442372
  22.1 5.1 %collective-permute-start.7 = (bf16[64,512]{1,0:T(8,128)(2,1)S(1)}, bf16[64,512]{1,0:T(8,128)(2,1)S(1)}, u32[]{:S(2)}, u32[]{:S(2)}) collective-permute-start(bf16[64,512]{1,0:T(8,128)(2,1)S(1)} %shard_map.47), channel_id=1, source_target_pairs={{0,2},{1,3},{2,0},{3,1},{4,6},{5,7},{6,4},{7,5},{8,10},{9,11},{10,... | collective-permute-start | bytes 196616 | tf_op jit(solution)/shard_map/ppermute | solution.py:19
  27.2 17.9 %collective-permute-start.14 = (bf16[512,896]{1,0:T(8,128)(2,1)S(1)}, bf16[512,896]{1,0:T(8,128)(2,1)S(1)}, u32[]{:S(2)}, u32[]{:S(2)}) collective-permute-start(bf16[512,896]{1,0:T(8,128)(2,1)S(1)} %collective-permute-done.11.refs_5_), channel_id=1, source_target_pairs={{0,4},{1,3},{2,6},{3,1},{4,0},{5,7},{6,2},{7,5},{8,12},{9,11},{10,... | collective-permute-start | bytes 2752520 | tf_op jit(solution)/shard_map/ppermute | solution.py:28
  28.2 6.9 %collective-permute-start.10 = (bf16[64,1024]{1,0:T(8,128)(2,1)S(1)}, bf16[64,1024]{1,0:T(8,128)(2,1)S(1)}, u32[]{:S(2)}, u32[]{:S(2)}) collective-permute-start(bf16[64,1024]{1,0:T(8,128)(2,1)S(1)} %pad_maximum_fusion.refs_0_), channel_id=1, source_target_pairs={{0,24},{4,28},{8,16},{12,20},{16,8},{20,12},{24,0},{28,4},{1,25},{... | collective-permute-start | bytes 393224 | tf_op jit(solution)/shard_map/ppermute | solution.py:19
  30.7 7.1 %collective-permute-start.8 = (bf16[64,1024]{1,0:T(8,128)(2,1)S(1)}, bf16[64,1024]{1,0:T(8,128)(2,1)S(1)}, u32[]{:S(2)}, u32[]{:S(2)}) collective-permute-start(bf16[64,1024]{1,0:T(8,128)(2,1)S(1)} %pad_maximum_fusion.refs_0_), channel_id=1, source_target_pairs={{0,8},{4,12},{8,0},{12,4},{16,24},{20,28},{24,16},{28,20},{1,9},{5... | collective-permute-start | bytes 393224 | tf_op jit(solution)/shard_map/ppermute | solution.py:19
  30.7 7.1 %collective-permute-start.9 = (bf16[64,1024]{1,0:T(8,128)(2,1)S(1)}, bf16[64,1024]{1,0:T(8,128)(2,1)S(1)}, u32[]{:S(2)}, u32[]{:S(2)}) collective-permute-start(bf16[64,1024]{1,0:T(8,128)(2,1)S(1)} %pad_maximum_fusion.refs_0_), channel_id=1, source_target_pairs={{0,16},{4,20},{8,24},{12,28},{16,0},{20,4},{24,8},{28,12},{1,17},{... | collective-permute-start | bytes 393224 | tf_op jit(solution)/shard_map/ppermute | solution.py:19
  38.8 7.3 %collective-permute-start.13 = (bf16[128,1792]{1,0:T(8,128)(2,1)S(1)}, bf16[128,1792]{1,0:T(8,128)(2,1)S(1)}, u32[]{:S(2)}, u32[]{:S(2)}) collective-permute-start(bf16[128,1792]{1,0:T(8,128)(2,1)S(1)} %get-tuple-element.13), channel_id=1, source_target_pairs={{0,1},{1,0},{2,3},{3,2},{4,5},{5,4},{6,7},{7,6},{8,9},{9,8},{10,11... | collective-permute-start | bytes 1376264 | tf_op jit(solution)/shard_map/ppermute | solution.py:19
  45.6 1.7 %collective-permute-start.15 = (bf16[128,896]{1,0:T(8,128)(2,1)S(1)}, bf16[128,896]{1,0:T(8,128)(2,1)S(1)}, u32[]{:S(2)}, u32[]{:S(2)}) collective-permute-start(bf16[128,896]{1,0:T(8,128)(2,1)S(1)} %get-tuple-element.16), channel_id=1, source_target_pairs={{0,1},{1,0},{2,3},{3,2},{4,5},{5,4},{6,7},{7,6},{8,9},{9,8},{10,11... | collective-permute-start | bytes 688136 | tf_op jit(solution)/shard_map/ppermute | solution.py:19
  47.5 9.8 %collective-permute-start.16 = (bf16[32,1792]{1,0:T(8,128)(2,1)S(1)}, bf16[32,1792]{1,0:T(8,128)(2,1)S(1)}, u32[]{:S(2)}, u32[]{:S(2)}) collective-permute-start(bf16[32,1792]{1,0:T(8,128)(2,1)S(1)} %get-tuple-element.23), channel_id=1, source_target_pairs={{0,16},{4,20},{8,24},{12,28},{16,0},{20,4},{24,8},{28,12},{1,17},{... | collective-permute-start | bytes 344072 | tf_op jit(solution)/shard_map/ppermute | solution.py:19
  49.3 8.0 %collective-permute-start.17 = (bf16[32,1792]{1,0:T(8,128)(2,1)S(1)}, bf16[32,1792]{1,0:T(8,128)(2,1)S(1)}, u32[]{:S(2)}, u32[]{:S(2)}) collective-permute-start(bf16[32,1792]{1,0:T(8,128)(2,1)S(1)} %get-tuple-element.22), channel_id=1, source_target_pairs={{0,8},{4,12},{8,0},{12,4},{16,24},{20,28},{24,16},{28,20},{1,9},{5... | collective-permute-start | bytes 344072 | tf_op jit(solution)/shard_map/ppermute | solution.py:19
  51.5 7.9 %collective-permute-start.18 = (bf16[32,1792]{1,0:T(8,128)(2,1)S(1)}, bf16[32,1792]{1,0:T(8,128)(2,1)S(1)}, u32[]{:S(2)}, u32[]{:S(2)}) collective-permute-start(bf16[32,1792]{1,0:T(8,128)(2,1)S(1)} %get-tuple-element.21), channel_id=1, source_target_pairs={{0,24},{4,28},{8,16},{12,20},{16,8},{20,12},{24,0},{28,4},{1,25},{... | collective-permute-start | bytes 344072 | tf_op jit(solution)/shard_map/ppermute | solution.py:19
  59.5 0.8 %copy-start.3 = (bf16[32,7168]{1,0:T(8,128)(2,1)}, bf16[32,7168]{1,0:T(8,128)(2,1)S(1)}, u32[]{:S(2)}) copy-start(bf16[32,7168]{1,0:T(8,128)(2,1)S(1)} %slice_dynamic-update-slice_fusion.1) | copy-start | bytes 1376260

commit v5 on v4

--- a/solution.py
+++ b/solution.py
@@ -182,8 +182,9 @@
     last = list(range(1 + len(rest) // 2))
     keep_last, away = projection([(depth, last, last)], corner, *rest[1::2])
     other_last = send(away, "exp", heads, 1).astype(jnp.float32)
-    left = keep[:, :width] + other[:, :width]
-    right = keep[:, width:] + other[:, width:] + keep_last + other_last
+    here = keep[:, :width] + other[:, :width]
+    beside = keep[:, width:] + other[:, width:] + keep_last + other_last
+    left, right = jnp.where(ctx % 2 == 0, here, beside), jnp.where(ctx % 2 == 0, beside, here)
     result = jnp.concatenate([left, right], 1).astype(jnp.bfloat16)
     result = result.reshape(count // 2, part, 2 * width)
 
@@ -193,10 +194,7 @@
     final = jnp.zeros((part, count * width), jnp.bfloat16)
     for s in [0] + shifts:
         block = send(result[s // 2], "ctx", count, s) if s else result[0]
-        for side in range(2):
-            final = lax.dynamic_update_slice(
-                final, block[:, side * width : (side + 1) * width], (0, (ctx ^ (s + side)) * width)
-            )
+        final = lax.dynamic_update_slice(final, block, (0, (ctx ^ s) // 2 * 2 * width))
     return final
 
 

time: 61.1 us -> 60.5 us (level)
  starting transfers between devices: 29.1 us -> 27.9 us
  local copies, waits for them, and re-layouts: 4.01 us -> 5.19 us
  waiting for transfers between devices: 22 us -> 21.3 us
    gather x2, local copies, waits for them, and re-layouts: 0.73 us -> 2.63 us  [shards(): rows = jnp.take(queries.reshape(heads, part, own_heads, lat), order, axis=0)]
    ppermute x13, waiting for transfers between devices: 18.8 us -> 17.5 us  [send(): return lax.ppermute(value, axis, [(i, i ^ shift) for i in range(size)])]
    ppermute x13, starting transfers between devices: 19 us -> 18 us  [send(): return lax.ppermute(value, axis, [(i, i ^ shift) for i in range(size)])]
    unnamed x9, local copies, waits for them, and re-layouts: 2.13 us -> 1.48 us
  transfers between devices with their start and end apart: 19 -> 19, of which waited for: 11 -> 12; matrix products, arithmetic and copies ran while one was open for 5% -> 8% of each run, Pallas kernels for 9% -> 9%
where the time goes in v5:
time: 60.5 us; the launch traced here: 60.2 us
  starting transfers between devices  27.9 us (46%)
  waiting for transfers between devices  21.3 us (35%)
  local copies, waits for them, and re-layouts  5.19 us (9%)
  Pallas kernels  5.16 us (9%)
    ppermute x13, starting transfers between devices, send(): return lax.ppermute(value, axis, [(i, i ^ shift) for i in range(size)])  18 us
    ppermute x13, waiting for transfers between devices, send(): return lax.ppermute(value, axis, [(i, i ^ shift) for i in range(size)])  17.5 us
    ppermute x6, starting transfers between devices, route(): return lax.ppermute(value, ('ctx', 'exp'), pairs)  9.95 us
    ppermute x6, waiting for transfers between devices, route(): return lax.ppermute(value, ('ctx', 'exp'), pairs)  3.74 us
    pallas_call x2, Pallas kernels, attention(): pl.pallas_call(functools.partial(attend, part, low), out_shape=jax.ShapeD...  3.68 us
    gather x2, local copies, waits for them, and re-layouts, shards(): rows = jnp.take(queries.reshape(heads, part, own_heads, lat), order, axis=0)  2.63 us
    pallas_call x2, Pallas kernels, projection(): pl.pallas_call(functools.partial(project, len(values), groups), out_shape...  1.49 us
    unnamed x9, local copies, waits for them, and re-layouts  1.48 us
  transfers between devices with their start and end apart: 19, of which 12 were waited for; matrix products, arithmetic and copies ran while one was open for 8% of the time, Pallas kernels for 9%

profile of v5, /device:TPU:0, one launch (start us, length us, event | category | flops | bytes accessed | tf_op | source)
XLA Modules:
  0.0 60.2 jit_solution(13271446915548551593)
XLA Ops:
  0.0 5.0 %collective-permute-start = (bf16[576,128]{1,0:T(8,128)(2,1)}, bf16[576,128]{1,0:T(8,128)(2,1)S(1)}, u32[]{:S(2)}, u32[]{:S(2)}) collective-permute-start(bf16[576,128]{1,0:T(8,128)(2,1)} %bitcast.17), channel_id=1, source_target_pairs={{0,24},{1,29},{2,26},{3,31},{4,28},{5,25},{6,30},{7,27},{8,16},{9,... | collective-permute-start | bytes 442376 | tf_op jit(solution)/shard_map/ppermute | solution.py:28
  5.1 0.6 collective-permute-start.4
  5.6 1.7 %collective-permute-start.6 = (bf16[576,128]{1,0:T(8,128)(2,1)}, bf16[576,128]{1,0:T(8,128)(2,1)S(1)}, u32[]{:S(2)}, u32[]{:S(2)}) collective-permute-start(bf16[576,128]{1,0:T(8,128)(2,1)} %bitcast.20), channel_id=1, source_target_pairs={{0,4},{4,0},{8,12},{12,8},{16,20},{20,16},{24,28},{28,24},{1,5},{5... | collective-permute-start | bytes 442376 | tf_op jit(solution)/shard_map/ppermute | solution.py:19
  7.4 1.5 %collective-permute-start.11 = (bf16[512,896]{1,0:T(8,128)(2,1)}, bf16[512,896]{1,0:T(8,128)(2,1)S(1)}, u32[]{:S(2)}, u32[]{:S(2)}) collective-permute-start(bf16[512,896]{1,0:T(8,128)(2,1)} %refs_4_.1), channel_id=1, source_target_pairs={{0,2},{1,5},{2,0},{3,7},{4,6},{5,1},{6,4},{7,3},{8,10},{9,13},{10,... | collective-permute-start | bytes 2752520 | tf_op jit(solution)/shard_map/ppermute | solution.py:28
  8.8 1.4 %copy.5 = bf16[128,4,576]{2,0,1:T(8,128)(2,1)S(1)} copy(bf16[128,4,576]{0,2,1:T(8,128)(2,1)} %param.4) | data formatting | bytes 1179648 | tf_op args[0]
  10.3 1.5 %gather_fusion = bf16[4,32,4,576]{3,1,2,0:T(8,128)(2,1)} fusion(bf16[4,32,4,576]{3,1,2,0:T(8,128)(2,1)S(1)} %copy.6, s32[1024]{0:T(1024)S(1)} %pad_clamp_fusion), kind=kCustom, calls=%fused_computation | custom fusion | bytes 1179664 | tf_op jit(solution)/shard_map/jit(_take)/gather | solution.py:124
  11.8 1.2 %copy.7 = bf16[4,32,4,576]{3,1,0,2:T(8,128)(2,1)S(1)} copy(bf16[4,32,4,576]{3,1,2,0:T(8,128)(2,1)} %gather_fusion) | data formatting | bytes 1179648 | tf_op jit(solution)/shard_map/jit(_take)/gather | solution.py:124
  13.4 0.6 %collective-permute-done.6.refs_7_ = bf16[576,128]{1,0:T(8,128)(2,1)S(1)} collective-permute-done((bf16[576,128]{1,0:T(8,128)(2,1)}, bf16[576,128]{1,0:T(8,128)(2,1)S(1)}, u32[]{:S(2)}, u32[]{:S(2)}) %collective-permute-start.6) | collective-permute-done | bytes 147488 | tf_op jit(solution)/shard_map/ppermute | solution.py:19
  14.1 1.9 %collective-permute-start.12 = (bf16[512,896]{1,0:T(8,128)(2,1)S(1)}, bf16[512,896]{1,0:T(8,128)(2,1)S(1)}, u32[]{:S(2)}, u32[]{:S(2)}) collective-permute-start(bf16[512,896]{1,0:T(8,128)(2,1)S(1)} %copy-done), channel_id=1, source_target_pairs={{0,4},{1,3},{2,6},{3,1},{4,0},{5,7},{6,2},{7,5},{8,12},{9,11},{10,... | collective-permute-start | bytes 2752520 | tf_op jit(solution)/shard_map/ppermute | solution.py:28
  16.1 2.6 %collective-permute-done.2.refs_3_ = bf16[576,128]{1,0:T(8,128)(2,1)S(1)} collective-permute-done((bf16[576,128]{1,0:T(8,128)(2,1)}, bf16[576,128]{1,0:T(8,128)(2,1)S(1)}, u32[]{:S(2)}, u32[]{:S(2)}) %collective-permute-start.2) | collective-permute-done | bytes 147488 | tf_op jit(solution)/shard_map/ppermute | solution.py:28
  18.7 0.5 collective-permute-start.5
  19.3 0.8 %collective-permute-done.3.refs_4_ = bf16[576,128]{1,0:T(8,128)(2,1)S(1)} collective-permute-done((bf16[576,128]{1,0:T(8,128)(2,1)S(1)}, bf16[576,128]{1,0:T(8,128)(2,1)S(1)}, u32[]{:S(2)}, u32[]{:S(2)}) %collective-permute-start.3) | collective-permute-done | bytes 147488 | tf_op jit(solution)/shard_map/ppermute | solution.py:19
  20.3 1.8 %shard_map.47 = bf16[64,512]{1,0:T(8,128)(2,1)S(1)} custom-call(s32[10]{0:T(128)S(1)} %stack.40.place, bf16[4,64,576]{2,1,0:T(8,128)(2,1)S(1)} %get-tuple-element.20.query, bf16[576,128]{1,0:T(8,128)(2,1)S(1)} %bitcast.21, bf16[576,128]{1,0:T(8,128)(2,1)S(1)} %collective-permute-done.refs_1_, bf16[576,128]{1,0:T(8,128)(2,1)S(1)} %collective-permute-done.1.refs_2_, ...), custom_call_target="tpu_custom_call" | custom-call | flops 570425344 | bytes 2293760 | tf_op jit(solution)/shard_map/pallas_call | solution.py:130
  22.1 1.6 %collective-permute-start.7 = (bf16[64,512]{1,0:T(8,128)(2,1)S(1)}, bf16[64,512]{1,0:T(8,128)(2,1)S(1)}, u32[]{:S(2)}, u32[]{:S(2)}) collective-permute-start(bf16[64,512]{1,0:T(8,128)(2,1)S(1)} %shard_map.47), channel_id=1, source_target_pairs={{0,2},{1,3},{2,0},{3,1},{4,6},{5,7},{6,4},{7,5},{8,10},{9,11},{10,... | collective-permute-start | bytes 196616 | tf_op jit(solution)/shard_map/ppermute | solution.py:19
  23.7 1.8 %shard_map.46 = bf16[64,512]{1,0:T(8,128)(2,1)S(1)} custom-call(s32[10]{0:T(128)S(1)} %stack.40.place, bf16[4,64,576]{2,1,0:T(8,128)(2,1)S(1)} %get-tuple-element.19.query, bf16[576,128]{1,0:T(8,128)(2,1)S(1)} %bitcast.22, bf16[576,128]{1,0:T(8,128)(2,1)S(1)} %collective-permute-done.refs_1_, bf16[576,128]{1,0:T(8,128)(2,1)S(1)} %collective-permute-done.1.refs_2_, ...), custom_call_target="tpu_custom_call" | custom-call | flops 570425344 | bytes 2293760 | tf_op jit(solution)/shard_map/pallas_call | solution.py:130
  25.5 1.7 %collective-permute-done.7 = bf16[64,512]{1,0:T(8,128)(2,1)S(1)} collective-permute-done((bf16[64,512]{1,0:T(8,128)(2,1)S(1)}, bf16[64,512]{1,0:T(8,128)(2,1)S(1)}, u32[]{:S(2)}, u32[]{:S(2)}) %collective-permute-start.7) | collective-permute-done | bytes 65568 | tf_op jit(solution)/shard_map/ppermute | solution.py:19
  27.2 0.9 %collective-permute-start.14 = (bf16[512,896]{1,0:T(8,128)(2,1)S(1)}, bf16[512,896]{1,0:T(8,128)(2,1)S(1)}, u32[]{:S(2)}, u32[]{:S(2)}) collective-permute-start(bf16[512,896]{1,0:T(8,128)(2,1)S(1)} %collective-permute-done.11.refs_5_), channel_id=1, source_target_pairs={{0,4},{1,3},{2,6},{3,1},{4,0},{5,7},{6,2},{7,5},{8,12},{9,11},{10,... | collective-permute-start | bytes 2752520 | tf_op jit(solution)/shard_map/ppermute | solution.py:28
  28.6 2.6 %collective-permute-start.9 = (bf16[64,1024]{1,0:T(8,128)(2,1)S(1)}, bf16[64,1024]{1,0:T(8,128)(2,1)S(1)}, u32[]{:S(2)}, u32[]{:S(2)}) collective-permute-start(bf16[64,1024]{1,0:T(8,128)(2,1)S(1)} %pad_maximum_fusion.refs_0_), channel_id=1, source_target_pairs={{0,16},{4,20},{8,24},{12,28},{16,0},{20,4},{24,8},{28,12},{1,17},{... | collective-permute-start | bytes 393224 | tf_op jit(solution)/shard_map/ppermute | solution.py:19
  31.2 1.4 %collective-permute-start.10 = (bf16[64,1024]{1,0:T(8,128)(2,1)S(1)}, bf16[64,1024]{1,0:T(8,128)(2,1)S(1)}, u32[]{:S(2)}, u32[]{:S(2)}) collective-permute-start(bf16[64,1024]{1,0:T(8,128)(2,1)S(1)} %pad_maximum_fusion.refs_0_), channel_id=1, source_target_pairs={{0,24},{4,28},{8,16},{12,20},{16,8},{20,12},{24,0},{28,4},{1,25},{... | collective-permute-start | bytes 393224 | tf_op jit(solution)/shard_map/ppermute | solution.py:19
  32.6 1.7 %collective-permute-done.8.refs_1_ = bf16[64,1024]{1,0:T(8,128)(2,1)S(1)} collective-permute-done((bf16[64,1024]{1,0:T(8,128)(2,1)S(1)}, bf16[64,1024]{1,0:T(8,128)(2,1)S(1)}, u32[]{:S(2)}, u32[]{:S(2)}) %collective-permute-start.8) | collective-permute-done | bytes 131104 | tf_op jit(solution)/shard_map/ppermute | solution.py:19
  34.3 1.6 %collective-permute-done.9.refs_2_ = bf16[64,1024]{1,0:T(8,128)(2,1)S(1)} collective-permute-done((bf16[64,1024]{1,0:T(8,128)(2,1)S(1)}, bf16[64,1024]{1,0:T(8,128)(2,1)S(1)}, u32[]{:S(2)}, u32[]{:S(2)}) %collective-permute-start.9) | collective-permute-done | bytes 131104 | tf_op jit(solution)/shard_map/ppermute | solution.py:19
  35.9 2.3 %collective-permute-done.10.refs_3_ = bf16[64,1024]{1,0:T(8,128)(2,1)S(1)} collective-permute-done((bf16[64,1024]{1,0:T(8,128)(2,1)S(1)}, bf16[64,1024]{1,0:T(8,128)(2,1)S(1)}, u32[]{:S(2)}, u32[]{:S(2)}) %collective-permute-start.10) | collective-permute-done | bytes 131104 | tf_op jit(solution)/shard_map/ppermute | solution.py:19
  38.2 1.0 %shard_map.48 = (f32[128,1792]{1,0:T(8,128)S(1)}, bf16[128,1792]{1,0:T(8,128)(2,1)S(1)}) custom-call(s32[1]{0:T(128)} %bitcast.place, bf16[64,1024]{1,0:T(8,128)(2,1)S(1)} %pad_maximum_fusion.refs_0_, bf16[64,1024]{1,0:T(8,128)(2,1)S(1)} %collective-permute-done.8.refs_1_, bf16[64,1024]{1,0:T(8,128)(2,1)S(1)} %collective-permute-done.9.refs_2_, ...), custom_call_target="tpu_custom_call" | custom-call | flops 704643072 | bytes 4653056 | tf_op jit(solution)/shard_map/pallas_call | solution.py:161
  39.2 4.8 %collective-permute-start.13 = (bf16[128,1792]{1,0:T(8,128)(2,1)S(1)}, bf16[128,1792]{1,0:T(8,128)(2,1)S(1)}, u32[]{:S(2)}, u32[]{:S(2)}) collective-permute-start(bf16[128,1792]{1,0:T(8,128)(2,1)S(1)} %get-tuple-element.13), channel_id=1, source_target_pairs={{0,1},{1,0},{2,3},{3,2},{4,5},{5,4},{6,7},{7,6},{8,9},{9,8},{10,11... | collective-permute-start | bytes 1376264 | tf_op jit(solution)/shard_map/ppermute | solution.py:19
  44.0 1.1 %collective-permute-done.14.refs_4_ = bf16[512,896]{1,0:T(8,128)(2,1)S(1)} collective-permute-done((bf16[512,896]{1,0:T(8,128)(2,1)S(1)}, bf16[512,896]{1,0:T(8,128)(2,1)S(1)}, u32[]{:S(2)}, u32[]{:S(2)}) %collective-permute-start.14) | collective-permute-done | bytes 917536 | tf_op jit(solution)/shard_map/ppermute | solution.py:28
  45.6 0.5 collective-permute-start.15
  46.2 1.0 %collective-permute-done.15 = bf16[128,896]{1,0:T(8,128)(2,1)S(1)} collective-permute-done((bf16[128,896]{1,0:T(8,128)(2,1)S(1)}, bf16[128,896]{1,0:T(8,128)(2,1)S(1)}, u32[]{:S(2)}, u32[]{:S(2)}) %collective-permute-start.15) | collective-permute-done | bytes 229408 | tf_op jit(solution)/shard_map/ppermute | solution.py:19
  47.5 1.9 %collective-permute-start.16 = (bf16[32,1792]{1,0:T(8,128)(2,1)S(1)}, bf16[32,1792]{1,0:T(8,128)(2,1)S(1)}, u32[]{:S(2)}, u32[]{:S(2)}) collective-permute-start(bf16[32,1792]{1,0:T(8,128)(2,1)S(1)} %get-tuple-element.23), channel_id=1, source_target_pairs={{0,16},{4,20},{8,24},{12,28},{16,0},{20,4},{24,8},{28,12},{1,17},{... | collective-permute-start | bytes 344072 | tf_op jit(solution)/shard_map/ppermute | solution.py:19
  49.4 2.2 %collective-permute-start.17 = (bf16[32,1792]{1,0:T(8,128)(2,1)S(1)}, bf16[32,1792]{1,0:T(8,128)(2,1)S(1)}, u32[]{:S(2)}, u32[]{:S(2)}) collective-permute-start(bf16[32,1792]{1,0:T(8,128)(2,1)S(1)} %get-tuple-element.24), channel_id=1, source_target_pairs={{0,8},{4,12},{8,0},{12,4},{16,24},{20,28},{24,16},{28,20},{1,9},{5... | collective-permute-start | bytes 344072 | tf_op jit(solution)/shard_map/ppermute | solution.py:19
  52.0 5.3 %collective-permute-done.16 = bf16[32,1792]{1,0:T(8,128)(2,1)S(1)} collective-permute-done((bf16[32,1792]{1,0:T(8,128)(2,1)S(1)}, bf16[32,1792]{1,0:T(8,128)(2,1)S(1)}, u32[]{:S(2)}, u32[]{:S(2)}) %collective-permute-start.16) | collective-permute-done | bytes 114720 | tf_op jit(solution)/shard_map/ppermute | solution.py:19
  57.3 2.2 %collective-permute-done.18 = bf16[32,1792]{1,0:T(8,128)(2,1)S(1)} collective-permute-done((bf16[32,1792]{1,0:T(8,128)(2,1)S(1)}, bf16[32,1792]{1,0:T(8,128)(2,1)S(1)}, u32[]{:S(2)}, u32[]{:S(2)}) %collective-permute-start.18) | collective-permute-done | bytes 114720 | tf_op jit(solution)/shard_map/ppermute | solution.py:19
  59.6 0.7 %constant_dynamic-update-slice_fusion = bf16[32,7168]{1,0:T(8,128)(2,1)} fusion(bf16[32,7168]{1,0:T(8,128)(2,1)} %copy-done.3, bf16[32,1792]{1,0:T(8,128)(2,1)S(1)} %collective-permute-done.18, s32[]{:T(128)S(6)} %select_n.111), kind=kLoop, calls=%fused_computation.24 | loop fusion | bytes 229380 | tf_op jit(solution)/shard_map/dynamic_update_slice | solution.py:197
  (39 shorter events, 2.5 us)
Async XLA Ops:
  0.0 16.1 %collective-permute-start = (bf16[576,128]{1,0:T(8,128)(2,1)}, bf16[576,128]{1,0:T(8,128)(2,1)S(1)}, u32[]{:S(2)}, u32[]{:S(2)}) collective-permute-start(bf16[576,128]{1,0:T(8,128)(2,1)} %bitcast.17), channel_id=1, source_target_pairs={{0,24},{1,29},{2,26},{3,31},{4,28},{5,25},{6,30},{7,27},{8,16},{9,... | collective-permute-start | bytes 442376 | tf_op jit(solution)/shard_map/ppermute | solution.py:28
  5.0 13.6 %collective-permute-start.2 = (bf16[576,128]{1,0:T(8,128)(2,1)}, bf16[576,128]{1,0:T(8,128)(2,1)S(1)}, u32[]{:S(2)}, u32[]{:S(2)}) collective-permute-start(bf16[576,128]{1,0:T(8,128)(2,1)} %bitcast.18), channel_id=1, source_target_pairs={{0,16},{1,21},{2,18},{3,23},{4,20},{5,17},{6,22},{7,19},{8,24},{9,... | collective-permute-start | bytes 442376 | tf_op jit(solution)/shard_map/ppermute | solution.py:28
  5.1 13.6 %collective-permute-start.4 = (bf16[576,128]{1,0:T(8,128)(2,1)}, bf16[576,128]{1,0:T(8,128)(2,1)S(1)}, u32[]{:S(2)}, u32[]{:S(2)}) collective-permute-start(bf16[576,128]{1,0:T(8,128)(2,1)} %bitcast.19), channel_id=1, source_target_pairs={{0,8},{1,13},{2,10},{3,15},{4,12},{5,9},{6,14},{7,11},{8,0},{9,5},... | collective-permute-start | bytes 442376 | tf_op jit(solution)/shard_map/ppermute | solution.py:28
  5.6 8.4 %collective-permute-start.6 = (bf16[576,128]{1,0:T(8,128)(2,1)}, bf16[576,128]{1,0:T(8,128)(2,1)S(1)}, u32[]{:S(2)}, u32[]{:S(2)}) collective-permute-start(bf16[576,128]{1,0:T(8,128)(2,1)} %bitcast.20), channel_id=1, source_target_pairs={{0,4},{4,0},{8,12},{12,8},{16,20},{20,16},{24,28},{28,24},{1,5},{5... | collective-permute-start | bytes 442376 | tf_op jit(solution)/shard_map/ppermute | solution.py:19
  7.4 19.9 %collective-permute-start.11 = (bf16[512,896]{1,0:T(8,128)(2,1)}, bf16[512,896]{1,0:T(8,128)(2,1)S(1)}, u32[]{:S(2)}, u32[]{:S(2)}) collective-permute-start(bf16[512,896]{1,0:T(8,128)(2,1)} %refs_4_.1), channel_id=1, source_target_pairs={{0,2},{1,5},{2,0},{3,7},{4,6},{5,1},{6,4},{7,3},{8,10},{9,13},{10,... | collective-permute-start | bytes 2752520 | tf_op jit(solution)/shard_map/ppermute | solution.py:28
  12.9 1.2 %copy-start = (bf16[512,896]{1,0:T(8,128)(2,1)S(1)}, bf16[512,896]{1,0:T(8,128)(2,1)}, u32[]{:S(2)}) copy-start(bf16[512,896]{1,0:T(8,128)(2,1)} %refs_4_.1) | copy-start | bytes 2752516
  14.1 24.1 %collective-permute-start.12 = (bf16[512,896]{1,0:T(8,128)(2,1)S(1)}, bf16[512,896]{1,0:T(8,128)(2,1)S(1)}, u32[]{:S(2)}, u32[]{:S(2)}) collective-permute-start(bf16[512,896]{1,0:T(8,128)(2,1)S(1)} %copy-done), channel_id=1, source_target_pairs={{0,4},{1,3},{2,6},{3,1},{4,0},{5,7},{6,2},{7,5},{8,12},{9,11},{10,... | collective-permute-start | bytes 2752520 | tf_op jit(solution)/shard_map/ppermute | solution.py:28
  16.1 3.2 %collective-permute-start.1 = (bf16[576,128]{1,0:T(8,128)(2,1)S(1)}, bf16[576,128]{1,0:T(8,128)(2,1)S(1)}, u32[]{:S(2)}, u32[]{:S(2)}) collective-permute-start(bf16[576,128]{1,0:T(8,128)(2,1)S(1)} %collective-permute-done.refs_1_), channel_id=1, source_target_pairs={{0,1},{1,0},{2,3},{3,2},{4,5},{5,4},{6,7},{7,6},{8,9},{9,8},{10,11... | collective-permute-start | bytes 442376 | tf_op jit(solution)/shard_map/ppermute | solution.py:19
  18.7 1.4 %collective-permute-start.3 = (bf16[576,128]{1,0:T(8,128)(2,1)S(1)}, bf16[576,128]{1,0:T(8,128)(2,1)S(1)}, u32[]{:S(2)}, u32[]{:S(2)}) collective-permute-start(bf16[576,128]{1,0:T(8,128)(2,1)S(1)} %collective-permute-done.2.refs_3_), channel_id=1, source_target_pairs={{0,1},{1,0},{2,3},{3,2},{4,5},{5,4},{6,7},{7,6},{8,9},{9,8},{10,11... | collective-permute-start | bytes 442376 | tf_op jit(solution)/shard_map/ppermute | solution.py:19
  18.7 1.6 %collective-permute-start.5 = (bf16[576,128]{1,0:T(8,128)(2,1)S(1)}, bf16[576,128]{1,0:T(8,128)(2,1)S(1)}, u32[]{:S(2)}, u32[]{:S(2)}) collective-permute-start(bf16[576,128]{1,0:T(8,128)(2,1)S(1)} %collective-permute-done.4.refs_5_), channel_id=1, source_target_pairs={{0,1},{1,0},{2,3},{3,2},{4,5},{5,4},{6,7},{7,6},{8,9},{9,8},{10,11... | collective-permute-start | bytes 442376 | tf_op jit(solution)/shard_map/ppermute | solution.py:19
  19.2 1.1 %copy-start.1 = (bf16[4,512,128]{2,1,0:T(8,128)(2,1)S(1)}, bf16[4,512,128]{2,1,0:T(8,128)(2,1)}, u32[]{:S(2)}) copy-start(bf16[4,512,128]{2,1,0:T(8,128)(2,1)} %refs_8_.3) | copy-start | bytes 1572868
  19.2 1.1 %copy-start.2 = (bf16[128,576]{0,1:T(8,128)(2,1)S(1)}, bf16[128,576]{0,1:T(8,128)(2,1)}, u32[]{:S(2)}) copy-start(bf16[128,576]{0,1:T(8,128)(2,1)} %param.5) | copy-start | bytes 442372
  22.1 5.1 %collective-permute-start.7 = (bf16[64,512]{1,0:T(8,128)(2,1)S(1)}, bf16[64,512]{1,0:T(8,128)(2,1)S(1)}, u32[]{:S(2)}, u32[]{:S(2)}) collective-permute-start(bf16[64,512]{1,0:T(8,128)(2,1)S(1)} %shard_map.47), channel_id=1, source_target_pairs={{0,2},{1,3},{2,0},{3,1},{4,6},{5,7},{6,4},{7,5},{8,10},{9,11},{10,... | collective-permute-start | bytes 196616 | tf_op jit(solution)/shard_map/ppermute | solution.py:19
  27.2 17.9 %collective-permute-start.14 = (bf16[512,896]{1,0:T(8,128)(2,1)S(1)}, bf16[512,896]{1,0:T(8,128)(2,1)S(1)}, u32[]{:S(2)}, u32[]{:S(2)}) collective-permute-start(bf16[512,896]{1,0:T(8,128)(2,1)S(1)} %collective-permute-done.11.refs_5_), channel_id=1, source_target_pairs={{0,4},{1,3},{2,6},{3,1},{4,0},{5,7},{6,2},{7,5},{8,12},{9,11},{10,... | collective-permute-start | bytes 2752520 | tf_op jit(solution)/shard_map/ppermute | solution.py:28
  28.1 6.2 %collective-permute-start.8 = (bf16[64,1024]{1,0:T(8,128)(2,1)S(1)}, bf16[64,1024]{1,0:T(8,128)(2,1)S(1)}, u32[]{:S(2)}, u32[]{:S(2)}) collective-permute-start(bf16[64,1024]{1,0:T(8,128)(2,1)S(1)} %pad_maximum_fusion.refs_0_), channel_id=1, source_target_pairs={{0,8},{4,12},{8,0},{12,4},{16,24},{20,28},{24,16},{28,20},{1,9},{5... | collective-permute-start | bytes 393224 | tf_op jit(solution)/shard_map/ppermute | solution.py:19
  28.6 7.3 %collective-permute-start.9 = (bf16[64,1024]{1,0:T(8,128)(2,1)S(1)}, bf16[64,1024]{1,0:T(8,128)(2,1)S(1)}, u32[]{:S(2)}, u32[]{:S(2)}) collective-permute-start(bf16[64,1024]{1,0:T(8,128)(2,1)S(1)} %pad_maximum_fusion.refs_0_), channel_id=1, source_target_pairs={{0,16},{4,20},{8,24},{12,28},{16,0},{20,4},{24,8},{28,12},{1,17},{... | collective-permute-start | bytes 393224 | tf_op jit(solution)/shard_map/ppermute | solution.py:19
  31.2 7.0 %collective-permute-start.10 = (bf16[64,1024]{1,0:T(8,128)(2,1)S(1)}, bf16[64,1024]{1,0:T(8,128)(2,1)S(1)}, u32[]{:S(2)}, u32[]{:S(2)}) collective-permute-start(bf16[64,1024]{1,0:T(8,128)(2,1)S(1)} %pad_maximum_fusion.refs_0_), channel_id=1, source_target_pairs={{0,24},{4,28},{8,16},{12,20},{16,8},{20,12},{24,0},{28,4},{1,25},{... | collective-permute-start | bytes 393224 | tf_op jit(solution)/shard_map/ppermute | solution.py:19
  39.2 6.8 %collective-permute-start.13 = (bf16[128,1792]{1,0:T(8,128)(2,1)S(1)}, bf16[128,1792]{1,0:T(8,128)(2,1)S(1)}, u32[]{:S(2)}, u32[]{:S(2)}) collective-permute-start(bf16[128,1792]{1,0:T(8,128)(2,1)S(1)} %get-tuple-element.13), channel_id=1, source_target_pairs={{0,1},{1,0},{2,3},{3,2},{4,5},{5,4},{6,7},{7,6},{8,9},{9,8},{10,11... | collective-permute-start | bytes 1376264 | tf_op jit(solution)/shard_map/ppermute | solution.py:19
  45.6 1.6 %collective-permute-start.15 = (bf16[128,896]{1,0:T(8,128)(2,1)S(1)}, bf16[128,896]{1,0:T(8,128)(2,1)S(1)}, u32[]{:S(2)}, u32[]{:S(2)}) collective-permute-start(bf16[128,896]{1,0:T(8,128)(2,1)S(1)} %get-tuple-element.16), channel_id=1, source_target_pairs={{0,1},{1,0},{2,3},{3,2},{4,5},{5,4},{6,7},{7,6},{8,9},{9,8},{10,11... | collective-permute-start | bytes 688136 | tf_op jit(solution)/shard_map/ppermute | solution.py:19
  47.5 9.8 %collective-permute-start.16 = (bf16[32,1792]{1,0:T(8,128)(2,1)S(1)}, bf16[32,1792]{1,0:T(8,128)(2,1)S(1)}, u32[]{:S(2)}, u32[]{:S(2)}) collective-permute-start(bf16[32,1792]{1,0:T(8,128)(2,1)S(1)} %get-tuple-element.23), channel_id=1, source_target_pairs={{0,16},{4,20},{8,24},{12,28},{16,0},{20,4},{24,8},{28,12},{1,17},{... | collective-permute-start | bytes 344072 | tf_op jit(solution)/shard_map/ppermute | solution.py:19
  49.4 7.9 %collective-permute-start.17 = (bf16[32,1792]{1,0:T(8,128)(2,1)S(1)}, bf16[32,1792]{1,0:T(8,128)(2,1)S(1)}, u32[]{:S(2)}, u32[]{:S(2)}) collective-permute-start(bf16[32,1792]{1,0:T(8,128)(2,1)S(1)} %get-tuple-element.24), channel_id=1, source_target_pairs={{0,8},{4,12},{8,0},{12,4},{16,24},{20,28},{24,16},{28,20},{1,9},{5... | collective-permute-start | bytes 344072 | tf_op jit(solution)/shard_map/ppermute | solution.py:19
  51.6 7.9 %collective-permute-start.18 = (bf16[32,1792]{1,0:T(8,128)(2,1)S(1)}, bf16[32,1792]{1,0:T(8,128)(2,1)S(1)}, u32[]{:S(2)}, u32[]{:S(2)}) collective-permute-start(bf16[32,1792]{1,0:T(8,128)(2,1)S(1)} %get-tuple-element.21), channel_id=1, source_target_pairs={{0,24},{4,28},{8,16},{12,20},{16,8},{20,12},{24,0},{28,4},{1,25},{... | collective-permute-start | bytes 344072 | tf_op jit(solution)/shard_map/ppermute | solution.py:19
  57.3 2.3 %copy-start.3 = (bf16[32,7168]{1,0:T(8,128)(2,1)}, bf16[32,7168]{1,0:T(8,128)(2,1)S(1)}, u32[]{:S(2)}) copy-start(bf16[32,7168]{1,0:T(8,128)(2,1)S(1)} %constant_dynamic-update-slice_fusion.1) | copy-start | bytes 1376260

commit v6 on v5

--- a/solution.py
+++ b/solution.py
@@ -107,6 +107,25 @@
                 columns(j * width, depth, [pieces[i] for i in chosen[core]])
 
 
+def project_half(chips, depth, half, *refs):
+    *operands, out = refs
+    values, pieces = operands[:chips], operands[chips:]
+    rows = values[0].shape[0]
+    stop = depth + sum(piece.shape[0] for piece in pieces)
+    chosen = [
+        part[:, depth:stop].astype(jnp.float32)[half * rows // 2 : (half + 1) * rows // 2] for part in values
+    ]
+    chosen = jnp.concatenate(chosen, 0).astype(jnp.bfloat16)
+    total, at = None, 0
+    for piece in pieces:
+        term = jnp.dot(
+            chosen[:, at : at + piece.shape[0]], piece[...], preferred_element_type=jnp.float32
+        )
+        total = term if total is None else total + term
+        at += piece.shape[0]
+    out[...] = total.astype(out.dtype)
+
+
 def shards(queries, latents, value_up, out_weight):
     count, heads = lax.axis_size("ctx"), lax.axis_size("exp")
     ctx, exp = lax.axis_index("ctx"), lax.axis_index("exp")
@@ -179,9 +198,24 @@
         [(0, [0, 1, *others], [0, 2, *others]), (0, [2], [1])], out_weight, first, second, *rest[::2]
     )
     other = send(away, "exp", heads, 1).astype(jnp.float32)
-    last = list(range(1 + len(rest) // 2))
-    keep_last, away = projection([(depth, last, last)], corner, *rest[1::2])
-    other_last = send(away, "exp", heads, 1).astype(jnp.float32)
+    last = [corner, *rest[1::2]]
+
+    def last_half(half, dtype):
+        return pl.pallas_call(
+            functools.partial(project_half, len(values), depth, half),
+            out_shape=jax.ShapeDtypeStruct((mine, width), dtype),
+            in_specs=[VMEM] * (len(values) + len(last)),
+            out_specs=VMEM,
+            compiler_params=pltpu.CompilerParams(vmem_limit_bytes=2**24),
+            cost_estimate=pl.CostEstimate(
+                flops=2 * mine * sum(p.size for p in last),
+                bytes_accessed=2 * (len(values) * held.size + sum(p.size for p in last)) + 4 * mine * width,
+                transcendentals=0,
+            ),
+        )(*values, *last)
+
+    other_last = send(last_half(1, jnp.bfloat16), "exp", heads, 1).astype(jnp.float32)
+    keep_last = last_half(0, jnp.float32)
     here = keep[:, :width] + other[:, :width]
     beside = keep[:, width:] + other[:, width:] + keep_last + other_last
     left, right = jnp.where(ctx % 2 == 0, here, beside), jnp.where(ctx % 2 == 0, beside, here)

time: 60.5 us -> 62.1 us (1.026)
  Pallas kernels: 5.16 us -> 7.27 us
  local copies, waits for them, and re-layouts: 5.19 us -> 3.19 us
  waiting for transfers between devices: 21.3 us -> 23.1 us
    ppermute x13, waiting for transfers between devices: 17.5 us -> 20.4 us  [send(): return lax.ppermute(value, axis, [(i, i ^ shift) for i in range(size)])]
    gather x2, local copies, waits for them, and re-layouts: 2.63 us -> 0.73 us  [shards(): rows = jnp.take(queries.reshape(heads, part, own_heads, lat), order, axis=0)]
    pallas_call x2 -> x1, Pallas kernels: 1.49 us -> 2.97 us  [projection(): pl.pallas_call(functools.partial(project, len(values), groups), out_shape...]
    ppermute x6, waiting for transfers between devices: 3.74 us -> 2.63 us  [route(): return lax.ppermute(value, ('ctx', 'exp'), pairs)]
  transfers between devices with their start and end apart: 19 -> 19, of which waited for: 12 -> 11; matrix products, arithmetic and copies ran while one was open for 8% -> 4% of each run, Pallas kernels for 9% -> 12%
where the time goes in v6:
time: 62.1 us; the launch traced here: 61.9 us
  starting transfers between devices  27.6 us (44%)
  waiting for transfers between devices  23.1 us (37%)
  Pallas kernels  7.27 us (12%)
  local copies, waits for them, and re-layouts  3.19 us (5%)
    ppermute x13, waiting for transfers between devices, send(): return lax.ppermute(value, axis, [(i, i ^ shift) for i in range(size)])  20.4 us
    ppermute x13, starting transfers between devices, send(): return lax.ppermute(value, axis, [(i, i ^ shift) for i in range(size)])  17.6 us
    ppermute x6, starting transfers between devices, route(): return lax.ppermute(value, ('ctx', 'exp'), pairs)  10.1 us
    pallas_call x2, Pallas kernels, attention(): pl.pallas_call(functools.partial(attend, part, low), out_shape=jax.ShapeD...  3.68 us
    pallas_call x1, Pallas kernels, projection(): pl.pallas_call(functools.partial(project, len(values), groups), out_shape...  2.97 us
    ppermute x6, waiting for transfers between devices, route(): return lax.ppermute(value, ('ctx', 'exp'), pairs)  2.63 us
    unnamed x9, local copies, waits for them, and re-layouts  1.38 us
  transfers between devices with their start and end apart: 19, of which 11 were waited for; matrix products, arithmetic and copies ran while one was open for 4% of the time, Pallas kernels for 12%

profile of v6, /device:TPU:0, one launch (start us, length us, event | category | flops | bytes accessed | tf_op | source)
XLA Modules:
  0.0 61.9 jit_solution(17486457438672610860)
XLA Ops:
  0.0 5.0 %collective-permute-start = (bf16[576,128]{1,0:T(8,128)(2,1)}, bf16[576,128]{1,0:T(8,128)(2,1)S(1)}, u32[]{:S(2)}, u32[]{:S(2)}) collective-permute-start(bf16[576,128]{1,0:T(8,128)(2,1)} %bitcast.17), channel_id=1, source_target_pairs={{0,24},{1,29},{2,26},{3,31},{4,28},{5,25},{6,30},{7,27},{8,16},{9,... | collective-permute-start | bytes 442376 | tf_op jit(solution)/shard_map/ppermute | solution.py:28
  5.1 0.6 collective-permute-start.4
  5.6 1.7 %collective-permute-start.6 = (bf16[576,128]{1,0:T(8,128)(2,1)}, bf16[576,128]{1,0:T(8,128)(2,1)S(1)}, u32[]{:S(2)}, u32[]{:S(2)}) collective-permute-start(bf16[576,128]{1,0:T(8,128)(2,1)} %bitcast.20), channel_id=1, source_target_pairs={{0,4},{4,0},{8,12},{12,8},{16,20},{20,16},{24,28},{28,24},{1,5},{5... | collective-permute-start | bytes 442376 | tf_op jit(solution)/shard_map/ppermute | solution.py:19
  7.4 1.5 %collective-permute-start.11 = (bf16[512,896]{1,0:T(8,128)(2,1)}, bf16[512,896]{1,0:T(8,128)(2,1)}, u32[]{:S(2)}, u32[]{:S(2)}) collective-permute-start(bf16[512,896]{1,0:T(8,128)(2,1)} %refs_4_.1), channel_id=1, source_target_pairs={{0,2},{1,5},{2,0},{3,7},{4,6},{5,1},{6,4},{7,3},{8,10},{9,13},{10,... | collective-permute-start | bytes 2752520 | tf_op jit(solution)/shard_map/ppermute | solution.py:28
  8.8 1.4 %copy.5 = bf16[128,4,576]{2,0,1:T(8,128)(2,1)S(1)} copy(bf16[128,4,576]{0,2,1:T(8,128)(2,1)} %param.4) | data formatting | bytes 1179648 | tf_op args[0]
  10.3 0.7 %gather_fusion = bf16[4,32,4,576]{3,1,2,0:T(8,128)(2,1)S(1)} fusion(bf16[4,32,4,576]{3,1,2,0:T(8,128)(2,1)S(1)} %copy.6, s32[1024]{0:T(1024)S(1)} %pad_clamp_fusion), kind=kCustom, calls=%fused_computation | custom fusion | bytes 1179664 | tf_op jit(solution)/shard_map/jit(_take)/gather | solution.py:143
  11.5 2.5 %collective-permute-done.6.refs_7_ = bf16[576,128]{1,0:T(8,128)(2,1)S(1)} collective-permute-done((bf16[576,128]{1,0:T(8,128)(2,1)}, bf16[576,128]{1,0:T(8,128)(2,1)S(1)}, u32[]{:S(2)}, u32[]{:S(2)}) %collective-permute-start.6) | collective-permute-done | bytes 147488 | tf_op jit(solution)/shard_map/ppermute | solution.py:19
  14.0 2.0 %collective-permute-start.12 = (bf16[512,896]{1,0:T(8,128)(2,1)S(1)}, bf16[512,896]{1,0:T(8,128)(2,1)S(1)}, u32[]{:S(2)}, u32[]{:S(2)}) collective-permute-start(bf16[512,896]{1,0:T(8,128)(2,1)S(1)} %copy-done), channel_id=1, source_target_pairs={{0,4},{1,3},{2,6},{3,1},{4,0},{5,7},{6,2},{7,5},{8,12},{9,11},{10,... | collective-permute-start | bytes 2752520 | tf_op jit(solution)/shard_map/ppermute | solution.py:28
  16.1 2.6 %collective-permute-done.2.refs_3_ = bf16[576,128]{1,0:T(8,128)(2,1)S(1)} collective-permute-done((bf16[576,128]{1,0:T(8,128)(2,1)}, bf16[576,128]{1,0:T(8,128)(2,1)S(1)}, u32[]{:S(2)}, u32[]{:S(2)}) %collective-permute-start.2) | collective-permute-done | bytes 147488 | tf_op jit(solution)/shard_map/ppermute | solution.py:28
  18.7 0.5 collective-permute-start.5
  19.3 0.8 %collective-permute-done.3.refs_4_ = bf16[576,128]{1,0:T(8,128)(2,1)S(1)} collective-permute-done((bf16[576,128]{1,0:T(8,128)(2,1)S(1)}, bf16[576,128]{1,0:T(8,128)(2,1)S(1)}, u32[]{:S(2)}, u32[]{:S(2)}) %collective-permute-start.3) | collective-permute-done | bytes 147488 | tf_op jit(solution)/shard_map/ppermute | solution.py:19
  20.3 1.8 %shard_map.47 = bf16[64,512]{1,0:T(8,128)(2,1)S(1)} custom-call(s32[10]{0:T(128)S(1)} %stack.40.place, bf16[4,64,576]{2,1,0:T(8,128)(2,1)S(1)} %get-tuple-element.16.query, bf16[576,128]{1,0:T(8,128)(2,1)S(1)} %bitcast.21, bf16[576,128]{1,0:T(8,128)(2,1)S(1)} %collective-permute-done.refs_1_, bf16[576,128]{1,0:T(8,128)(2,1)S(1)} %collective-permute-done.1.refs_2_, ...), custom_call_target="tpu_custom_call" | custom-call | flops 570425344 | bytes 2293760 | tf_op jit(solution)/shard_map/pallas_call | solution.py:149
  22.1 1.6 %collective-permute-start.7 = (bf16[64,512]{1,0:T(8,128)(2,1)S(1)}, bf16[64,512]{1,0:T(8,128)(2,1)S(1)}, u32[]{:S(2)}, u32[]{:S(2)}) collective-permute-start(bf16[64,512]{1,0:T(8,128)(2,1)S(1)} %shard_map.47), channel_id=1, source_target_pairs={{0,2},{1,3},{2,0},{3,1},{4,6},{5,7},{6,4},{7,5},{8,10},{9,11},{10,... | collective-permute-start | bytes 196616 | tf_op jit(solution)/shard_map/ppermute | solution.py:19
  23.7 1.8 %shard_map.46 = bf16[64,512]{1,0:T(8,128)(2,1)S(1)} custom-call(s32[10]{0:T(128)S(1)} %stack.40.place, bf16[4,64,576]{2,1,0:T(8,128)(2,1)S(1)} %get-tuple-element.15.query, bf16[576,128]{1,0:T(8,128)(2,1)S(1)} %bitcast.22, bf16[576,128]{1,0:T(8,128)(2,1)S(1)} %collective-permute-done.refs_1_, bf16[576,128]{1,0:T(8,128)(2,1)S(1)} %collective-permute-done.1.refs_2_, ...), custom_call_target="tpu_custom_call" | custom-call | flops 570425344 | bytes 2293760 | tf_op jit(solution)/shard_map/pallas_call | solution.py:149
  25.5 1.7 %collective-permute-done.7 = bf16[64,512]{1,0:T(8,128)(2,1)S(1)} collective-permute-done((bf16[64,512]{1,0:T(8,128)(2,1)S(1)}, bf16[64,512]{1,0:T(8,128)(2,1)S(1)}, u32[]{:S(2)}, u32[]{:S(2)}) %collective-permute-start.7) | collective-permute-done | bytes 65568 | tf_op jit(solution)/shard_map/ppermute | solution.py:19
  27.2 0.9 %collective-permute-start.14 = (bf16[512,896]{1,0:T(8,128)(2,1)}, bf16[512,896]{1,0:T(8,128)(2,1)S(1)}, u32[]{:S(2)}, u32[]{:S(2)}) collective-permute-start(bf16[512,896]{1,0:T(8,128)(2,1)} %collective-permute-done.11.refs_5_), channel_id=1, source_target_pairs={{0,4},{1,3},{2,6},{3,1},{4,0},{5,7},{6,2},{7,5},{8,12},{9,11},{10,... | collective-permute-start | bytes 2752520 | tf_op jit(solution)/shard_map/ppermute | solution.py:28
  28.1 0.5 collective-permute-start.8
  28.6 2.6 %collective-permute-start.9 = (bf16[64,1024]{1,0:T(8,128)(2,1)S(1)}, bf16[64,1024]{1,0:T(8,128)(2,1)S(1)}, u32[]{:S(2)}, u32[]{:S(2)}) collective-permute-start(bf16[64,1024]{1,0:T(8,128)(2,1)S(1)} %pad_maximum_fusion.refs_0_), channel_id=1, source_target_pairs={{0,16},{4,20},{8,24},{12,28},{16,0},{20,4},{24,8},{28,12},{1,17},{... | collective-permute-start | bytes 393224 | tf_op jit(solution)/shard_map/ppermute | solution.py:19
  31.2 1.4 %collective-permute-start.10 = (bf16[64,1024]{1,0:T(8,128)(2,1)S(1)}, bf16[64,1024]{1,0:T(8,128)(2,1)S(1)}, u32[]{:S(2)}, u32[]{:S(2)}) collective-permute-start(bf16[64,1024]{1,0:T(8,128)(2,1)S(1)} %pad_maximum_fusion.refs_0_), channel_id=1, source_target_pairs={{0,24},{4,28},{8,16},{12,20},{16,8},{20,12},{24,0},{28,4},{1,25},{... | collective-permute-start | bytes 393224 | tf_op jit(solution)/shard_map/ppermute | solution.py:19
  32.6 1.7 %collective-permute-done.8.refs_1_ = bf16[64,1024]{1,0:T(8,128)(2,1)S(1)} collective-permute-done((bf16[64,1024]{1,0:T(8,128)(2,1)S(1)}, bf16[64,1024]{1,0:T(8,128)(2,1)S(1)}, u32[]{:S(2)}, u32[]{:S(2)}) %collective-permute-start.8) | collective-permute-done | bytes 131104 | tf_op jit(solution)/shard_map/ppermute | solution.py:19
  34.3 1.6 %collective-permute-done.9.refs_2_ = bf16[64,1024]{1,0:T(8,128)(2,1)S(1)} collective-permute-done((bf16[64,1024]{1,0:T(8,128)(2,1)S(1)}, bf16[64,1024]{1,0:T(8,128)(2,1)S(1)}, u32[]{:S(2)}, u32[]{:S(2)}) %collective-permute-start.9) | collective-permute-done | bytes 131104 | tf_op jit(solution)/shard_map/ppermute | solution.py:19
  35.9 2.3 %collective-permute-done.10.refs_3_ = bf16[64,1024]{1,0:T(8,128)(2,1)S(1)} collective-permute-done((bf16[64,1024]{1,0:T(8,128)(2,1)S(1)}, bf16[64,1024]{1,0:T(8,128)(2,1)S(1)}, u32[]{:S(2)}, u32[]{:S(2)}) %collective-permute-start.10) | collective-permute-done | bytes 131104 | tf_op jit(solution)/shard_map/ppermute | solution.py:19
  38.2 3.0 %shard_map.48 = (f32[128,1792]{1,0:T(8,128)S(1)}, bf16[128,1792]{1,0:T(8,128)(2,1)}) custom-call(s32[1]{0:T(128)} %bitcast.place, bf16[64,1024]{1,0:T(8,128)(2,1)S(1)} %pad_maximum_fusion.refs_0_, bf16[64,1024]{1,0:T(8,128)(2,1)S(1)} %collective-permute-done.8.refs_1_, bf16[64,1024]{1,0:T(8,128)(2,1)S(1)} %collective-permute-done.9.refs_2_, ...), custom_call_target="tpu_custom_call" | custom-call | flops 704643072 | bytes 4653056 | tf_op jit(solution)/shard_map/pallas_call | solution.py:180
  41.2 4.7 %collective-permute-start.13 = (bf16[128,1792]{1,0:T(8,128)(2,1)}, bf16[128,1792]{1,0:T(8,128)(2,1)S(1)}, u32[]{:S(2)}, u32[]{:S(2)}) collective-permute-start(bf16[128,1792]{1,0:T(8,128)(2,1)} %get-tuple-element.11), channel_id=1, source_target_pairs={{0,1},{1,0},{2,3},{3,2},{4,5},{5,4},{6,7},{7,6},{8,9},{9,8},{10,11... | collective-permute-start | bytes 1376264 | tf_op jit(solution)/shard_map/ppermute | solution.py:19
  45.9 0.3 shard_map.50
  46.3 1.2 %collective-permute-done.13 = bf16[128,1792]{1,0:T(8,128)(2,1)S(1)} collective-permute-done((bf16[128,1792]{1,0:T(8,128)(2,1)}, bf16[128,1792]{1,0:T(8,128)(2,1)S(1)}, u32[]{:S(2)}, u32[]{:S(2)}) %collective-permute-start.13) | collective-permute-done | bytes 458784 | tf_op jit(solution)/shard_map/ppermute | solution.py:19
  48.3 2.9 %collective-permute-start.16 = (bf16[32,1792]{1,0:T(8,128)(2,1)S(1)}, bf16[32,1792]{1,0:T(8,128)(2,1)S(1)}, u32[]{:S(2)}, u32[]{:S(2)}) collective-permute-start(bf16[32,1792]{1,0:T(8,128)(2,1)S(1)} %get-tuple-element.19), channel_id=1, source_target_pairs={{0,16},{4,20},{8,24},{12,28},{16,0},{20,4},{24,8},{28,12},{1,17},{... | collective-permute-start | bytes 344072 | tf_op jit(solution)/shard_map/ppermute | solution.py:19
  51.2 0.4 collective-permute-start.17
  51.5 1.3 %collective-permute-start.18 = (bf16[32,1792]{1,0:T(8,128)(2,1)S(1)}, bf16[32,1792]{1,0:T(8,128)(2,1)S(1)}, u32[]{:S(2)}, u32[]{:S(2)}) collective-permute-start(bf16[32,1792]{1,0:T(8,128)(2,1)S(1)} %get-tuple-element.17), channel_id=1, source_target_pairs={{0,24},{4,28},{8,16},{12,20},{16,8},{20,12},{24,0},{28,4},{1,25},{... | collective-permute-start | bytes 344072 | tf_op jit(solution)/shard_map/ppermute | solution.py:19
  52.8 4.8 %collective-permute-done.16 = bf16[32,1792]{1,0:T(8,128)(2,1)S(1)} collective-permute-done((bf16[32,1792]{1,0:T(8,128)(2,1)S(1)}, bf16[32,1792]{1,0:T(8,128)(2,1)S(1)}, u32[]{:S(2)}, u32[]{:S(2)}) %collective-permute-start.16) | collective-permute-done | bytes 114720 | tf_op jit(solution)/shard_map/ppermute | solution.py:19
  57.7 3.5 %collective-permute-done.18 = bf16[32,1792]{1,0:T(8,128)(2,1)S(1)} collective-permute-done((bf16[32,1792]{1,0:T(8,128)(2,1)S(1)}, bf16[32,1792]{1,0:T(8,128)(2,1)S(1)}, u32[]{:S(2)}, u32[]{:S(2)}) %collective-permute-start.18) | collective-permute-done | bytes 114720 | tf_op jit(solution)/shard_map/ppermute | solution.py:19
  61.3 0.7 %constant_dynamic-update-slice_fusion = bf16[32,7168]{1,0:T(8,128)(2,1)} fusion(bf16[32,7168]{1,0:T(8,128)(2,1)} %copy-done.3, bf16[32,1792]{1,0:T(8,128)(2,1)S(1)} %collective-permute-done.18, s32[]{:T(128)S(6)} %select_n.111), kind=kLoop, calls=%fused_computation.24 | loop fusion | bytes 229380 | tf_op jit(solution)/shard_map/dynamic_update_slice | solution.py:231
  (40 shorter events, 1.7 us)
Async XLA Ops:
  0.0 16.1 %collective-permute-start = (bf16[576,128]{1,0:T(8,128)(2,1)}, bf16[576,128]{1,0:T(8,128)(2,1)S(1)}, u32[]{:S(2)}, u32[]{:S(2)}) collective-permute-start(bf16[576,128]{1,0:T(8,128)(2,1)} %bitcast.17), channel_id=1, source_target_pairs={{0,24},{1,29},{2,26},{3,31},{4,28},{5,25},{6,30},{7,27},{8,16},{9,... | collective-permute-start | bytes 442376 | tf_op jit(solution)/shard_map/ppermute | solution.py:28
  5.0 13.6 %collective-permute-start.2 = (bf16[576,128]{1,0:T(8,128)(2,1)}, bf16[576,128]{1,0:T(8,128)(2,1)S(1)}, u32[]{:S(2)}, u32[]{:S(2)}) collective-permute-start(bf16[576,128]{1,0:T(8,128)(2,1)} %bitcast.18), channel_id=1, source_target_pairs={{0,16},{1,21},{2,18},{3,23},{4,20},{5,17},{6,22},{7,19},{8,24},{9,... | collective-permute-start | bytes 442376 | tf_op jit(solution)/shard_map/ppermute | solution.py:28
  5.1 13.6 %collective-permute-start.4 = (bf16[576,128]{1,0:T(8,128)(2,1)}, bf16[576,128]{1,0:T(8,128)(2,1)S(1)}, u32[]{:S(2)}, u32[]{:S(2)}) collective-permute-start(bf16[576,128]{1,0:T(8,128)(2,1)} %bitcast.19), channel_id=1, source_target_pairs={{0,8},{1,13},{2,10},{3,15},{4,12},{5,9},{6,14},{7,11},{8,0},{9,5},... | collective-permute-start | bytes 442376 | tf_op jit(solution)/shard_map/ppermute | solution.py:28
  5.6 8.4 %collective-permute-start.6 = (bf16[576,128]{1,0:T(8,128)(2,1)}, bf16[576,128]{1,0:T(8,128)(2,1)S(1)}, u32[]{:S(2)}, u32[]{:S(2)}) collective-permute-start(bf16[576,128]{1,0:T(8,128)(2,1)} %bitcast.20), channel_id=1, source_target_pairs={{0,4},{4,0},{8,12},{12,8},{16,20},{20,16},{24,28},{28,24},{1,5},{5... | collective-permute-start | bytes 442376 | tf_op jit(solution)/shard_map/ppermute | solution.py:19
  7.4 19.9 %collective-permute-start.11 = (bf16[512,896]{1,0:T(8,128)(2,1)}, bf16[512,896]{1,0:T(8,128)(2,1)}, u32[]{:S(2)}, u32[]{:S(2)}) collective-permute-start(bf16[512,896]{1,0:T(8,128)(2,1)} %refs_4_.1), channel_id=1, source_target_pairs={{0,2},{1,5},{2,0},{3,7},{4,6},{5,1},{6,4},{7,3},{8,10},{9,13},{10,... | collective-permute-start | bytes 2752520 | tf_op jit(solution)/shard_map/ppermute | solution.py:28
  11.1 3.0 %copy-start = (bf16[512,896]{1,0:T(8,128)(2,1)S(1)}, bf16[512,896]{1,0:T(8,128)(2,1)}, u32[]{:S(2)}) copy-start(bf16[512,896]{1,0:T(8,128)(2,1)} %refs_4_.1) | copy-start | bytes 2752516
  14.0 24.2 %collective-permute-start.12 = (bf16[512,896]{1,0:T(8,128)(2,1)S(1)}, bf16[512,896]{1,0:T(8,128)(2,1)S(1)}, u32[]{:S(2)}, u32[]{:S(2)}) collective-permute-start(bf16[512,896]{1,0:T(8,128)(2,1)S(1)} %copy-done), channel_id=1, source_target_pairs={{0,4},{1,3},{2,6},{3,1},{4,0},{5,7},{6,2},{7,5},{8,12},{9,11},{10,... | collective-permute-start | bytes 2752520 | tf_op jit(solution)/shard_map/ppermute | solution.py:28
  16.1 3.2 %collective-permute-start.1 = (bf16[576,128]{1,0:T(8,128)(2,1)S(1)}, bf16[576,128]{1,0:T(8,128)(2,1)S(1)}, u32[]{:S(2)}, u32[]{:S(2)}) collective-permute-start(bf16[576,128]{1,0:T(8,128)(2,1)S(1)} %collective-permute-done.refs_1_), channel_id=1, source_target_pairs={{0,1},{1,0},{2,3},{3,2},{4,5},{5,4},{6,7},{7,6},{8,9},{9,8},{10,11... | collective-permute-start | bytes 442376 | tf_op jit(solution)/shard_map/ppermute | solution.py:19
  18.7 1.4 %collective-permute-start.3 = (bf16[576,128]{1,0:T(8,128)(2,1)S(1)}, bf16[576,128]{1,0:T(8,128)(2,1)S(1)}, u32[]{:S(2)}, u32[]{:S(2)}) collective-permute-start(bf16[576,128]{1,0:T(8,128)(2,1)S(1)} %collective-permute-done.2.refs_3_), channel_id=1, source_target_pairs={{0,1},{1,0},{2,3},{3,2},{4,5},{5,4},{6,7},{7,6},{8,9},{9,8},{10,11... | collective-permute-start | bytes 442376 | tf_op jit(solution)/shard_map/ppermute | solution.py:19
  18.7 1.6 %collective-permute-start.5 = (bf16[576,128]{1,0:T(8,128)(2,1)S(1)}, bf16[576,128]{1,0:T(8,128)(2,1)S(1)}, u32[]{:S(2)}, u32[]{:S(2)}) collective-permute-start(bf16[576,128]{1,0:T(8,128)(2,1)S(1)} %collective-permute-done.4.refs_5_), channel_id=1, source_target_pairs={{0,1},{1,0},{2,3},{3,2},{4,5},{5,4},{6,7},{7,6},{8,9},{9,8},{10,11... | collective-permute-start | bytes 442376 | tf_op jit(solution)/shard_map/ppermute | solution.py:19
  19.2 1.1 %copy-start.1 = (bf16[4,512,128]{2,1,0:T(8,128)(2,1)S(1)}, bf16[4,512,128]{2,1,0:T(8,128)(2,1)}, u32[]{:S(2)}) copy-start(bf16[4,512,128]{2,1,0:T(8,128)(2,1)} %refs_8_.3) | copy-start | bytes 1572868
  19.2 1.1 %copy-start.2 = (bf16[128,576]{0,1:T(8,128)(2,1)S(1)}, bf16[128,576]{0,1:T(8,128)(2,1)}, u32[]{:S(2)}) copy-start(bf16[128,576]{0,1:T(8,128)(2,1)} %param.5) | copy-start | bytes 442372
  22.1 5.1 %collective-permute-start.7 = (bf16[64,512]{1,0:T(8,128)(2,1)S(1)}, bf16[64,512]{1,0:T(8,128)(2,1)S(1)}, u32[]{:S(2)}, u32[]{:S(2)}) collective-permute-start(bf16[64,512]{1,0:T(8,128)(2,1)S(1)} %shard_map.47), channel_id=1, source_target_pairs={{0,2},{1,3},{2,0},{3,1},{4,6},{5,7},{6,4},{7,5},{8,10},{9,11},{10,... | collective-permute-start | bytes 196616 | tf_op jit(solution)/shard_map/ppermute | solution.py:19
  27.2 18.7 %collective-permute-start.14 = (bf16[512,896]{1,0:T(8,128)(2,1)}, bf16[512,896]{1,0:T(8,128)(2,1)S(1)}, u32[]{:S(2)}, u32[]{:S(2)}) collective-permute-start(bf16[512,896]{1,0:T(8,128)(2,1)} %collective-permute-done.11.refs_5_), channel_id=1, source_target_pairs={{0,4},{1,3},{2,6},{3,1},{4,0},{5,7},{6,2},{7,5},{8,12},{9,11},{10,... | collective-permute-start | bytes 2752520 | tf_op jit(solution)/shard_map/ppermute | solution.py:28
  28.1 6.2 %collective-permute-start.8 = (bf16[64,1024]{1,0:T(8,128)(2,1)S(1)}, bf16[64,1024]{1,0:T(8,128)(2,1)S(1)}, u32[]{:S(2)}, u32[]{:S(2)}) collective-permute-start(bf16[64,1024]{1,0:T(8,128)(2,1)S(1)} %pad_maximum_fusion.refs_0_), channel_id=1, source_target_pairs={{0,8},{4,12},{8,0},{12,4},{16,24},{20,28},{24,16},{28,20},{1,9},{5... | collective-permute-start | bytes 393224 | tf_op jit(solution)/shard_map/ppermute | solution.py:19
  28.6 7.3 %collective-permute-start.9 = (bf16[64,1024]{1,0:T(8,128)(2,1)S(1)}, bf16[64,1024]{1,0:T(8,128)(2,1)S(1)}, u32[]{:S(2)}, u32[]{:S(2)}) collective-permute-start(bf16[64,1024]{1,0:T(8,128)(2,1)S(1)} %pad_maximum_fusion.refs_0_), channel_id=1, source_target_pairs={{0,16},{4,20},{8,24},{12,28},{16,0},{20,4},{24,8},{28,12},{1,17},{... | collective-permute-start | bytes 393224 | tf_op jit(solution)/shard_map/ppermute | solution.py:19
  31.2 7.0 %collective-permute-start.10 = (bf16[64,1024]{1,0:T(8,128)(2,1)S(1)}, bf16[64,1024]{1,0:T(8,128)(2,1)S(1)}, u32[]{:S(2)}, u32[]{:S(2)}) collective-permute-start(bf16[64,1024]{1,0:T(8,128)(2,1)S(1)} %pad_maximum_fusion.refs_0_), channel_id=1, source_target_pairs={{0,24},{4,28},{8,16},{12,20},{16,8},{20,12},{24,0},{28,4},{1,25},{... | collective-permute-start | bytes 393224 | tf_op jit(solution)/shard_map/ppermute | solution.py:19
  41.2 6.4 %collective-permute-start.13 = (bf16[128,1792]{1,0:T(8,128)(2,1)}, bf16[128,1792]{1,0:T(8,128)(2,1)S(1)}, u32[]{:S(2)}, u32[]{:S(2)}) collective-permute-start(bf16[128,1792]{1,0:T(8,128)(2,1)} %get-tuple-element.11), channel_id=1, source_target_pairs={{0,1},{1,0},{2,3},{3,2},{4,5},{5,4},{6,7},{7,6},{8,9},{9,8},{10,11... | collective-permute-start | bytes 1376264 | tf_op jit(solution)/shard_map/ppermute | solution.py:19
  46.2 1.7 %collective-permute-start.15 = (bf16[128,896]{1,0:T(8,128)(2,1)S(1)}, bf16[128,896]{1,0:T(8,128)(2,1)S(1)}, u32[]{:S(2)}, u32[]{:S(2)}) collective-permute-start(bf16[128,896]{1,0:T(8,128)(2,1)S(1)} %shard_map.50), channel_id=1, source_target_pairs={{0,1},{1,0},{2,3},{3,2},{4,5},{5,4},{6,7},{7,6},{8,9},{9,8},{10,11... | collective-permute-start | bytes 688136 | tf_op jit(solution)/shard_map/ppermute | solution.py:19
  48.3 9.4 %collective-permute-start.16 = (bf16[32,1792]{1,0:T(8,128)(2,1)S(1)}, bf16[32,1792]{1,0:T(8,128)(2,1)S(1)}, u32[]{:S(2)}, u32[]{:S(2)}) collective-permute-start(bf16[32,1792]{1,0:T(8,128)(2,1)S(1)} %get-tuple-element.19), channel_id=1, source_target_pairs={{0,16},{4,20},{8,24},{12,28},{16,0},{20,4},{24,8},{28,12},{1,17},{... | collective-permute-start | bytes 344072 | tf_op jit(solution)/shard_map/ppermute | solution.py:19
  51.2 6.5 %collective-permute-start.17 = (bf16[32,1792]{1,0:T(8,128)(2,1)S(1)}, bf16[32,1792]{1,0:T(8,128)(2,1)S(1)}, u32[]{:S(2)}, u32[]{:S(2)}) collective-permute-start(bf16[32,1792]{1,0:T(8,128)(2,1)S(1)} %get-tuple-element.20), channel_id=1, source_target_pairs={{0,8},{4,12},{8,0},{12,4},{16,24},{20,28},{24,16},{28,20},{1,9},{5... | collective-permute-start | bytes 344072 | tf_op jit(solution)/shard_map/ppermute | solution.py:19
  51.5 9.7 %collective-permute-start.18 = (bf16[32,1792]{1,0:T(8,128)(2,1)S(1)}, bf16[32,1792]{1,0:T(8,128)(2,1)S(1)}, u32[]{:S(2)}, u32[]{:S(2)}) collective-permute-start(bf16[32,1792]{1,0:T(8,128)(2,1)S(1)} %get-tuple-element.17), channel_id=1, source_target_pairs={{0,24},{4,28},{8,16},{12,20},{16,8},{20,12},{24,0},{28,4},{1,25},{... | collective-permute-start | bytes 344072 | tf_op jit(solution)/shard_map/ppermute | solution.py:19
  57.7 3.6 %copy-start.3 = (bf16[32,7168]{1,0:T(8,128)(2,1)}, bf16[32,7168]{1,0:T(8,128)(2,1)S(1)}, u32[]{:S(2)}) copy-start(bf16[32,7168]{1,0:T(8,128)(2,1)S(1)} %constant_dynamic-update-slice_fusion.1) | copy-start | bytes 1376260

commit v7 on v5

--- a/solution.py
+++ b/solution.py
@@ -148,7 +148,11 @@
     kept = attention(0, 2 * part)
     held = jnp.concatenate([kept] + away, 1)
     corner = route(after(first, kept, *away), count, heads, ((1, 0), (0, 2)))
-    values = [held] + [send(held, "ctx", count, s) for s in range(2, count, 2)]
+    shifts = list(range(2, count, 2))
+    if len(shifts) > 1:
+        shifts = [shifts[1], shifts[0]] + shifts[2:]
+    parts = {0: held, **{s: send(held, "ctx", count, s) for s in shifts}}
+    values = [parts[s] for s in range(0, count, 2)]
 
     rest = []
     for s in range(4, heads, 2):
@@ -188,9 +192,6 @@
     result = jnp.concatenate([left, right], 1).astype(jnp.bfloat16)
     result = result.reshape(count // 2, part, 2 * width)
 
-    shifts = list(range(2, count, 2))
-    if len(shifts) > 1:
-        shifts = [shifts[1], shifts[0]] + shifts[2:]
     final = jnp.zeros((part, count * width), jnp.bfloat16)
     for s in [0] + shifts:
         block = send(result[s // 2], "ctx", count, s) if s else result[0]

time: 60.5 us -> 60.5 us (level)
  no operation moved by 1% of the time
where the time goes in v7:
time: 60.5 us; the launch traced here: 60.2 us
  starting transfers between devices  27.9 us (46%)
  waiting for transfers between devices  21.3 us (35%)
  local copies, waits for them, and re-layouts  5.19 us (9%)
  Pallas kernels  5.16 us (9%)
    ppermute x13, starting transfers between devices, send(): return lax.ppermute(value, axis, [(i, i ^ shift) for i in range(size)])  18 us
    ppermute x13, waiting for transfers between devices, send(): return lax.ppermute(value, axis, [(i, i ^ shift) for i in range(size)])  17.5 us
    ppermute x6, starting transfers between devices, route(): return lax.ppermute(value, ('ctx', 'exp'), pairs)  9.95 us
    ppermute x6, waiting for transfers between devices, route(): return lax.ppermute(value, ('ctx', 'exp'), pairs)  3.74 us
    pallas_call x2, Pallas kernels, attention(): pl.pallas_call(functools.partial(attend, part, low), out_shape=jax.ShapeD...  3.68 us
    gather x2, local copies, waits for them, and re-layouts, shards(): rows = jnp.take(queries.reshape(heads, part, own_heads, lat), order, axis=0)  2.63 us
    pallas_call x2, Pallas kernels, projection(): pl.pallas_call(functools.partial(project, len(values), groups), out_shape...  1.49 us
    unnamed x9, local copies, waits for them, and re-layouts  1.48 us
  transfers between devices with their start and end apart: 19, of which 12 were waited for; matrix products, arithmetic and copies ran while one was open for 8% of the time, Pallas kernels for 9%

profile of v7, /device:TPU:0, one launch (start us, length us, event | category | flops | bytes accessed | tf_op | source)
XLA Modules:
  0.0 60.2 jit_solution(13271446915548551593)
XLA Ops:
  0.0 5.0 %collective-permute-start = (bf16[576,128]{1,0:T(8,128)(2,1)}, bf16[576,128]{1,0:T(8,128)(2,1)S(1)}, u32[]{:S(2)}, u32[]{:S(2)}) collective-permute-start(bf16[576,128]{1,0:T(8,128)(2,1)} %bitcast.17), channel_id=1, source_target_pairs={{0,24},{1,29},{2,26},{3,31},{4,28},{5,25},{6,30},{7,27},{8,16},{9,... | collective-permute-start | bytes 442376 | tf_op jit(solution)/shard_map/ppermute | solution.py:28
  5.1 0.6 collective-permute-start.4
  5.6 1.7 %collective-permute-start.6 = (bf16[576,128]{1,0:T(8,128)(2,1)}, bf16[576,128]{1,0:T(8,128)(2,1)S(1)}, u32[]{:S(2)}, u32[]{:S(2)}) collective-permute-start(bf16[576,128]{1,0:T(8,128)(2,1)} %bitcast.20), channel_id=1, source_target_pairs={{0,4},{4,0},{8,12},{12,8},{16,20},{20,16},{24,28},{28,24},{1,5},{5... | collective-permute-start | bytes 442376 | tf_op jit(solution)/shard_map/ppermute | solution.py:19
  7.4 1.5 %collective-permute-start.11 = (bf16[512,896]{1,0:T(8,128)(2,1)}, bf16[512,896]{1,0:T(8,128)(2,1)S(1)}, u32[]{:S(2)}, u32[]{:S(2)}) collective-permute-start(bf16[512,896]{1,0:T(8,128)(2,1)} %refs_4_.1), channel_id=1, source_target_pairs={{0,2},{1,5},{2,0},{3,7},{4,6},{5,1},{6,4},{7,3},{8,10},{9,13},{10,... | collective-permute-start | bytes 2752520 | tf_op jit(solution)/shard_map/ppermute | solution.py:28
  8.8 1.4 %copy.5 = bf16[128,4,576]{2,0,1:T(8,128)(2,1)S(1)} copy(bf16[128,4,576]{0,2,1:T(8,128)(2,1)} %param.4) | data formatting | bytes 1179648 | tf_op args[0]
  10.3 1.5 %gather_fusion = bf16[4,32,4,576]{3,1,2,0:T(8,128)(2,1)} fusion(bf16[4,32,4,576]{3,1,2,0:T(8,128)(2,1)S(1)} %copy.6, s32[1024]{0:T(1024)S(1)} %pad_clamp_fusion), kind=kCustom, calls=%fused_computation | custom fusion | bytes 1179664 | tf_op jit(solution)/shard_map/jit(_take)/gather | solution.py:124
  11.8 1.2 %copy.7 = bf16[4,32,4,576]{3,1,0,2:T(8,128)(2,1)S(1)} copy(bf16[4,32,4,576]{3,1,2,0:T(8,128)(2,1)} %gather_fusion) | data formatting | bytes 1179648 | tf_op jit(solution)/shard_map/jit(_take)/gather | solution.py:124
  13.4 0.6 %collective-permute-done.6.refs_7_ = bf16[576,128]{1,0:T(8,128)(2,1)S(1)} collective-permute-done((bf16[576,128]{1,0:T(8,128)(2,1)}, bf16[576,128]{1,0:T(8,128)(2,1)S(1)}, u32[]{:S(2)}, u32[]{:S(2)}) %collective-permute-start.6) | collective-permute-done | bytes 147488 | tf_op jit(solution)/shard_map/ppermute | solution.py:19
  14.1 1.9 %collective-permute-start.12 = (bf16[512,896]{1,0:T(8,128)(2,1)S(1)}, bf16[512,896]{1,0:T(8,128)(2,1)S(1)}, u32[]{:S(2)}, u32[]{:S(2)}) collective-permute-start(bf16[512,896]{1,0:T(8,128)(2,1)S(1)} %copy-done), channel_id=1, source_target_pairs={{0,4},{1,3},{2,6},{3,1},{4,0},{5,7},{6,2},{7,5},{8,12},{9,11},{10,... | collective-permute-start | bytes 2752520 | tf_op jit(solution)/shard_map/ppermute | solution.py:28
  16.1 2.6 %collective-permute-done.2.refs_3_ = bf16[576,128]{1,0:T(8,128)(2,1)S(1)} collective-permute-done((bf16[576,128]{1,0:T(8,128)(2,1)}, bf16[576,128]{1,0:T(8,128)(2,1)S(1)}, u32[]{:S(2)}, u32[]{:S(2)}) %collective-permute-start.2) | collective-permute-done | bytes 147488 | tf_op jit(solution)/shard_map/ppermute | solution.py:28
  18.7 0.5 collective-permute-start.5
  19.3 0.8 %collective-permute-done.3.refs_4_ = bf16[576,128]{1,0:T(8,128)(2,1)S(1)} collective-permute-done((bf16[576,128]{1,0:T(8,128)(2,1)S(1)}, bf16[576,128]{1,0:T(8,128)(2,1)S(1)}, u32[]{:S(2)}, u32[]{:S(2)}) %collective-permute-start.3) | collective-permute-done | bytes 147488 | tf_op jit(solution)/shard_map/ppermute | solution.py:19
  20.3 1.8 %shard_map.47 = bf16[64,512]{1,0:T(8,128)(2,1)S(1)} custom-call(s32[10]{0:T(128)S(1)} %stack.40.place, bf16[4,64,576]{2,1,0:T(8,128)(2,1)S(1)} %get-tuple-element.20.query, bf16[576,128]{1,0:T(8,128)(2,1)S(1)} %bitcast.21, bf16[576,128]{1,0:T(8,128)(2,1)S(1)} %collective-permute-done.refs_1_, bf16[576,128]{1,0:T(8,128)(2,1)S(1)} %collective-permute-done.1.refs_2_, ...), custom_call_target="tpu_custom_call" | custom-call | flops 570425344 | bytes 2293760 | tf_op jit(solution)/shard_map/pallas_call | solution.py:130
  22.1 1.6 %collective-permute-start.7 = (bf16[64,512]{1,0:T(8,128)(2,1)S(1)}, bf16[64,512]{1,0:T(8,128)(2,1)S(1)}, u32[]{:S(2)}, u32[]{:S(2)}) collective-permute-start(bf16[64,512]{1,0:T(8,128)(2,1)S(1)} %shard_map.47), channel_id=1, source_target_pairs={{0,2},{1,3},{2,0},{3,1},{4,6},{5,7},{6,4},{7,5},{8,10},{9,11},{10,... | collective-permute-start | bytes 196616 | tf_op jit(solution)/shard_map/ppermute | solution.py:19
  23.7 1.8 %shard_map.46 = bf16[64,512]{1,0:T(8,128)(2,1)S(1)} custom-call(s32[10]{0:T(128)S(1)} %stack.40.place, bf16[4,64,576]{2,1,0:T(8,128)(2,1)S(1)} %get-tuple-element.19.query, bf16[576,128]{1,0:T(8,128)(2,1)S(1)} %bitcast.22, bf16[576,128]{1,0:T(8,128)(2,1)S(1)} %collective-permute-done.refs_1_, bf16[576,128]{1,0:T(8,128)(2,1)S(1)} %collective-permute-done.1.refs_2_, ...), custom_call_target="tpu_custom_call" | custom-call | flops 570425344 | bytes 2293760 | tf_op jit(solution)/shard_map/pallas_call | solution.py:130
  25.5 1.7 %collective-permute-done.7 = bf16[64,512]{1,0:T(8,128)(2,1)S(1)} collective-permute-done((bf16[64,512]{1,0:T(8,128)(2,1)S(1)}, bf16[64,512]{1,0:T(8,128)(2,1)S(1)}, u32[]{:S(2)}, u32[]{:S(2)}) %collective-permute-start.7) | collective-permute-done | bytes 65568 | tf_op jit(solution)/shard_map/ppermute | solution.py:19
  27.2 0.9 %collective-permute-start.14 = (bf16[512,896]{1,0:T(8,128)(2,1)S(1)}, bf16[512,896]{1,0:T(8,128)(2,1)S(1)}, u32[]{:S(2)}, u32[]{:S(2)}) collective-permute-start(bf16[512,896]{1,0:T(8,128)(2,1)S(1)} %collective-permute-done.11.refs_5_), channel_id=1, source_target_pairs={{0,4},{1,3},{2,6},{3,1},{4,0},{5,7},{6,2},{7,5},{8,12},{9,11},{10,... | collective-permute-start | bytes 2752520 | tf_op jit(solution)/shard_map/ppermute | solution.py:28
  28.6 2.6 %collective-permute-start.9 = (bf16[64,1024]{1,0:T(8,128)(2,1)S(1)}, bf16[64,1024]{1,0:T(8,128)(2,1)S(1)}, u32[]{:S(2)}, u32[]{:S(2)}) collective-permute-start(bf16[64,1024]{1,0:T(8,128)(2,1)S(1)} %pad_maximum_fusion.refs_0_), channel_id=1, source_target_pairs={{0,16},{4,20},{8,24},{12,28},{16,0},{20,4},{24,8},{28,12},{1,17},{... | collective-permute-start | bytes 393224 | tf_op jit(solution)/shard_map/ppermute | solution.py:19
  31.2 1.4 %collective-permute-start.10 = (bf16[64,1024]{1,0:T(8,128)(2,1)S(1)}, bf16[64,1024]{1,0:T(8,128)(2,1)S(1)}, u32[]{:S(2)}, u32[]{:S(2)}) collective-permute-start(bf16[64,1024]{1,0:T(8,128)(2,1)S(1)} %pad_maximum_fusion.refs_0_), channel_id=1, source_target_pairs={{0,24},{4,28},{8,16},{12,20},{16,8},{20,12},{24,0},{28,4},{1,25},{... | collective-permute-start | bytes 393224 | tf_op jit(solution)/shard_map/ppermute | solution.py:19
  32.6 1.7 %collective-permute-done.8.refs_1_ = bf16[64,1024]{1,0:T(8,128)(2,1)S(1)} collective-permute-done((bf16[64,1024]{1,0:T(8,128)(2,1)S(1)}, bf16[64,1024]{1,0:T(8,128)(2,1)S(1)}, u32[]{:S(2)}, u32[]{:S(2)}) %collective-permute-start.8) | collective-permute-done | bytes 131104 | tf_op jit(solution)/shard_map/ppermute | solution.py:19
  34.3 1.6 %collective-permute-done.9.refs_2_ = bf16[64,1024]{1,0:T(8,128)(2,1)S(1)} collective-permute-done((bf16[64,1024]{1,0:T(8,128)(2,1)S(1)}, bf16[64,1024]{1,0:T(8,128)(2,1)S(1)}, u32[]{:S(2)}, u32[]{:S(2)}) %collective-permute-start.9) | collective-permute-done | bytes 131104 | tf_op jit(solution)/shard_map/ppermute | solution.py:19
  35.9 2.3 %collective-permute-done.10.refs_3_ = bf16[64,1024]{1,0:T(8,128)(2,1)S(1)} collective-permute-done((bf16[64,1024]{1,0:T(8,128)(2,1)S(1)}, bf16[64,1024]{1,0:T(8,128)(2,1)S(1)}, u32[]{:S(2)}, u32[]{:S(2)}) %collective-permute-start.10) | collective-permute-done | bytes 131104 | tf_op jit(solution)/shard_map/ppermute | solution.py:19
  38.2 1.0 %shard_map.48 = (f32[128,1792]{1,0:T(8,128)S(1)}, bf16[128,1792]{1,0:T(8,128)(2,1)S(1)}) custom-call(s32[1]{0:T(128)} %bitcast.place, bf16[64,1024]{1,0:T(8,128)(2,1)S(1)} %pad_maximum_fusion.refs_0_, bf16[64,1024]{1,0:T(8,128)(2,1)S(1)} %collective-permute-done.8.refs_1_, bf16[64,1024]{1,0:T(8,128)(2,1)S(1)} %collective-permute-done.9.refs_2_, ...), custom_call_target="tpu_custom_call" | custom-call | flops 704643072 | bytes 4653056 | tf_op jit(solution)/shard_map/pallas_call | solution.py:165
  39.2 4.8 %collective-permute-start.13 = (bf16[128,1792]{1,0:T(8,128)(2,1)S(1)}, bf16[128,1792]{1,0:T(8,128)(2,1)S(1)}, u32[]{:S(2)}, u32[]{:S(2)}) collective-permute-start(bf16[128,1792]{1,0:T(8,128)(2,1)S(1)} %get-tuple-element.13), channel_id=1, source_target_pairs={{0,1},{1,0},{2,3},{3,2},{4,5},{5,4},{6,7},{7,6},{8,9},{9,8},{10,11... | collective-permute-start | bytes 1376264 | tf_op jit(solution)/shard_map/ppermute | solution.py:19
  44.0 1.1 %collective-permute-done.14.refs_4_ = bf16[512,896]{1,0:T(8,128)(2,1)S(1)} collective-permute-done((bf16[512,896]{1,0:T(8,128)(2,1)S(1)}, bf16[512,896]{1,0:T(8,128)(2,1)S(1)}, u32[]{:S(2)}, u32[]{:S(2)}) %collective-permute-start.14) | collective-permute-done | bytes 917536 | tf_op jit(solution)/shard_map/ppermute | solution.py:28
  45.6 0.5 collective-permute-start.15
  46.2 1.0 %collective-permute-done.15 = bf16[128,896]{1,0:T(8,128)(2,1)S(1)} collective-permute-done((bf16[128,896]{1,0:T(8,128)(2,1)S(1)}, bf16[128,896]{1,0:T(8,128)(2,1)S(1)}, u32[]{:S(2)}, u32[]{:S(2)}) %collective-permute-start.15) | collective-permute-done | bytes 229408 | tf_op jit(solution)/shard_map/ppermute | solution.py:19
  47.5 1.9 %collective-permute-start.16 = (bf16[32,1792]{1,0:T(8,128)(2,1)S(1)}, bf16[32,1792]{1,0:T(8,128)(2,1)S(1)}, u32[]{:S(2)}, u32[]{:S(2)}) collective-permute-start(bf16[32,1792]{1,0:T(8,128)(2,1)S(1)} %get-tuple-element.23), channel_id=1, source_target_pairs={{0,16},{4,20},{8,24},{12,28},{16,0},{20,4},{24,8},{28,12},{1,17},{... | collective-permute-start | bytes 344072 | tf_op jit(solution)/shard_map/ppermute | solution.py:19
  49.4 2.2 %collective-permute-start.17 = (bf16[32,1792]{1,0:T(8,128)(2,1)S(1)}, bf16[32,1792]{1,0:T(8,128)(2,1)S(1)}, u32[]{:S(2)}, u32[]{:S(2)}) collective-permute-start(bf16[32,1792]{1,0:T(8,128)(2,1)S(1)} %get-tuple-element.24), channel_id=1, source_target_pairs={{0,8},{4,12},{8,0},{12,4},{16,24},{20,28},{24,16},{28,20},{1,9},{5... | collective-permute-start | bytes 344072 | tf_op jit(solution)/shard_map/ppermute | solution.py:19
  52.0 5.3 %collective-permute-done.16 = bf16[32,1792]{1,0:T(8,128)(2,1)S(1)} collective-permute-done((bf16[32,1792]{1,0:T(8,128)(2,1)S(1)}, bf16[32,1792]{1,0:T(8,128)(2,1)S(1)}, u32[]{:S(2)}, u32[]{:S(2)}) %collective-permute-start.16) | collective-permute-done | bytes 114720 | tf_op jit(solution)/shard_map/ppermute | solution.py:19
  57.3 2.2 %collective-permute-done.18 = bf16[32,1792]{1,0:T(8,128)(2,1)S(1)} collective-permute-done((bf16[32,1792]{1,0:T(8,128)(2,1)S(1)}, bf16[32,1792]{1,0:T(8,128)(2,1)S(1)}, u32[]{:S(2)}, u32[]{:S(2)}) %collective-permute-start.18) | collective-permute-done | bytes 114720 | tf_op jit(solution)/shard_map/ppermute | solution.py:19
  59.6 0.7 %constant_dynamic-update-slice_fusion = bf16[32,7168]{1,0:T(8,128)(2,1)} fusion(bf16[32,7168]{1,0:T(8,128)(2,1)} %copy-done.3, bf16[32,1792]{1,0:T(8,128)(2,1)S(1)} %collective-permute-done.18, s32[]{:T(128)S(6)} %select_n.111), kind=kLoop, calls=%fused_computation.24 | loop fusion | bytes 229380 | tf_op jit(solution)/shard_map/dynamic_update_slice | solution.py:198
  (39 shorter events, 2.5 us)
Async XLA Ops:
  0.0 16.1 %collective-permute-start = (bf16[576,128]{1,0:T(8,128)(2,1)}, bf16[576,128]{1,0:T(8,128)(2,1)S(1)}, u32[]{:S(2)}, u32[]{:S(2)}) collective-permute-start(bf16[576,128]{1,0:T(8,128)(2,1)} %bitcast.17), channel_id=1, source_target_pairs={{0,24},{1,29},{2,26},{3,31},{4,28},{5,25},{6,30},{7,27},{8,16},{9,... | collective-permute-start | bytes 442376 | tf_op jit(solution)/shard_map/ppermute | solution.py:28
  5.0 13.6 %collective-permute-start.2 = (bf16[576,128]{1,0:T(8,128)(2,1)}, bf16[576,128]{1,0:T(8,128)(2,1)S(1)}, u32[]{:S(2)}, u32[]{:S(2)}) collective-permute-start(bf16[576,128]{1,0:T(8,128)(2,1)} %bitcast.18), channel_id=1, source_target_pairs={{0,16},{1,21},{2,18},{3,23},{4,20},{5,17},{6,22},{7,19},{8,24},{9,... | collective-permute-start | bytes 442376 | tf_op jit(solution)/shard_map/ppermute | solution.py:28
  5.1 13.6 %collective-permute-start.4 = (bf16[576,128]{1,0:T(8,128)(2,1)}, bf16[576,128]{1,0:T(8,128)(2,1)S(1)}, u32[]{:S(2)}, u32[]{:S(2)}) collective-permute-start(bf16[576,128]{1,0:T(8,128)(2,1)} %bitcast.19), channel_id=1, source_target_pairs={{0,8},{1,13},{2,10},{3,15},{4,12},{5,9},{6,14},{7,11},{8,0},{9,5},... | collective-permute-start | bytes 442376 | tf_op jit(solution)/shard_map/ppermute | solution.py:28
  5.6 8.4 %collective-permute-start.6 = (bf16[576,128]{1,0:T(8,128)(2,1)}, bf16[576,128]{1,0:T(8,128)(2,1)S(1)}, u32[]{:S(2)}, u32[]{:S(2)}) collective-permute-start(bf16[576,128]{1,0:T(8,128)(2,1)} %bitcast.20), channel_id=1, source_target_pairs={{0,4},{4,0},{8,12},{12,8},{16,20},{20,16},{24,28},{28,24},{1,5},{5... | collective-permute-start | bytes 442376 | tf_op jit(solution)/shard_map/ppermute | solution.py:19
  7.4 19.9 %collective-permute-start.11 = (bf16[512,896]{1,0:T(8,128)(2,1)}, bf16[512,896]{1,0:T(8,128)(2,1)S(1)}, u32[]{:S(2)}, u32[]{:S(2)}) collective-permute-start(bf16[512,896]{1,0:T(8,128)(2,1)} %refs_4_.1), channel_id=1, source_target_pairs={{0,2},{1,5},{2,0},{3,7},{4,6},{5,1},{6,4},{7,3},{8,10},{9,13},{10,... | collective-permute-start | bytes 2752520 | tf_op jit(solution)/shard_map/ppermute | solution.py:28
  12.9 1.2 %copy-start = (bf16[512,896]{1,0:T(8,128)(2,1)S(1)}, bf16[512,896]{1,0:T(8,128)(2,1)}, u32[]{:S(2)}) copy-start(bf16[512,896]{1,0:T(8,128)(2,1)} %refs_4_.1) | copy-start | bytes 2752516
  14.1 24.1 %collective-permute-start.12 = (bf16[512,896]{1,0:T(8,128)(2,1)S(1)}, bf16[512,896]{1,0:T(8,128)(2,1)S(1)}, u32[]{:S(2)}, u32[]{:S(2)}) collective-permute-start(bf16[512,896]{1,0:T(8,128)(2,1)S(1)} %copy-done), channel_id=1, source_target_pairs={{0,4},{1,3},{2,6},{3,1},{4,0},{5,7},{6,2},{7,5},{8,12},{9,11},{10,... | collective-permute-start | bytes 2752520 | tf_op jit(solution)/shard_map/ppermute | solution.py:28
  16.1 3.2 %collective-permute-start.1 = (bf16[576,128]{1,0:T(8,128)(2,1)S(1)}, bf16[576,128]{1,0:T(8,128)(2,1)S(1)}, u32[]{:S(2)}, u32[]{:S(2)}) collective-permute-start(bf16[576,128]{1,0:T(8,128)(2,1)S(1)} %collective-permute-done.refs_1_), channel_id=1, source_target_pairs={{0,1},{1,0},{2,3},{3,2},{4,5},{5,4},{6,7},{7,6},{8,9},{9,8},{10,11... | collective-permute-start | bytes 442376 | tf_op jit(solution)/shard_map/ppermute | solution.py:19
  18.7 1.4 %collective-permute-start.3 = (bf16[576,128]{1,0:T(8,128)(2,1)S(1)}, bf16[576,128]{1,0:T(8,128)(2,1)S(1)}, u32[]{:S(2)}, u32[]{:S(2)}) collective-permute-start(bf16[576,128]{1,0:T(8,128)(2,1)S(1)} %collective-permute-done.2.refs_3_), channel_id=1, source_target_pairs={{0,1},{1,0},{2,3},{3,2},{4,5},{5,4},{6,7},{7,6},{8,9},{9,8},{10,11... | collective-permute-start | bytes 442376 | tf_op jit(solution)/shard_map/ppermute | solution.py:19
  18.7 1.6 %collective-permute-start.5 = (bf16[576,128]{1,0:T(8,128)(2,1)S(1)}, bf16[576,128]{1,0:T(8,128)(2,1)S(1)}, u32[]{:S(2)}, u32[]{:S(2)}) collective-permute-start(bf16[576,128]{1,0:T(8,128)(2,1)S(1)} %collective-permute-done.4.refs_5_), channel_id=1, source_target_pairs={{0,1},{1,0},{2,3},{3,2},{4,5},{5,4},{6,7},{7,6},{8,9},{9,8},{10,11... | collective-permute-start | bytes 442376 | tf_op jit(solution)/shard_map/ppermute | solution.py:19
  19.2 1.1 %copy-start.1 = (bf16[4,512,128]{2,1,0:T(8,128)(2,1)S(1)}, bf16[4,512,128]{2,1,0:T(8,128)(2,1)}, u32[]{:S(2)}) copy-start(bf16[4,512,128]{2,1,0:T(8,128)(2,1)} %refs_8_.3) | copy-start | bytes 1572868
  19.2 1.1 %copy-start.2 = (bf16[128,576]{0,1:T(8,128)(2,1)S(1)}, bf16[128,576]{0,1:T(8,128)(2,1)}, u32[]{:S(2)}) copy-start(bf16[128,576]{0,1:T(8,128)(2,1)} %param.5) | copy-start | bytes 442372
  22.1 5.1 %collective-permute-start.7 = (bf16[64,512]{1,0:T(8,128)(2,1)S(1)}, bf16[64,512]{1,0:T(8,128)(2,1)S(1)}, u32[]{:S(2)}, u32[]{:S(2)}) collective-permute-start(bf16[64,512]{1,0:T(8,128)(2,1)S(1)} %shard_map.47), channel_id=1, source_target_pairs={{0,2},{1,3},{2,0},{3,1},{4,6},{5,7},{6,4},{7,5},{8,10},{9,11},{10,... | collective-permute-start | bytes 196616 | tf_op jit(solution)/shard_map/ppermute | solution.py:19
  27.2 17.9 %collective-permute-start.14 = (bf16[512,896]{1,0:T(8,128)(2,1)S(1)}, bf16[512,896]{1,0:T(8,128)(2,1)S(1)}, u32[]{:S(2)}, u32[]{:S(2)}) collective-permute-start(bf16[512,896]{1,0:T(8,128)(2,1)S(1)} %collective-permute-done.11.refs_5_), channel_id=1, source_target_pairs={{0,4},{1,3},{2,6},{3,1},{4,0},{5,7},{6,2},{7,5},{8,12},{9,11},{10,... | collective-permute-start | bytes 2752520 | tf_op jit(solution)/shard_map/ppermute | solution.py:28
  28.1 6.2 %collective-permute-start.8 = (bf16[64,1024]{1,0:T(8,128)(2,1)S(1)}, bf16[64,1024]{1,0:T(8,128)(2,1)S(1)}, u32[]{:S(2)}, u32[]{:S(2)}) collective-permute-start(bf16[64,1024]{1,0:T(8,128)(2,1)S(1)} %pad_maximum_fusion.refs_0_), channel_id=1, source_target_pairs={{0,8},{4,12},{8,0},{12,4},{16,24},{20,28},{24,16},{28,20},{1,9},{5... | collective-permute-start | bytes 393224 | tf_op jit(solution)/shard_map/ppermute | solution.py:19
  28.6 7.3 %collective-permute-start.9 = (bf16[64,1024]{1,0:T(8,128)(2,1)S(1)}, bf16[64,1024]{1,0:T(8,128)(2,1)S(1)}, u32[]{:S(2)}, u32[]{:S(2)}) collective-permute-start(bf16[64,1024]{1,0:T(8,128)(2,1)S(1)} %pad_maximum_fusion.refs_0_), channel_id=1, source_target_pairs={{0,16},{4,20},{8,24},{12,28},{16,0},{20,4},{24,8},{28,12},{1,17},{... | collective-permute-start | bytes 393224 | tf_op jit(solution)/shard_map/ppermute | solution.py:19
  31.2 7.0 %collective-permute-start.10 = (bf16[64,1024]{1,0:T(8,128)(2,1)S(1)}, bf16[64,1024]{1,0:T(8,128)(2,1)S(1)}, u32[]{:S(2)}, u32[]{:S(2)}) collective-permute-start(bf16[64,1024]{1,0:T(8,128)(2,1)S(1)} %pad_maximum_fusion.refs_0_), channel_id=1, source_target_pairs={{0,24},{4,28},{8,16},{12,20},{16,8},{20,12},{24,0},{28,4},{1,25},{... | collective-permute-start | bytes 393224 | tf_op jit(solution)/shard_map/ppermute | solution.py:19
  39.2 6.8 %collective-permute-start.13 = (bf16[128,1792]{1,0:T(8,128)(2,1)S(1)}, bf16[128,1792]{1,0:T(8,128)(2,1)S(1)}, u32[]{:S(2)}, u32[]{:S(2)}) collective-permute-start(bf16[128,1792]{1,0:T(8,128)(2,1)S(1)} %get-tuple-element.13), channel_id=1, source_target_pairs={{0,1},{1,0},{2,3},{3,2},{4,5},{5,4},{6,7},{7,6},{8,9},{9,8},{10,11... | collective-permute-start | bytes 1376264 | tf_op jit(solution)/shard_map/ppermute | solution.py:19
  45.6 1.6 %collective-permute-start.15 = (bf16[128,896]{1,0:T(8,128)(2,1)S(1)}, bf16[128,896]{1,0:T(8,128)(2,1)S(1)}, u32[]{:S(2)}, u32[]{:S(2)}) collective-permute-start(bf16[128,896]{1,0:T(8,128)(2,1)S(1)} %get-tuple-element.16), channel_id=1, source_target_pairs={{0,1},{1,0},{2,3},{3,2},{4,5},{5,4},{6,7},{7,6},{8,9},{9,8},{10,11... | collective-permute-start | bytes 688136 | tf_op jit(solution)/shard_map/ppermute | solution.py:19
  47.5 9.8 %collective-permute-start.16 = (bf16[32,1792]{1,0:T(8,128)(2,1)S(1)}, bf16[32,1792]{1,0:T(8,128)(2,1)S(1)}, u32[]{:S(2)}, u32[]{:S(2)}) collective-permute-start(bf16[32,1792]{1,0:T(8,128)(2,1)S(1)} %get-tuple-element.23), channel_id=1, source_target_pairs={{0,16},{4,20},{8,24},{12,28},{16,0},{20,4},{24,8},{28,12},{1,17},{... | collective-permute-start | bytes 344072 | tf_op jit(solution)/shard_map/ppermute | solution.py:19
  49.4 7.9 %collective-permute-start.17 = (bf16[32,1792]{1,0:T(8,128)(2,1)S(1)}, bf16[32,1792]{1,0:T(8,128)(2,1)S(1)}, u32[]{:S(2)}, u32[]{:S(2)}) collective-permute-start(bf16[32,1792]{1,0:T(8,128)(2,1)S(1)} %get-tuple-element.24), channel_id=1, source_target_pairs={{0,8},{4,12},{8,0},{12,4},{16,24},{20,28},{24,16},{28,20},{1,9},{5... | collective-permute-start | bytes 344072 | tf_op jit(solution)/shard_map/ppermute | solution.py:19
  51.6 7.9 %collective-permute-start.18 = (bf16[32,1792]{1,0:T(8,128)(2,1)S(1)}, bf16[32,1792]{1,0:T(8,128)(2,1)S(1)}, u32[]{:S(2)}, u32[]{:S(2)}) collective-permute-start(bf16[32,1792]{1,0:T(8,128)(2,1)S(1)} %get-tuple-element.21), channel_id=1, source_target_pairs={{0,24},{4,28},{8,16},{12,20},{16,8},{20,12},{24,0},{28,4},{1,25},{... | collective-permute-start | bytes 344072 | tf_op jit(solution)/shard_map/ppermute | solution.py:19
  57.3 2.3 %copy-start.3 = (bf16[32,7168]{1,0:T(8,128)(2,1)}, bf16[32,7168]{1,0:T(8,128)(2,1)S(1)}, u32[]{:S(2)}) copy-start(bf16[32,7168]{1,0:T(8,128)(2,1)S(1)} %constant_dynamic-update-slice_fusion.1) | copy-start | bytes 1376260
